TPU v7x, 32 devices: a whole 2x2x4 slice. The times are simulated.
32 devices in a mesh: dp: 8 (over z, x), mp: 4 (over y, core).
Axes of the slice: x: 2, y: 2, z: 4, core: 2. Of those that a mesh axis runs over, the one named last changes fastest.
Arguments:
- block_input: bfloat16 [16384, 1152], P(('dp', 'mp')), may hold values from -6 to 6
- cotangent: bfloat16 [16384, 1152], P(('dp', 'mp')), may hold values from -6 to 6
- expert_ids: int32 [16384], P(('dp', 'mp')), may hold values from 0 to 3, as said below
- slot_ids: int32 [16384], P(('dp', 'mp')), may hold values from 0 to 191, as said below
- inward_proj: float32 [2, 1152, 2304], P(None, None, ('dp', 'mp')), may hold values from -0.1875 to 0.1875
- select_proj: float32 [2304, 104], P(('dp', 'mp')), may hold values from -0.125 to 0.125
- delta_proj: float32 [72, 2304], P(None, ('dp', 'mp')), may hold values from -0.75 to 0.75
- channel_params: float32 [23, 2304], P(None, ('dp', 'mp')), may hold values from -7 to 3, as said below
- outward_proj: float32 [2304, 1152], P(('dp', 'mp')), may hold values from -0.25 to 0.25
- expert_up: float32 [4, 1152, 3072], P('mp', None, 'dp'), may hold values from -0.1875 to 0.1875
- expert_down: float32 [4, 3072, 1152], P('mp', 'dp'), may hold values from -0.4375 to 0.4375
- norm_gains: float32 [2, 1152], replicated, may hold values from 0.5 to 1.5
- router_weight: float32 [1152, 4], replicated, may hold values from -0.125 to 0.125
- inward_velocity: float32 [2, 1152, 2304], P(None, None, ('dp', 'mp')), may hold values from -3 to 3
- select_velocity: float32 [2304, 104], P(('dp', 'mp')), may hold values from -1.75 to 1.75
- delta_velocity: float32 [72, 2304], P(None, ('dp', 'mp')), may hold values from -0.1875 to 0.1875
- channel_velocity: float32 [23, 2304], P(None, ('dp', 'mp')), may hold values from -1.75 to 1.75
- outward_velocity: float32 [2304, 1152], P(('dp', 'mp')), may hold values from -2.5 to 2.5
- upward_velocity: float32 [4, 1152, 3072], P('mp', None, 'dp'), may hold values from -0.875 to 0.875
- downward_velocity: float32 [4, 3072, 1152], P('mp', 'dp'), may hold values from -0.5 to 0.5
- gains_velocity: float32 [2, 1152], replicated, may hold values from -6 to 6
- router_velocity: float32 [1152, 4], replicated, may hold values from -6 to 6
- inward_average: float32 [2, 1152, 2304], P(None, None, ('dp', 'mp')), may hold values from -0.1875 to 0.1875
- select_average: float32 [2304, 104], P(('dp', 'mp')), may hold values from -0.125 to 0.125
- delta_average: float32 [72, 2304], P(None, ('dp', 'mp')), may hold values from -0.75 to 0.75
- channel_average: float32 [23, 2304], P(None, ('dp', 'mp')), may hold values from -7 to 3, as said below
- outward_average: float32 [2304, 1152], P(('dp', 'mp')), may hold values from -0.25 to 0.25
- upward_average: float32 [4, 1152, 3072], P('mp', None, 'dp'), may hold values from -0.1875 to 0.1875
- downward_average: float32 [4, 3072, 1152], P('mp', 'dp'), may hold values from -0.4375 to 0.4375
- gains_average: float32 [2, 1152], replicated, may hold values from 0.5 to 1.5
- router_average: float32 [1152, 4], replicated, may hold values from -0.125 to 0.125
Outputs:
- block_output: bfloat16 [16384, 1152], P(('dp', 'mp'))
- block_grad: float32 [16384, 1152], P(('dp', 'mp'))
- inward_weight: float32 [2, 1152, 2304], P(None, None, ('dp', 'mp'))
- inward_momentum: float32 [2, 1152, 2304], P(None, None, ('dp', 'mp'))
- inward_smoothed: float32 [2, 1152, 2304], P(None, None, ('dp', 'mp'))
- inward_copy: bfloat16 [2, 1152, 2304], P(None, None, ('dp', 'mp'))
- select_weight: float32 [2304, 104], P(('dp', 'mp'))
- select_momentum: float32 [2304, 104], P(('dp', 'mp'))
- select_smoothed: float32 [2304, 104], P(('dp', 'mp'))
- select_copy: bfloat16 [2304, 104], P(('dp', 'mp'))
- delta_weight: float32 [72, 2304], P(None, ('dp', 'mp'))
- delta_momentum: float32 [72, 2304], P(None, ('dp', 'mp'))
- delta_smoothed: float32 [72, 2304], P(None, ('dp', 'mp'))
- delta_copy: bfloat16 [72, 2304], P(None, ('dp', 'mp'))
- channel_weight: float32 [23, 2304], P(None, ('dp', 'mp'))
- channel_momentum: float32 [23, 2304], P(None, ('dp', 'mp'))
- channel_smoothed: float32 [23, 2304], P(None, ('dp', 'mp'))
- channel_copy: bfloat16 [23, 2304], P(None, ('dp', 'mp'))
- outward_weight: float32 [2304, 1152], P(('dp', 'mp'))
- outward_momentum: float32 [2304, 1152], P(('dp', 'mp'))
- outward_smoothed: float32 [2304, 1152], P(('dp', 'mp'))
- outward_copy: bfloat16 [2304, 1152], P(('dp', 'mp'))
- upward_weight: float32 [4, 1152, 3072], P('mp', None, 'dp')
- upward_momentum: float32 [4, 1152, 3072], P('mp', None, 'dp')
- upward_smoothed: float32 [4, 1152, 3072], P('mp', None, 'dp')
- upward_copy: bfloat16 [4, 1152, 3072], P('mp', None, 'dp')
- downward_weight: float32 [4, 3072, 1152], P('mp', 'dp')
- downward_momentum: float32 [4, 3072, 1152], P('mp', 'dp')
- downward_smoothed: float32 [4, 3072, 1152], P('mp', 'dp')
- downward_copy: bfloat16 [4, 3072, 1152], P('mp', 'dp')
- gains_weight: float32 [2, 1152], replicated
- gains_momentum: float32 [2, 1152], replicated
- gains_smoothed: float32 [2, 1152], replicated
- gains_copy: bfloat16 [2, 1152], replicated
- router_new: float32 [1152, 4], replicated
- router_momentum: float32 [1152, 4], replicated
- router_smoothed: float32 [1152, 4], replicated
- router_copy: bfloat16 [1152, 4], replicated
Inputs may be any that keep to these rules, and one draw needn't show every extreme that they name: `expert_ids`: in every block of 512 rows that one device holds no expert is named by more than 192 rows. `slot_ids`: rows of one block of 512 that name the same expert hold different slots. `channel_params`: rows 0 to 3 are convolution taps, row 4 their bias, row 5 the step bias, row 6 the skip gain, the last 16 rows the logarithms of the decay rates. `channel_average`: laid out as channel_params.
All inputs are finite; a program needn't handle non-finite values.
Results may differ from a plain program's by a relative error of at most 0.013.
Values may be sent and summed in bfloat16 or wider, within the bound.
No kernel may reach another device: no remote copies, remote signals or barrier semaphores. Data moves between devices by JAX's collectives and lax.ppermute only.
A program may use at most 384 MiB of HBM per device.

v0:
```python
import math

import jax
import jax.numpy as jnp
from jax import lax
from jax.sharding import PartitionSpec as P

CONV = 4
DT_RANK = 72
SPAN = 256
SUB = 16
CAP = 192


EPSILON = 1e-05
MOMENT = 0.9
SMOOTH = 0.6
LEARNING = (0.02, 0.03, 0.4, 0.3, 0.04, 0.07, 0.3, 0.3, 0.01)
HIGHEST = lax.Precision.HIGHEST


def contract_rows(left, right):
    return lax.dot_general(
        left, right, (((0,), (0,)), ((), ())), preferred_element_type=jnp.float32
    )


def contract_cols(left, right):
    return lax.dot_general(
        left, right, (((1,), (1,)), ((), ())), preferred_element_type=jnp.float32
    )


def rms_norm(values, gain):
    factor = lax.rsqrt(jnp.mean(values * values, axis=-1, keepdims=True) + EPSILON)
    return values * factor * gain


def conv_act(conv_in, channel):
    length = conv_in.shape[0]
    padded = jnp.pad(conv_in, ((CONV - 1, 0), (0, 0)))
    total = channel[CONV] + jnp.zeros_like(conv_in)
    for offset in range(CONV):
        total = total + channel[offset] * padded[offset : offset + length]
    return jax.nn.silu(total)


def block_scan(activated, delta, bmat, cmat, rate, skip_gain):
    length, channels = activated.shape
    states = bmat.shape[1]
    block_count = length // SPAN
    sub_count = SPAN // SUB
    lower_ones = jnp.tril(jnp.ones((SUB, SUB), jnp.float32))
    inputs_all = (
        activated.reshape(block_count, sub_count, SUB, channels),
        delta.reshape(block_count, sub_count, SUB, channels),
        bmat.reshape(block_count, sub_count, SUB, states),
        cmat.reshape(block_count, sub_count, SUB, states),
    )

    def span_step(carried, inputs_part):
        act_part, delta_part, bmat_part, cmat_part = inputs_part
        elapsed = jnp.cumsum(delta_part, axis=1)
        middle = elapsed[:, SUB // 2 : SUB // 2 + 1, :]
        shifted = (elapsed - middle)[:, :, None, :] * rate
        driven = (
            jnp.exp(shifted) * (delta_part * act_part)[:, :, None, :] * bmat_part[:, :, :, None]
        )
        summed = jnp.einsum("tj,sjnc->stnc", lower_ones, driven, precision=HIGHEST)
        local_state = jnp.exp(-shifted) * summed
        decayed = jnp.exp(-elapsed[:, :, None, :] * rate)

        def sub_step(start_state, entry_pair):
            decay_end, local_end = entry_pair
            return (decay_end * start_state + local_end, start_state)

        last_state, starts = lax.scan(sub_step, carried, (decayed[:, -1], local_state[:, -1]))
        full_state = decayed * starts[:, None] + local_state
        output = jnp.sum(cmat_part[:, :, :, None] * full_state, axis=2) + skip_gain * act_part
        return (last_state, output)

    last_state, outputs = lax.scan(
        jax.checkpoint(span_step), jnp.zeros((states, channels), activated.dtype), inputs_all
    )
    return outputs.reshape(length, channels)


def mixer_tail(activated, gate_in, delta_lin, select_tail, channel):
    states = select_tail.shape[1] // 2
    delta = jax.nn.softplus(delta_lin + channel[CONV + 1])
    rate = jnp.exp(channel[CONV + 3 :])
    scanned = block_scan(
        activated, delta, select_tail[:, :states], select_tail[:, states:], rate, channel[CONV + 2]
    )
    return scanned * jax.nn.silu(gate_in)


def gelu_exact(values):
    return jax.nn.gelu(values, approximate=False)


def nesterov(weight, velocity, average, step_grad, rate):
    momentum = MOMENT * velocity + step_grad
    new_weight = weight - rate * (step_grad + MOMENT * momentum)
    smoothed = SMOOTH * average + (1.0 - SMOOTH) * new_weight
    return [new_weight, momentum, smoothed, new_weight.astype(jnp.bfloat16)]


def body(
    block_input,
    cotangent,
    expert_ids,
    slot_ids,
    inward_proj,
    select_proj,
    delta_proj,
    channel_params,
    outward_proj,
    expert_up,
    expert_down,
    norm_gains,
    router_weight,
    inward_velocity,
    select_velocity,
    delta_velocity,
    channel_velocity,
    outward_velocity,
    upward_velocity,
    downward_velocity,
    gains_velocity,
    router_velocity,
    inward_average,
    select_average,
    delta_average,
    channel_average,
    outward_average,
    upward_average,
    downward_average,
    gains_average,
    router_average,
):
    tok_rows, width = block_input.shape
    sources = lax.axis_size("mp")
    inward_b, select_b, delta_b, channel_b, outward_b, up_b, down_b = (
        lax.all_gather(inward_proj.astype(jnp.bfloat16), "dp", axis=2, tiled=True),
        lax.all_gather(select_proj.astype(jnp.bfloat16), "dp", axis=0, tiled=True),
        lax.all_gather(delta_proj.astype(jnp.bfloat16), "dp", axis=1, tiled=True),
        lax.all_gather(channel_params.astype(jnp.bfloat16), "dp", axis=1, tiled=True),
        lax.all_gather(outward_proj.astype(jnp.bfloat16), "dp", axis=0, tiled=True),
        lax.all_gather(expert_up.astype(jnp.bfloat16), "dp", axis=2, tiled=True),
        lax.all_gather(expert_down.astype(jnp.bfloat16), "dp", axis=1, tiled=True),
    )
    source = block_input.astype(jnp.float32)
    normed, norm_back_first = jax.vjp(rms_norm, source, norm_gains[0])
    normed_b = normed.astype(jnp.bfloat16)
    sequence_rows = lax.all_gather(normed_b, "mp", axis=0, tiled=True)
    conv_in = jnp.dot(sequence_rows, inward_b[0], preferred_element_type=jnp.float32)
    gate_in = jnp.dot(sequence_rows, inward_b[1], preferred_element_type=jnp.float32)
    channel = channel_b.astype(jnp.float32)
    activated, conv_back = jax.vjp(conv_act, conv_in, channel)
    activated_b = activated.astype(jnp.bfloat16)
    selected = lax.psum(jnp.dot(activated_b, select_b, preferred_element_type=jnp.float32), "mp")
    rank_b = selected[:, :DT_RANK].astype(jnp.bfloat16)
    delta_lin = jnp.dot(rank_b, delta_b, preferred_element_type=jnp.float32)
    gated, tail_back = jax.vjp(
        mixer_tail, activated, gate_in, delta_lin, selected[:, DT_RANK:], channel
    )
    gated_b = gated.astype(jnp.bfloat16)
    mixer_out = lax.psum_scatter(
        jnp.dot(gated_b, outward_b, preferred_element_type=jnp.float32),
        "mp",
        scatter_dimension=0,
        tiled=True,
    )
    residual = source + mixer_out
    normed_next, norm_back_second = jax.vjp(rms_norm, residual, norm_gains[1])
    logits = jnp.dot(
        normed_next, router_weight, precision=HIGHEST, preferred_element_type=jnp.float32
    )
    probs = jax.nn.softmax(logits, axis=-1)
    experts_all = router_weight.shape[1]
    choose = (expert_ids[:, None] == jnp.arange(experts_all, dtype=jnp.int32)[None, :]).astype(
        jnp.float32
    )
    gate_prob = jnp.sum(probs * choose, axis=1)
    slot_index = expert_ids * CAP + slot_ids
    outgoing = (
        jnp.zeros((experts_all * CAP, width), jnp.bfloat16)
        .at[slot_index]
        .set(normed_next.astype(jnp.bfloat16))
    )
    local_count = up_b.shape[0]
    arrived = lax.all_to_all(
        outgoing.reshape(experts_all, CAP, width), "mp", split_axis=0, concat_axis=0, tiled=True
    ).reshape(sources, local_count, CAP, width)
    up_lin = jnp.einsum("secd,edh->sech", arrived, up_b, preferred_element_type=jnp.float32)
    activation, gelu_back = jax.vjp(gelu_exact, up_lin)
    activation_b = activation.astype(jnp.bfloat16)
    expert_out = jnp.einsum(
        "sech,ehd->secd", activation_b, down_b, preferred_element_type=jnp.float32
    ).astype(jnp.bfloat16)
    returned = lax.all_to_all(
        expert_out.reshape(experts_all, CAP, width), "mp", split_axis=0, concat_axis=0, tiled=True
    )
    tokens_out = returned.reshape(experts_all * CAP, width)[slot_index].astype(jnp.float32)
    block_output = (residual + gate_prob[:, None] * tokens_out).astype(jnp.bfloat16)
    grad_out = cotangent.astype(jnp.float32)
    d_gate = jnp.sum(grad_out * tokens_out, axis=1)
    d_logits = (d_gate * gate_prob)[:, None] * (choose - probs)
    d_tokens = (gate_prob[:, None] * grad_out).astype(jnp.bfloat16)
    back_out = jnp.zeros((experts_all * CAP, width), jnp.bfloat16).at[slot_index].set(d_tokens)
    d_buffer = lax.all_to_all(
        back_out.reshape(experts_all, CAP, width), "mp", split_axis=0, concat_axis=0, tiled=True
    ).reshape(sources, local_count, CAP, width)
    d_activation = jnp.einsum(
        "secd,ehd->sech", d_buffer, down_b, preferred_element_type=jnp.float32
    )
    d_up = gelu_back(d_activation)[0].astype(jnp.bfloat16)
    grad_down = jnp.einsum(
        "sech,secd->ehd", activation_b, d_buffer, preferred_element_type=jnp.float32
    )
    grad_up = jnp.einsum("secd,sech->edh", arrived, d_up, preferred_element_type=jnp.float32)
    d_rows = jnp.einsum("sech,edh->secd", d_up, up_b, preferred_element_type=jnp.float32).astype(
        jnp.bfloat16
    )
    d_arrived = lax.all_to_all(
        d_rows.reshape(experts_all, CAP, width), "mp", split_axis=0, concat_axis=0, tiled=True
    )
    router_part = lax.dot_general(
        d_logits,
        router_weight,
        (((1,), (1,)), ((), ())),
        precision=HIGHEST,
        preferred_element_type=jnp.float32,
    )
    d_normed_next = (
        d_arrived.reshape(experts_all * CAP, width)[slot_index].astype(jnp.float32) + router_part
    )
    grad_router = lax.dot_general(
        normed_next,
        d_logits,
        (((0,), (0,)), ((), ())),
        precision=HIGHEST,
        preferred_element_type=jnp.float32,
    )
    d_residual_norm, grad_gain_second = norm_back_second(d_normed_next)
    d_residual = grad_out + d_residual_norm
    d_mixer_b = d_residual.astype(jnp.bfloat16)
    portion = lax.all_gather(d_mixer_b, "mp", axis=0, tiled=True)
    d_part = contract_cols(portion, outward_b)
    weight_sum = contract_rows(gated_b, portion)
    d_activated_tail, d_gate_in, d_delta_lin, d_select_tail, grad_channel_tail = tail_back(d_part)
    d_delta_b = d_delta_lin.astype(jnp.bfloat16)
    grad_delta = contract_rows(rank_b, d_delta_b)
    d_rank = contract_cols(d_delta_b, delta_b)
    d_selected = lax.psum(
        jnp.concatenate([d_rank, d_select_tail], axis=1).astype(jnp.bfloat16), "mp"
    )
    grad_select = contract_rows(activated_b, d_selected)
    d_activated = d_activated_tail + contract_cols(d_selected, select_b)
    d_conv_in, grad_channel_conv = conv_back(d_activated)
    grad_channel = grad_channel_tail + grad_channel_conv
    d_conv_b = d_conv_in.astype(jnp.bfloat16)
    d_gate_b = d_gate_in.astype(jnp.bfloat16)
    grad_inward = jnp.stack(
        [contract_rows(sequence_rows, d_conv_b), contract_rows(sequence_rows, d_gate_b)]
    )
    d_normed = lax.psum_scatter(
        (contract_cols(d_conv_b, inward_b[0]) + contract_cols(d_gate_b, inward_b[1])).astype(
            jnp.bfloat16
        ),
        "mp",
        scatter_dimension=0,
        tiled=True,
    ).astype(jnp.float32)
    d_source_norm, grad_gain_first = norm_back_first(d_normed)
    block_grad = d_residual + d_source_norm
    reduced = tuple(
        (
            lax.psum_scatter(
                grad_inward.astype(jnp.bfloat16), "dp", scatter_dimension=2, tiled=True
            ).astype(jnp.float32),
            lax.psum_scatter(
                grad_select.astype(jnp.bfloat16), "dp", scatter_dimension=0, tiled=True
            ).astype(jnp.float32),
            lax.psum_scatter(
                grad_delta.astype(jnp.bfloat16), "dp", scatter_dimension=1, tiled=True
            ).astype(jnp.float32),
            lax.psum_scatter(
                grad_channel.astype(jnp.bfloat16), "dp", scatter_dimension=1, tiled=True
            ).astype(jnp.float32),
            lax.psum_scatter(
                weight_sum.astype(jnp.bfloat16), "dp", scatter_dimension=0, tiled=True
            ).astype(jnp.float32),
            lax.psum_scatter(
                grad_up.astype(jnp.bfloat16), "dp", scatter_dimension=2, tiled=True
            ).astype(jnp.float32),
            lax.psum_scatter(
                grad_down.astype(jnp.bfloat16), "dp", scatter_dimension=1, tiled=True
            ).astype(jnp.float32),
        )
    )
    shared = lax.psum((jnp.stack([grad_gain_first, grad_gain_second]), grad_router), ("dp", "mp"))
    factor = 1.0 / math.sqrt(tok_rows * lax.axis_size("dp") * sources)
    gradients = reduced + tuple(shared)
    masters = (
        inward_proj,
        select_proj,
        delta_proj,
        channel_params,
        outward_proj,
        expert_up,
        expert_down,
        norm_gains,
        router_weight,
    )
    velocities = (
        inward_velocity,
        select_velocity,
        delta_velocity,
        channel_velocity,
        outward_velocity,
        upward_velocity,
        downward_velocity,
        gains_velocity,
        router_velocity,
    )
    averages = (
        inward_average,
        select_average,
        delta_average,
        channel_average,
        outward_average,
        upward_average,
        downward_average,
        gains_average,
        router_average,
    )
    results = [block_output, block_grad]
    for position in range(9):
        results.extend(
            nesterov(
                masters[position],
                velocities[position],
                averages[position],
                gradients[position] * factor,
                LEARNING[position],
            )
        )
    return tuple(results)


def solution(mesh):
    in_specs = (
        P(("dp", "mp"), None),
        P(("dp", "mp"), None),
        P(("dp", "mp")),
        P(("dp", "mp")),
        P(None, None, ("dp", "mp")),
        P(("dp", "mp"), None),
        P(None, ("dp", "mp")),
        P(None, ("dp", "mp")),
        P(("dp", "mp"), None),
        P("mp", None, "dp"),
        P("mp", "dp", None),
        P(),
        P(),
        P(None, None, ("dp", "mp")),
        P(("dp", "mp"), None),
        P(None, ("dp", "mp")),
        P(None, ("dp", "mp")),
        P(("dp", "mp"), None),
        P("mp", None, "dp"),
        P("mp", "dp", None),
        P(),
        P(),
        P(None, None, ("dp", "mp")),
        P(("dp", "mp"), None),
        P(None, ("dp", "mp")),
        P(None, ("dp", "mp")),
        P(("dp", "mp"), None),
        P("mp", None, "dp"),
        P("mp", "dp", None),
        P(),
        P(),
    )
    out_specs = (
        P(("dp", "mp"), None),
        P(("dp", "mp"), None),
        P(None, None, ("dp", "mp")),
        P(None, None, ("dp", "mp")),
        P(None, None, ("dp", "mp")),
        P(None, None, ("dp", "mp")),
        P(("dp", "mp"), None),
        P(("dp", "mp"), None),
        P(("dp", "mp"), None),
        P(("dp", "mp"), None),
        P(None, ("dp", "mp")),
        P(None, ("dp", "mp")),
        P(None, ("dp", "mp")),
        P(None, ("dp", "mp")),
        P(None, ("dp", "mp")),
        P(None, ("dp", "mp")),
        P(None, ("dp", "mp")),
        P(None, ("dp", "mp")),
        P(("dp", "mp"), None),
        P(("dp", "mp"), None),
        P(("dp", "mp"), None),
        P(("dp", "mp"), None),
        P("mp", None, "dp"),
        P("mp", None, "dp"),
        P("mp", None, "dp"),
        P("mp", None, "dp"),
        P("mp", "dp", None),
        P("mp", "dp", None),
        P("mp", "dp", None),
        P("mp", "dp", None),
        P(),
        P(),
        P(),
        P(),
        P(),
        P(),
        P(),
        P(),
    )
    return jax.shard_map(body, mesh=mesh, in_specs=in_specs, out_specs=out_specs, check_vma=False)
```

profile of v0, /device:TPU:0, one launch (start us, length us, event | category | flops | bytes accessed | tf_op | source)
XLA Modules:
  0.0 2603.9 jit_solution(421361877656191031)
XLA Ops:
  14.4 32.5 %all-gather = bf16[8,72,23]{1,2,0:T(8,128)(2,1)S(1)} all-gather(bf16[1,72,23]{1,2,0:T(8,128)(2,1)S(1)} %convert_bitcast_fusion), channel_id=1, replica_groups=mesh['dp'=8,'mp'=4] {'dp'}, dimensions={0}, use_global_device_ids=true | all-gather | bytes 29808 | tf_op jit(solution)/shard_map/all_gather | solution.py:148
  47.1 31.0 %all_gather.30 = bf16[576,104]{1,0:T(8,128)(2,1)S(1)} all-gather(bf16[72,104]{1,0:T(8,128)(2,1)S(1)} %convert_element_type.174), channel_id=1, replica_groups=mesh['dp'=8,'mp'=4] {'dp'}, dimensions={0}, use_global_device_ids=true | all-gather | bytes 134784 | tf_op jit(solution)/shard_map/all_gather | solution.py:146
  78.8 30.2 %all-gather.8.cloned.1.call-done = bf16[2048,1152]{1,0:T(8,128)(2,1)} async-done(((bf16[512,1152]{1,0:T(8,128)(2,1)}), bf16[2048,1152]{1,0:T(8,128)(2,1)}) %all-gather.8.cloned.1.call-update) | async-done | bytes 4718608 | tf_op jit(solution)/shard_map/all_gather | solution.py:156
  125.8 30.6 %all_gather.31 = bf16[72,576]{0,1:T(8,128)(2,1)S(1)} all-gather(bf16[72,72]{0,1:T(8,128)(2,1)S(1)} %copy.198), channel_id=1, replica_groups=mesh['dp'=8,'mp'=4] {'dp'}, dimensions={1}, use_global_device_ids=true | all-gather | bytes 93312 | tf_op jit(solution)/shard_map/all_gather | solution.py:147
  182.2 267.3 %while.125 = (s32[]{:T(128)}, f32[16,576]{1,0:T(8,128)S(1)}, f32[8,16,16,576]{3,2,1,0:T(8,128)}, f32[8,16,576]{2,1,0:T(8,128)}, f32[8,16,16,576]{3,2,1,0:T(8,128...) while((s32[]{:T(128)}, f32[16,576]{1,0:T(8,128)S(1)}, ...), condition=%wide.region_7.8_spmd.clone, body=%wide.region_2.7_spmd.clone.sunk | while | flops 484116992 | bytes 85109832 | solution.py:82
  477.1 75.5 %reduce-scatter.18.cloned.1.call-done = f32[512,1152]{1,0:T(8,128)} async-done(((f32[2048,1152]{1,0:T(8,128)}), f32[512,1152]{1,0:T(8,128)}) %reduce-scatter.18.cloned.1.call-update) | async-done | bytes 2359312 | tf_op jit(solution)/shard_map/reduce_scatter | solution.py:169
  590.0 74.7 %all-gather.14.cloned.1.call-done = bf16[1,1152,3072]{2,1,0:T(8,128)(2,1)} async-done(((bf16[1,1152,384]{2,1,0:T(8,128)(2,1)}), bf16[1,1152,3072]{2,1,0:T(8,128)(2,1)}) %all-gather.14.cloned.1.call-update) | async-done | bytes 7077904 | tf_op jit(solution)/shard_map/all_gather | solution.py:150
  677.2 27.8 %fusion.62 = bf16[1,3072,1152]{2,1,0:T(8,128)(2,1)} fusion(bf16[4,192,1152]{2,1,0:T(8,128)(2,1)S(1)} %all-to-all-done.2, f32[4,192,3072]{2,1,0:T(8,128)} %fusion.87), kind=kOutput, calls=%fused_computation.128 | convolution fusion | flops 5592711168 | bytes 18284544 | tf_op jit(solution)/shard_map/sech,secd->ehd/dot_general | solution.py:219
  705.1 127.3 %reduce-scatter.22.cloned.1.call-done = bf16[1,384,1152]{2,1,0:T(8,128)(2,1)} async-done(((bf16[1,3072,1152]{2,1,0:T(8,128)(2,1)}), bf16[1,384,1152]{2,1,0:T(8,128)(2,1)}) %reduce-scatter.22.cloned.1.call-update) | async-done | bytes 884752 | tf_op jit(solution)/shard_map/reduce_scatter | solution.py:298
  836.5 108.0 %all-gather.16.cloned.1.call-done = bf16[1,3072,1152]{2,1,0:T(8,128)(2,1)} async-done(((bf16[1,384,1152]{2,1,0:T(8,128)(2,1)}), bf16[1,3072,1152]{2,1,0:T(8,128)(2,1)}) %all-gather.16.cloned.1.call-update) | async-done | bytes 7077904 | tf_op jit(solution)/shard_map/all_gather | solution.py:151
  944.5 30.3 %fusion.69 = bf16[4,1,192,3072]{3,2,0,1:T(8,128)(2,1)S(1)} fusion(f32[4,192,3072]{2,1,0:T(8,128)} %fusion.87, bf16[4,192,1152]{2,1,0:T(8,128)(2,1)} %copy-done.30, bf16[1,3072,1152]{2,1,0:T(8,128)(2,1)} %all-gather.16.cloned.1.call-done), kind=kOutput, calls=%fused_computation.137 | convolution fusion | flops 5605687296 | bytes 23003136 | tf_op jit(solution)/shard_map/secd,ehd->sech/dot_general | solution.py:215
  991.1 29.7 %fusion.110 = bf16[4,192,1152]{2,1,0:T(8,128)(2,1)} fusion(bf16[1,3072,1152]{2,1,0:T(8,128)(2,1)} %all-gather.16.cloned.1.call-done, f32[4,192,3072]{2,1,0:T(8,128)} %fusion.87), kind=kOutput, calls=%fused_computation.207 | convolution fusion | flops 5590056960 | bytes 18284544 | tf_op jit(solution)/shard_map/sech,ehd->secd/dot_general | solution.py:199
  1027.5 19.0 all-to-all-done.1
  1063.7 34.8 %all-gather.18.cloned.1.call-done = bf16[2048,1152]{1,0:T(8,128)(2,1)} async-done(((bf16[512,1152]{1,0:T(8,128)(2,1)}), bf16[2048,1152]{1,0:T(8,128)(2,1)}) %all-gather.18.cloned.1.call-update) | async-done | bytes 4718608 | tf_op jit(solution)/shard_map/all_gather | solution.py:249
  1124.7 910.0 %while.128 = (s32[]{:T(128)}, f32[16,576]{1,0:T(8,128)}, f32[576]{0:T(1024)S(1)}, f32[16,576]{1,0:T(8,128)S(1)}, f32[8,16,16,576]{3,2,1,0:T(8,128)}, /*index=5*/...) while((s32[]{:T(128)}, f32[16,576]{1,0:T(8,128)}, ...), condition=%wide.region_34.35_spmd.clone, body=%wide.region_17.34_spmd.clone.sunk | while | flops 1032092736 | bytes 223206736 | solution.py:82
  1136.3 17.8 multiply_exponential_fusion.7
  1174.6 23.0 while.131
  1199.9 20.2 fusion.241
  1250.0 17.8 multiply_exponential_fusion.7
  1288.3 23.0 while.131
  1313.6 20.2 fusion.241
  1363.7 17.8 multiply_exponential_fusion.7
  1402.0 23.0 while.131
  1427.3 20.2 fusion.241
  1477.4 17.8 multiply_exponential_fusion.7
  1515.7 23.0 while.131
  1541.0 20.2 fusion.241
  1591.0 17.8 multiply_exponential_fusion.7
  1629.4 23.0 while.131
  1654.7 20.2 fusion.241
  1704.7 17.8 multiply_exponential_fusion.7
  1743.1 23.0 while.131
  1768.4 20.2 fusion.241
  1818.4 17.8 multiply_exponential_fusion.7
  1856.7 23.0 while.131
  1882.0 20.2 fusion.241
  1932.1 17.8 multiply_exponential_fusion.7
  1970.4 23.0 while.131
  1995.7 20.2 fusion.241
  2054.2 31.4 %all-reduce.29.cloned.1.call-done = bf16[2048,104]{0,1:T(8,128)(2,1)} async-done(((bf16[2048,104]{0,1:T(8,128)(2,1)}), bf16[2048,104]{0,1:T(8,128)(2,1)}) %all-reduce.29.cloned.1.call-update) | async-done | bytes 426000 | tf_op jit(solution)/shard_map/psum | solution.py:256
  2108.9 17.4 multiply_reduce_fusion.11
  2155.7 30.2 %copy.228 = bf16[1,1152,3072]{1,0,2:T(2,128)(2,1)} copy(bf16[1,1152,3072]{2,1,0:T(8,128)(2,1)} %fusion.61) | data formatting | bytes 14155776
  2221.1 37.7 %all-reduce.20 = bf16[23,576]{1,0:T(8,128)(2,1)S(1)} all-reduce(bf16[23,576]{1,0:T(8,128)(2,1)S(1)} %add_convert_fusion.2), channel_id=7, replica_groups=mesh['dp'=8,'mp'=4] {'dp'}, use_global_device_ids=true, to_apply=%region_47.48.clone | all-reduce | flops 13248 | bytes 52992
  2264.3 23.1 reduce-scatter.30.cloned.1.call-done
  2291.8 68.6 %reduce-scatter.24.cloned.1.call-done = bf16[72,2304]{1,0:T(8,128)(2,1)} async-done(((bf16[576,2304]{1,0:T(8,128)(2,1)}), bf16[72,2304]{1,0:T(8,128)(2,1)}) %reduce-scatter.24.cloned.1.call-update) | async-done | bytes 331792
  2366.6 125.9 %reduce-scatter.26.cloned.1.call-done = bf16[384,1152]{1,0:T(8,128)(2,1)} async-done(((bf16[3072,1152]{1,0:T(8,128)(2,1)}), bf16[384,1152]{1,0:T(8,128)(2,1)}) %reduce-scatter.26.cloned.1.call-update) | async-done | bytes 884752
  2506.8 35.1 %reduce-scatter.20.cloned.1.call-done = bf16[512,1152]{1,0:T(8,128)(2,1)} async-done(((bf16[2048,1152]{1,0:T(8,128)(2,1)}), bf16[512,1152]{1,0:T(8,128)(2,1)}) %reduce-scatter.20.cloned.1.call-update) | async-done | bytes 1179664 | tf_op jit(solution)/shard_map/reduce_scatter | solution.py:268
  2546.7 40.4 %all-reduce.22 = (f32[2,1152]{1,0:T(2,128)}, f32[1152,4]{0,1:T(4,128)}) all-reduce(f32[2,1152]{1,0:T(2,128)} %pad_maximum_fusion.2, f32[1152,4]{0,1:T(4,128)} %fusion.126), channel_id=1, replica_groups=mesh['dp'=8,'mp'=4] {'dp','mp'}, use_global_device_ids=true, to_apply=%region_53.54 | all-reduce | flops 6912 | bytes 55296 | tf_op jit(solution)/shard_map/psum | solution.py:303
  (1987 shorter events, 1323.9 us)
Async XLA Ops:
  7.2 71.5 %all-gather.10.cloned.1.call-start = ((), (), s32[]{:S(2)}) async-start(), calls=%async_computation.12 | async-start | bytes 2985984 | tf_op jit(solution)/shard_map/all_gather | solution.py:145
  9.2 99.8 %all-gather.8.cloned.1.call-start = ((), (), s32[]{:S(2)}) async-start(), calls=%async_computation.11 | async-start | bytes 5898240 | tf_op jit(solution)/shard_map/all_gather | solution.py:156
  10.0 554.1 %copy-start.49 = (f32[1152]{0:T(1024)}, f32[1152]{0:T(1024)S(1)}, u32[]{:S(2)}) copy-start(f32[1152]{0:T(1024)S(1)} %get-tuple-element.1005) | copy-start | bytes 13828
  14.3 148.0 %all-reduce.27.cloned.1.call-start = ((), (), s32[]{:S(2)}) async-start(), calls=%async_computation.13 | async-start | bytes 1703936 | tf_op jit(solution)/shard_map/psum | solution.py:162
  47.0 78.0 %copy-start.47 = (f32[576,23]{0,1:T(8,128)}, f32[576,23]{0,1:T(8,128)S(1)}, u32[]{:S(2)}) copy-start(f32[576,23]{0,1:T(8,128)S(1)} %reshape.389) | copy-start | bytes 158980
  78.1 42.4 %copy-start.42 = (bf16[576,104]{1,0:T(8,128)(2,1)}, bf16[576,104]{1,0:T(8,128)(2,1)S(1)}, u32[]{:S(2)}) copy-start(bf16[576,104]{1,0:T(8,128)(2,1)S(1)} %all_gather.30) | copy-start | bytes 359428
  78.7 35.7 %copy-start.82 = (f32[576]{0:T(1024)}, f32[576]{0:T(1024)S(1)}, u32[]{:S(2)}) copy-start(f32[576]{0:T(1024)S(1)} %get-tuple-element.1000) | copy-start | bytes 6916
  78.7 35.7 %copy-start.84 = (f32[576]{0:T(1024)}, f32[576]{0:T(1024)S(1)}, u32[]{:S(2)}) copy-start(f32[576]{0:T(1024)S(1)} %get-tuple-element.1001) | copy-start | bytes 6916
  78.7 35.7 %copy-start.86 = (f32[576]{0:T(1024)}, f32[576]{0:T(1024)S(1)}, u32[]{:S(2)}) copy-start(f32[576]{0:T(1024)S(1)} %get-tuple-element.1002) | copy-start | bytes 6916
  78.7 35.7 %copy-start.88 = (f32[576]{0:T(1024)}, f32[576]{0:T(1024)S(1)}, u32[]{:S(2)}) copy-start(f32[576]{0:T(1024)S(1)} %get-tuple-element.1003) | copy-start | bytes 6916
  78.7 88.5 %copy-start.80 = (f32[576]{0:T(1024)}, f32[576]{0:T(1024)S(1)}, u32[]{:S(2)}) copy-start(f32[576]{0:T(1024)S(1)} %get-tuple-element.999) | copy-start | bytes 6916
  124.2 339.9 %all-gather.12.cloned.1.call-start = ((), (), s32[]{:S(2)}) async-start(), calls=%async_computation.14 | async-start | bytes 1492992 | tf_op jit(solution)/shard_map/all_gather | solution.py:149
  125.0 427.6 %reduce-scatter.18.cloned.1.call-start = ((), (), s32[]{:S(2)}) async-start(), calls=%async_computation.15 | async-start | bytes 11796480 | tf_op jit(solution)/shard_map/reduce_scatter | solution.py:169
  474.0 78.6 %copy-start.16 = (bf16[512,1152]{1,0:T(8,128)(2,1)S(1)}, bf16[512,1152]{1,0:T(8,128)(2,1)}, u32[]{:S(2)}) copy-start(bf16[512,1152]{1,0:T(8,128)(2,1)} %param.41) | copy-start | bytes 3538948
  474.0 190.8 %all-gather.14.cloned.1.call-start = ((), (), s32[]{:S(2)}) async-start(), calls=%async_computation.16 | async-start | bytes 7962624 | tf_op jit(solution)/shard_map/all_gather | solution.py:150
  559.5 26.9 %all-to-all-start = ((bf16[4,192,1152]{2,1,0:T(8,128)(2,1)}), bf16[4,192,1152]{2,1,0:T(8,128)(2,1)}, u32[]{:S(2)}, u32[]{:S(2)}) async-start(bf16[4,192,1152]{2,1,0:T(8,128)(2,1)} %bitcast.452), calls=%async_computation.1 | async-start | bytes 3538944 | tf_op jit(solution)/shard_map/all_to_all | solution.py:193
  567.9 108.1 %copy-start.73 = (f32[512]{0:T(512)}, f32[512]{0:T(512)S(1)}, u32[]{:S(2)}) copy-start(f32[512]{0:T(512)S(1)} %get-tuple-element.1124) | copy-start | bytes 6148
  586.4 89.6 %all-to-all-start.2 = ((bf16[4,192,1152]{2,1,0:T(8,128)(2,1)}), bf16[4,192,1152]{2,1,0:T(8,128)(2,1)S(1)}, u32[]{:S(2)}, u32[]{:S(2)}) async-start(bf16[4,192,1152]{2,1,0:T(8,128)(2,1)} %bitcast.38), calls=%async_computation.3 | async-start | bytes 3538944 | tf_op jit(solution)/shard_map/all_to_all | solution.py:212
  590.0 242.4 %reduce-scatter.22.cloned.1.call-start = ((), (), s32[]{:S(2)}) async-start(), calls=%async_computation.21 | async-start | bytes 7962624 | tf_op jit(solution)/shard_map/reduce_scatter | solution.py:298
  705.0 127.4 %copy-start.28 = (f32[1,384,1152]{2,1,0:T(8,128)S(1)}, f32[1,384,1152]{2,1,0:T(8,128)}, u32[]{:S(2)}) copy-start(f32[1,384,1152]{2,1,0:T(8,128)} %param.51) | copy-start | bytes 5308420
  705.0 127.4 %copy-start.29 = (f32[1,384,1152]{2,1,0:T(8,128)S(1)}, f32[1,384,1152]{2,1,0:T(8,128)}, u32[]{:S(2)}) copy-start(f32[1,384,1152]{2,1,0:T(8,128)} %param.60) | copy-start | bytes 5308420
  705.0 239.4 %all-gather.16.cloned.1.call-start = ((), (), s32[]{:S(2)}) async-start(), calls=%async_computation.17 | async-start | bytes 7962624 | tf_op jit(solution)/shard_map/all_gather | solution.py:151
  987.3 33.5 %all-to-all-start.3 = ((bf16[4,192,1152]{2,1,0:T(8,128)(2,1)}), bf16[4,192,1152]{2,1,0:T(8,128)(2,1)S(1)}, u32[]{:S(2)}, u32[]{:S(2)}) async-start(bf16[4,192,1152]{2,1,0:T(8,128)(2,1)} %fusion.105), calls=%async_computation.4 | async-start | bytes 3538944 | tf_op jit(solution)/shard_map/all_to_all | solution.py:226
  991.1 33.3 %copy-start.91 = (s32[512]{0:T(512)S(1)}, s32[512]{0:T(512)}, u32[]{:S(2)}) copy-start(s32[512]{0:T(512)} %compare_select_fusion.3) | copy-start | bytes 6148
  1020.8 25.7 all-to-all-start.1
  1024.4 74.2 %all-gather.18.cloned.1.call-start = ((), (), s32[]{:S(2)}) async-start(), calls=%async_computation.18 | async-start | bytes 5898240 | tf_op jit(solution)/shard_map/all_gather | solution.py:249
  1063.7 1021.9 %all-reduce.29.cloned.1.call-start = ((), (), s32[]{:S(2)}) async-start(), calls=%async_computation.19 | async-start | bytes 851968 | tf_op jit(solution)/shard_map/psum | solution.py:256
  1198.1 22.0 slice-start
  1311.8 22.0 slice-start
  1425.5 22.0 slice-start
  1539.2 22.0 slice-start
  1652.9 22.0 slice-start
  1766.6 22.0 slice-start
  1880.2 22.0 slice-start
  1993.9 22.0 slice-start
  2052.5 162.8 %all-reduce.31.cloned.1.call-start = ((), (), s32[]{:S(2)}) async-start(), calls=%async_computation.24 | async-start | bytes 184320
  2054.1 35.4 %copy-start.97 = (bf16[2048,576]{0,1:T(8,128)(2,1)S(1)}, bf16[2048,576]{0,1:T(8,128)(2,1)}, u32[]{:S(2)}) copy-start(bf16[2048,576]{0,1:T(8,128)(2,1)} %get-tuple-element.1166) | copy-start | bytes 7077892
  2054.1 207.4 %reduce-scatter.28.cloned.1.call-start = ((), (), s32[]{:S(2)}) async-start(), calls=%async_computation.25 | async-start | bytes 165888
  2089.4 198.0 %reduce-scatter.30.cloned.1.call-start = ((), (), s32[]{:S(2)}) async-start(), calls=%async_computation.26 | async-start | bytes 1492992
  2102.0 258.4 %reduce-scatter.24.cloned.1.call-start = ((), (), s32[]{:S(2)}) async-start(), calls=%async_computation.22 | async-start | bytes 2985984
  2145.6 346.9 %reduce-scatter.26.cloned.1.call-start = ((), (), s32[]{:S(2)}) async-start(), calls=%async_computation.23 | async-start | bytes 7962624
  2195.0 346.8 %reduce-scatter.20.cloned.1.call-start = ((), (), s32[]{:S(2)}) async-start(), calls=%async_computation.20 | async-start | bytes 5898240 | tf_op jit(solution)/shard_map/reduce_scatter | solution.py:268
  2207.1 80.3 %copy-start.37 = (f32[72,1152]{1,0:T(8,128)S(1)}, f32[72,1152]{1,0:T(8,128)}, u32[]{:S(2)}) copy-start(f32[72,1152]{1,0:T(8,128)} %param.49) | copy-start | bytes 995332
  2208.9 152.6 %copy-start.26 = (f32[2,1152,72]{1,2,0:T(8,128)S(1)}, f32[2,1152,72]{1,2,0:T(8,128)}, u32[]{:S(2)}) copy-start(f32[2,1152,72]{1,2,0:T(8,128)} %param.45) | copy-start | bytes 1990660
  2216.8 75.0 %copy-start.53 = (f32[72,72]{1,0:T(8,128)}, f32[72,72]{1,0:T(8,128)S(1)}, u32[]{:S(2)}) copy-start(f32[72,72]{1,0:T(8,128)S(1)} %get-tuple-element.1116) | copy-start | bytes 62212
  2262.9 232.9 %copy-start.54 = (f32[72,104]{1,0:T(8,128)}, f32[72,104]{1,0:T(8,128)S(1)}, u32[]{:S(2)}) copy-start(f32[72,104]{1,0:T(8,128)S(1)} %get-tuple-element.1119) | copy-start | bytes 89860
  2504.1 37.7 %copy-start.17 = (bf16[512,1152]{1,0:T(8,128)(2,1)S(1)}, bf16[512,1152]{1,0:T(8,128)(2,1)}, u32[]{:S(2)}) copy-start(bf16[512,1152]{1,0:T(8,128)(2,1)} %param.41) | copy-start | bytes 3538948
  2504.1 37.7 %copy-start.59 = (f32[1152]{0:T(1024)S(1)}, f32[1152]{0:T(1024)}, u32[]{:S(2)}) copy-start(f32[1152]{0:T(1024)} %copy-done.58) | copy-start | bytes 13828
  (201 other events, 2381.3 us)
Sparse Core Ops, SparseCore 0:
  10.9 59.5 all-gather.9
  72.6 36.2 all-gather.7
  124.3 34.9 all-reduce.26
  162.2 42.3 all-gather.11
  474.1 78.3 reduce-scatter.17
  555.3 109.4 all-gather.13
  705.2 127.1 reduce-scatter.21
  836.6 107.8 all-gather.15
  1063.8 34.7 all-gather.17
  2052.7 32.8 all-reduce.28
  2089.9 69.3 all-reduce.30
  2163.3 57.4 reduce-scatter.27
  2224.9 62.4 reduce-scatter.29
  2290.9 69.4 reduce-scatter.23
  2364.4 128.0 reduce-scatter.25
  2494.9 46.8 reduce-scatter.19
where the time goes:
time: 2630 us; the launch traced here: 2600 us
  waiting for transfers between devices  768 us (29%)
  matrix products  633 us (24%)
  other arithmetic  626 us (24%)
  local copies, waits for them, and re-layouts  359 us (14%)
  blocking collectives  172 us (7%)
    dot_general x24, matrix products, span_step(): summed = jnp.einsum('tj,sjnc->stnc', lower_ones, driven, precision=HIGHEST)  406 us
    unnamed x21, waiting for transfers between devices  218 us
    reduce_scatter x1, waiting for transfers between devices, body(): lax.psum_scatter(grad_down.astype(jnp.bfloat16), 'dp', scatter_dimension=...  127 us
    reduce_sum x8, other arithmetic, span_step(): decayed = jnp.exp(-elapsed[:, :, None, :] * rate)  123 us
    all_gather x1, waiting for transfers between devices, body(): lax.all_gather(expert_down.astype(jnp.bfloat16), 'dp', axis=1, tiled=True)  108 us
    add x256, other arithmetic, sub_step(): return (decay_end * start_state + local_end, start_state)  105 us
    add_any x128, other arithmetic, sub_step(): return (decay_end * start_state + local_end, start_state)  103 us
    dynamic_update_slice x128, other arithmetic, span_step(): lax.scan(sub_step, carried, (decayed[:, -1], local_state[:, -1]))  80.2 us
  transfers between devices with their start and end apart: 20, of which 13 were waited for; matrix products, arithmetic and copies ran while one was open for 19% of the time, Pallas kernels for 0%

commit v1 on v0

v1 whole, which is shorter than its diff:
```python
import functools
import math

import jax
import jax.numpy as jnp
from jax import lax
from jax.experimental import pallas as pl
from jax.experimental.pallas import tpu as pltpu
from jax.sharding import PartitionSpec as P

bf16=jnp.bfloat16; f32=jnp.float32
CONV=4; DT_RANK=72; SUBT=16; NST=16
LOG2E=1.0/math.log(2.0)

def dotf(a,b,dims=((1,),(0,))):
    return lax.dot_general(a,b,(dims,((),())),preferred_element_type=f32)

def block_mask():
    r=lax.broadcasted_iota(jnp.int32,(SUBT,SUBT*NST),0)
    c=lax.broadcasted_iota(jnp.int32,(SUBT,SUBT*NST),1)
    return (c//NST==r).astype(f32)

def spread(first, rows):
    r=lax.broadcasted_iota(jnp.int32,(rows,SUBT*NST),0)
    c=lax.broadcasted_iota(jnp.int32,(rows,SUBT*NST),1)
    return (c%NST+first==r).astype(bf16)

def soft_parts(x):
    e=jnp.exp(-jnp.abs(x))
    return jnp.maximum(x,0.0)+jnp.log1p(e), jnp.where(x>=0,1.0,e)/(1.0+e)

def row8(ref,k,t):
    d=ref[k,pl.ds(t,8,stride=0),:]
    return jnp.concatenate([d,d],0)

def split_states(sel_ref,bts,cts,T):
    wide=sel_ref.shape[1]
    selT=jnp.concatenate([sel_ref[...],jnp.zeros((T,128-wide),f32)],1).T
    for k in range(T//SUBT):
        bts[k]=selT[DT_RANK:DT_RANK+NST,SUBT*k:SUBT*k+SUBT]
        cts[k]=selT[DT_RANK+NST:DT_RANK+2*NST,SUBT*k:SUBT*k+SUBT]

def blocked(sel_ref,k,place,mask):
    sel=sel_ref[pl.ds(pl.multiple_of(k*SUBT,SUBT),SUBT),:]
    return (dotf(sel.astype(bf16),place)*mask).astype(bf16)

def scan_fwd_kernel(rank_ref, delta_w_ref, act_ref, gate_ref, sel_ref, chan_ref, out_w_ref,
                    s_ref, xlin_ref, scanned_ref, gated_ref, mix_ref,
                    state, dscr, uscr, yscr, bts, cts, sA, sB, *, T):
    C=act_ref.shape[1]; NCH=T//SUBT
    @pl.when(pl.program_id(0)==0)
    def _():
        state[...]=jnp.zeros_like(state)
    x=dotf(rank_ref[...],delta_w_ref[...])+chan_ref[CONV+1:CONV+2,:]
    xlin_ref[...]=x
    sp,_=soft_parts(x)
    dscr[...]=sp.reshape(NCH,SUBT,C)
    uscr[...]=(sp*act_ref[...]).reshape(NCH,SUBT,C)
    split_states(sel_ref,bts,cts,T)
    nrate=-LOG2E*jnp.exp(chan_ref[CONV+3:CONV+3+NST,:])
    mask=block_mask()
    ec=spread(DT_RANK+NST,sel_ref.shape[1])
    def one(k,S,cur,prev):
        before=jnp.maximum(k-1,0)
        yv=dotf(blocked(sel_ref,before,ec,mask),prev[...])
        bt=bts[k]
        for t in range(SUBT):
            d=row8(dscr,k,t); u=row8(uscr,k,t)
            S=jnp.exp2(d*nrate)*S+u*jnp.broadcast_to(bt[:,t:t+1],(NST,C))
            cur[t*NST:t*NST+NST,:]=S.astype(bf16)
        yscr[before]=yv
        s_ref[k]=cur[...]
        return S
    def pair(j,S):
        S=one(2*j,S,sA,sB)
        return one(2*j+1,S,sB,sA)
    sB[...]=jnp.zeros_like(sB)
    state[...]=lax.fori_loop(0,NCH//2,pair,state[...])
    yscr[NCH-1]=dotf(blocked(sel_ref,NCH-1,ec,mask),sB[...])
    scanned=yscr[...].reshape(T,C)+chan_ref[CONV+2:CONV+3,:]*act_ref[...]
    scanned_ref[...]=scanned
    g=gate_ref[...]
    gated=(scanned*(g/(1.0+jnp.exp(-g)))).astype(bf16)
    gated_ref[...]=gated
    mix_ref[...]=dotf(gated,out_w_ref[...]).astype(mix_ref.dtype)

def row_spec(T,w,rev=None):
    return pl.BlockSpec((T,w),(lambda i:(i,0)) if rev is None else (lambda i:(rev-1-i,0)))
def full_spec(a): return pl.BlockSpec(a.shape,lambda i:(0,)*a.ndim)

def scan_fwd(rank_b, delta_w, act, gate, sel, chan, out_w, T=256):
    N,C=act.shape; W=out_w.shape[1]; g=N//T; nch=T//SUBT
    row=functools.partial(row_spec,T); full=full_spec
    return pl.pallas_call(
        functools.partial(scan_fwd_kernel,T=T),
        grid=(g,),
        in_specs=[row(rank_b.shape[1]),full(delta_w),row(C),row(C),row(sel.shape[1]),full(chan),full(out_w)],
        out_specs=[pl.BlockSpec((nch,SUBT*NST,C),lambda i:(i,0,0)),row(C),row(C),row(C),row(W)],
        out_shape=[jax.ShapeDtypeStruct((N//SUBT,SUBT*NST,C),bf16),jax.ShapeDtypeStruct((N,C),f32),jax.ShapeDtypeStruct((N,C),f32),
                   jax.ShapeDtypeStruct((N,C),bf16),jax.ShapeDtypeStruct((N,W),bf16)],
        scratch_shapes=[pltpu.VMEM((NST,C),f32)]+[pltpu.VMEM((nch,SUBT,C),f32)]*3+[pltpu.VMEM((nch,NST,SUBT),f32)]*2+[pltpu.VMEM((SUBT*NST,C),bf16)]*2,
        compiler_params=pltpu.CompilerParams(vmem_limit_bytes=48*2**20),
        cost_estimate=pl.CostEstimate(flops=2*N*C*W,bytes_accessed=N*C*50+N*W*2,transcendentals=N*C*NST),
    )(rank_b,delta_w,act,gate,sel,chan,out_w)

def scan_bwd_kernel(dmix_ref, out_w_ref, s_ref, before_ref, act_ref, gate_ref, xlin_ref, scanned_ref, sel_ref, chan_ref, delta_w_ref,
                    dgate_ref, dact_ref, ddl_ref, dsel_ref, gch_ref,
                    qscr, dscr, uscr, dyscr, lbscr, wsscr, bts, cts, dbs, dcs, dselT, lA, wA, *, T, g):
    C=act_ref.shape[1]; NCH=T//SUBT
    step=pl.program_id(0)
    @pl.when(step==0)
    def _():
        qscr[...]=jnp.zeros_like(qscr)
        gch_ref[...]=jnp.zeros_like(gch_ref)
        dselT[...]=jnp.zeros_like(dselT)
    dg=dotf(dmix_ref[...],out_w_ref[...],((1,),(1,)))
    gt=gate_ref[...]; sg=1.0/(1.0+jnp.exp(-gt))
    dgate_ref[...]=(dg*scanned_ref[...]*(sg*(1.0+gt*(1.0-sg)))).astype(bf16)
    dy=dg*(gt*sg)
    act=act_ref[...]
    sp,sigd=soft_parts(xlin_ref[...])
    dscr[...]=sp.reshape(NCH,SUBT,C)
    uscr[...]=(sp*act).reshape(NCH,SUBT,C)
    dyscr[...]=dy.reshape(NCH,SUBT,C)
    split_states(sel_ref,bts,cts,T)
    rate=jnp.exp(chan_ref[CONV+3:CONV+3+NST,:]); nrate=-LOG2E*rate
    mask=block_mask()
    eb=spread(DT_RANK,sel_ref.shape[1])
    ones=mask.astype(bf16)
    lane=lax.broadcasted_iota(jnp.int32,(NST,SUBT),1)
    first=jnp.where(step==g-1,0.0,1.0)*before_ref[0,SUBT*NST-NST:SUBT*NST,:].astype(f32)
    def chunk(j,carry):
        q,acc=carry
        k=NCH-1-j
        bt=bts[k]; ct=cts[k]
        dbT=jnp.zeros((NST,SUBT),f32); dcT=dbT
        s_t=s_ref[k,SUBT*NST-NST:SUBT*NST,:].astype(f32)
        s_before=jnp.where(k==0,first,s_ref[jnp.maximum(k-1,0),SUBT*NST-NST:SUBT*NST,:].astype(f32))
        for t in range(SUBT-1,-1,-1):
            d=row8(dscr,k,t); u=row8(uscr,k,t); dyr=row8(dyscr,k,t)
            lam=jnp.broadcast_to(ct[:,t:t+1],(NST,C))*dyr+q
            lA[t*NST:t*NST+NST,:]=lam.astype(bf16)
            q=jnp.exp2(d*nrate)*lam
            dcT=jnp.where(lane==t,jnp.sum(s_t*dyr,axis=1,keepdims=True),dcT)
            dbT=jnp.where(lane==t,jnp.sum(lam*u,axis=1,keepdims=True),dbT)
            s_p=s_ref[k,t*NST-NST:t*NST,:].astype(f32) if t>0 else s_before
            wr=q*s_p*rate
            wA[t*NST:t*NST+NST,:]=wr.astype(bf16)
            acc=acc+wr*d
            s_t=s_p
        dbs[k]=dbT; dcs[k]=dcT
        lbscr[k]=dotf(blocked(sel_ref,k,eb,mask),lA[...])
        wsscr[k]=dotf(ones,wA[...])
        return q,acc
    q,acc=lax.fori_loop(0,NCH,chunk,(qscr[...],jnp.zeros((NST,C),f32)))
    qscr[...]=q
    gch_ref[CONV+3:CONV+3+NST,:]+=-acc
    lamB=lbscr[...].reshape(T,C); ws=wsscr[...].reshape(T,C)
    dyf=dyscr[...].reshape(T,C); spf=dscr[...].reshape(T,C)
    dact_ref[...]=chan_ref[CONV+2:CONV+3,:]*dyf+spf*lamB
    ddl=(act*lamB-ws)*sigd
    ddl_ref[...]=ddl.astype(bf16)
    gch_ref[CONV+1:CONV+2,:]+=jnp.sum(ddl,axis=0,keepdims=True)
    gch_ref[CONV+2:CONV+3,:]+=jnp.sum(dyf*act,axis=0,keepdims=True)
    for k in range(NCH):
        dselT[DT_RANK:DT_RANK+NST,SUBT*k:SUBT*k+SUBT]=dbs[k]
        dselT[DT_RANK+NST:DT_RANK+2*NST,SUBT*k:SUBT*k+SUBT]=dcs[k]
    dsel=dotf(ddl_ref[...],delta_w_ref[...],((1,),(1,)))+dselT[...].T
    dsel_ref[...]=dsel[:,:dsel_ref.shape[1]].astype(bf16)

def scan_bwd(dmix, out_w, s_all, act, gate, xlin, scanned, sel, chan, delta_w, T=256):
    N,C=act.shape; g=N//T; nch=T//SUBT; XW=sel.shape[1]
    row=lambda w: row_spec(T,w,g); full=full_spec
    vm=pltpu.VMEM
    return pl.pallas_call(
        functools.partial(scan_bwd_kernel,T=T,g=g),
        grid=(g,),
        in_specs=[row(dmix.shape[1]),full(out_w),pl.BlockSpec((nch,SUBT*NST,C),lambda i:(g-1-i,0,0)),
                  pl.BlockSpec((1,SUBT*NST,C),lambda i:(jnp.maximum((g-1-i)*nch-1,0),0,0)),
                  row(C),row(C),row(C),row(C),row(XW),full(chan),full(delta_w)],
        out_specs=[row(C),row(C),row(C),row(XW),pl.BlockSpec((24,C),lambda i:(0,0))],
        out_shape=[jax.ShapeDtypeStruct((N,C),bf16),jax.ShapeDtypeStruct((N,C),f32),jax.ShapeDtypeStruct((N,C),bf16),
                   jax.ShapeDtypeStruct((N,XW),bf16),jax.ShapeDtypeStruct((24,C),f32)],
        scratch_shapes=[vm((NST,C),f32)]+[vm((nch,SUBT,C),f32)]*5+[vm((nch,NST,SUBT),f32)]*4+[vm((128,T),f32)]+[vm((SUBT*NST,C),bf16)]*2,
        compiler_params=pltpu.CompilerParams(vmem_limit_bytes=56*2**20),
        cost_estimate=pl.CostEstimate(flops=2*N*C*dmix.shape[1],bytes_accessed=N*C*60,transcendentals=N*C*NST),
    )(dmix,out_w,s_all,s_all,act,gate,xlin,scanned,sel,chan,delta_w)

CAP = 192
EPSILON = 1e-05
MOMENT = 0.9
SMOOTH = 0.6
LEARNING = (0.02, 0.03, 0.4, 0.3, 0.04, 0.07, 0.3, 0.3, 0.01)
HIGHEST = lax.Precision.HIGHEST
LANES = 128


def conv_fwd_kernel(seq_ref, w_ref, chan_ref, selw_ref, conv_ref, gate_ref, pre_ref, act_ref, actb_ref, sel_ref, buf, *, T):
    C = conv_ref.shape[1]

    @pl.when(pl.program_id(0) == 0)
    def _():
        buf[0:8, :] = jnp.zeros((8, C), f32)

    seq = seq_ref[...]
    conv = dotf(seq, w_ref[0:C, :], ((1,), (1,)))
    gate_ref[...] = dotf(seq, w_ref[C : 2 * C, :], ((1,), (1,)))
    conv_ref[...] = conv
    buf[8 : 8 + T, :] = conv
    pre = chan_ref[CONV : CONV + 1, :] + chan_ref[CONV - 1 : CONV, :] * conv
    for tap in range(CONV - 1):
        pre = pre + chan_ref[tap : tap + 1, :] * buf[8 - CONV + 1 + tap : 8 - CONV + 1 + tap + T, :]
    buf[0:8, :] = buf[T : T + 8, :]
    pre_ref[...] = pre
    act = pre / (1.0 + jnp.exp(-pre))
    act_ref[...] = act
    actb = act.astype(bf16)
    actb_ref[...] = actb
    sel_ref[...] = dotf(actb, selw_ref[...])


def conv_fwd(seq, w_in, chan, selw, T=256):
    N = seq.shape[0]
    C = chan.shape[1]
    row, full = functools.partial(row_spec, T), full_spec
    XW = selw.shape[1]
    shape = jax.ShapeDtypeStruct
    return pl.pallas_call(
        functools.partial(conv_fwd_kernel, T=T),
        grid=(N // T,),
        in_specs=[row(seq.shape[1]), full(w_in), full(chan), full(selw)],
        out_specs=[row(C), row(C), row(C), row(C), row(C), row(XW)],
        out_shape=[shape((N, C), f32)] * 4 + [shape((N, C), bf16), shape((N, XW), f32)],
        scratch_shapes=[pltpu.VMEM((T + 8, C), f32)],
        compiler_params=pltpu.CompilerParams(vmem_limit_bytes=48 * 2**20),
        cost_estimate=pl.CostEstimate(
            flops=4 * N * C * seq.shape[1], bytes_accessed=N * C * 20, transcendentals=N * C
        ),
    )(seq, w_in, chan, selw)


def conv_bwd_kernel(
    dact_ref, dsel_ref, selw_ref, pre_ref, conv_ref, dgate_ref, w_ref, seq_ref, chan_ref,
    dconv_ref, dnorm_ref, gch_ref, gain_ref, buf, *, T
):
    C = conv_ref.shape[1]

    @pl.when(pl.program_id(0) == 0)
    def _():
        buf[T : T + 8, :] = jnp.zeros((8, C), f32)
        gch_ref[...] = jnp.zeros_like(gch_ref)
        gain_ref[...] = jnp.zeros_like(gain_ref)

    pre = pre_ref[...]
    sig = 1.0 / (1.0 + jnp.exp(-pre))
    dact = dact_ref[...] + dotf(dsel_ref[...], selw_ref[...], ((1,), (1,)))
    dpre = dact * (sig * (1.0 + pre * (1.0 - sig)))
    buf[0:T, :] = dpre
    conv = conv_ref[...]
    total = chan_ref[CONV - 1 : CONV, :] * dpre
    gch_ref[CONV - 1 : CONV, :] += jnp.sum(conv * dpre, axis=0, keepdims=True)
    for tap in range(CONV - 1):
        later = buf[CONV - 1 - tap : CONV - 1 - tap + T, :]
        total = total + chan_ref[tap : tap + 1, :] * later
        gch_ref[tap : tap + 1, :] += jnp.sum(conv * later, axis=0, keepdims=True)
    gch_ref[CONV : CONV + 1, :] += jnp.sum(dpre, axis=0, keepdims=True)
    buf[T : T + 8, :] = buf[0:8, :]
    dconv = total.astype(bf16)
    dconv_ref[...] = dconv
    dnorm = dotf(dconv, w_ref[0:C, :]) + dotf(dgate_ref[...], w_ref[C : 2 * C, :])
    dnorm_ref[...] = dnorm.astype(bf16)
    gain_ref[0:1, :] += jnp.sum(dnorm * seq_ref[...].astype(f32), axis=0, keepdims=True)


def conv_bwd(dact, dsel, selw, pre, conv, dgate, w_in, seq, chan, T=256):
    N, C = conv.shape
    D = seq.shape[1]
    g = N // T
    row, full = lambda w: row_spec(T, w, g), full_spec
    shape = jax.ShapeDtypeStruct
    return pl.pallas_call(
        functools.partial(conv_bwd_kernel, T=T),
        grid=(g,),
        in_specs=[row(C), row(dsel.shape[1]), full(selw), row(C), row(C), row(C), full(w_in), row(D), full(chan)],
        out_specs=[row(C), row(D), pl.BlockSpec((8, C), lambda i: (0, 0)), pl.BlockSpec((8, D), lambda i: (0, 0))],
        out_shape=[shape((N, C), bf16), shape((N, D), bf16), shape((8, C), f32), shape((8, D), f32)],
        scratch_shapes=[pltpu.VMEM((T + 8, C), f32)],
        compiler_params=pltpu.CompilerParams(vmem_limit_bytes=48 * 2**20),
        cost_estimate=pl.CostEstimate(flops=4 * N * C * D, bytes_accessed=N * C * 20, transcendentals=N * C),
    )(dact, dsel, selw, pre, conv, dgate, w_in, seq, chan)


def experts_kernel(x_ref, dz_ref, up_ref, down_ref, out_ref, drow_ref, gup_ref, gdown_ref, acc_out, acc_row, *, steps):
    @pl.when(pl.program_id(0) == 0)
    def _():
        acc_out[...] = jnp.zeros_like(acc_out)
        acc_row[...] = jnp.zeros_like(acc_row)

    x, dz, up, down = x_ref[...], dz_ref[...], up_ref[...], down_ref[...]
    lin = dotf(x, up, ((1,), (1,)))
    cdf = 0.5 * (1.0 + lax.erf(lin * math.sqrt(0.5)))
    act = (lin * cdf).astype(bf16)
    slope = cdf + lin * jnp.exp(-0.5 * lin * lin) * (1.0 / math.sqrt(2.0 * math.pi))
    acc_out[...] += dotf(act, down)
    dlin = (dotf(dz, down, ((1,), (1,))) * slope).astype(bf16)
    acc_row[...] += dotf(dlin, up)
    gdown_ref[...] = dotf(act, dz, ((0,), (0,))).astype(bf16)
    gup_ref[...] = dotf(dlin, x, ((0,), (0,))).astype(bf16)

    @pl.when(pl.program_id(0) == steps - 1)
    def _():
        out_ref[...] = acc_out[...].astype(bf16)
        drow_ref[...] = acc_row[...].astype(bf16)


def experts(x, dz, up, down, block=384):
    R, D = x.shape
    H = up.shape[0]
    steps = H // block
    fix = pl.BlockSpec((R, D), lambda i: (0, 0))
    mov = pl.BlockSpec((block, D), lambda i: (i, 0))
    shape = jax.ShapeDtypeStruct
    return pl.pallas_call(
        functools.partial(experts_kernel, steps=steps),
        grid=(steps,),
        in_specs=[fix, fix, mov, mov],
        out_specs=[fix, fix, mov, mov],
        out_shape=[shape((R, D), bf16)] * 2 + [shape((H, D), bf16)] * 2,
        scratch_shapes=[pltpu.VMEM((R, D), f32)] * 2,
        compiler_params=pltpu.CompilerParams(vmem_limit_bytes=56 * 2**20),
        cost_estimate=pl.CostEstimate(flops=12 * R * D * H, bytes_accessed=8 * H * D, transcendentals=R * H),
    )(x, dz, up, down)


def contract_rows(left, right):
    return dotf(left, right, ((0,), (0,)))


def ring_pairs(n):
    order = list(range(0, n, 2)) + list(range(n - 1, 0, -2))
    ahead = [(order[i], order[(i + 1) % n]) for i in range(n)]
    return ahead, [(b, a) for a, b in ahead]


def ring_gather(ahead_part, back_part, axis):
    n = lax.axis_size(axis)
    ahead, back = ring_pairs(n)
    first, second = [ahead_part], [back_part]
    for _ in range(n - 1):
        first.append(lax.ppermute(first[-1], axis, ahead))
        second.append(lax.ppermute(second[-1], axis, back))
    return first, [second[-r % n] for r in range(n)]


def ring_scatter(ahead_parts, back_parts, axis):
    n = lax.axis_size(axis)
    ahead, back = ring_pairs(n)
    one, two = ahead_parts[1], back_parts[n - 1]
    for s in range(n - 1):
        one = add_up(lax.ppermute(one, axis, ahead), ahead_parts[(s + 2) % n])
        two = add_up(lax.ppermute(two, axis, back), back_parts[(n - 2 - s) % n])
    return one, two


def add_up(a, b):
    return (a.astype(f32) + b.astype(f32)).astype(a.dtype)


def swap(value, j):
    n = lax.axis_size("mp")
    return lax.ppermute(value, "mp", [(i, i ^ j) for i in range(n)])


def gather_mp(rows):
    near = swap(rows, 1)
    across = swap(rows, 2)
    return [rows, near, across, swap(across, 1)]


def sum_mp(value):
    value = value + swap(value, 1)
    return value + swap(value, 2)


def scatter_mp(value):
    me = lax.axis_index("mp")
    block = lambda j: lax.dynamic_index_in_dim(value, me ^ j, 0, keepdims=False).astype(f32)
    near = swap(jnp.stack([block(1), block(3)]).astype(bf16), 1).astype(f32)
    far = (block(2) + near[1]).astype(bf16)
    return block(0) + near[0] + swap(far, 2).astype(f32)


def butterfly(value):
    for j in (1, 2):
        value = value + swap(value, j)
    n = lax.axis_size("dp")
    step = 1
    while step < n:
        value = value + lax.ppermute(value, "dp", [(i, i ^ step) for i in range(n)])
        step *= 2
    return value


def nesterov(weight, velocity, average, step_grad, rate):
    momentum = MOMENT * velocity + step_grad
    new_weight = weight - rate * (step_grad + MOMENT * momentum)
    smoothed = SMOOTH * average + (1.0 - SMOOTH) * new_weight
    return [new_weight, momentum, smoothed, new_weight.astype(jnp.bfloat16)]


def scale_of(values):
    return lax.rsqrt(jnp.mean(values * values, axis=-1, keepdims=True) + EPSILON)


def after(value, *others):
    return lax.optimization_barrier((value,) + others)[0]


def body(
    block_input, cotangent, expert_ids, slot_ids,
    inward_proj, select_proj, delta_proj, channel_params, outward_proj, expert_up, expert_down, norm_gains, router_weight,
    inward_velocity, select_velocity, delta_velocity, channel_velocity, outward_velocity, upward_velocity,
    downward_velocity, gains_velocity, router_velocity,
    inward_average, select_average, delta_average, channel_average, outward_average, upward_average,
    downward_average, gains_average, router_average,
):
    tok_rows, width = block_input.shape
    ring = lax.axis_size("dp")
    peers = lax.axis_size("mp")
    me = lax.axis_index("mp")
    own = inward_proj.shape[2]
    inner = own * ring
    wide = -(-inner // LANES) * LANES
    spare = wide - inner
    xw = select_proj.shape[1]
    vrows = channel_params.shape[0]

    first_a = jnp.concatenate(
        [
            inward_proj[0].T,
            select_proj,
            delta_proj.T,
            channel_params.T,
            jnp.zeros((own, 1), f32),
        ],
        axis=1,
    ).astype(bf16)
    first_b = inward_proj[1].T.astype(bf16)
    half = 5 * LANES
    in_a, in_b = ring_gather(first_a, first_b, "dp")
    out_a, out_b = ring_gather(
        after(outward_proj[:, :half].astype(bf16), in_a[-1], in_b[1]),
        after(outward_proj[:, half:].astype(bf16), in_a[-1], in_b[1]),
        "dp",
    )
    up_t = expert_up[0].T.astype(bf16)
    down_b = expert_down[0].astype(bf16)
    units = up_t.shape[0]
    mid = units // 2
    ex_a, ex_b = ring_gather(
        after(jnp.concatenate([up_t[:mid], down_b[:mid]]), out_a[-1], out_b[1]),
        after(jnp.concatenate([up_t[mid:], down_b[mid:]]), out_a[-1], out_b[1]),
        "dp",
    )
    up_all = jnp.concatenate([p[:mid] for p in ex_a] + [p[:mid] for p in ex_b])
    down_all = jnp.concatenate([p[mid:] for p in ex_a] + [p[mid:] for p in ex_b])

    rows_a = jnp.concatenate(in_a + [jnp.zeros((spare, first_a.shape[1]), bf16)])
    zero_rows = jnp.zeros((spare, width), bf16)
    w_in = jnp.concatenate([rows_a[:, :width]] + in_b + [zero_rows])
    small = rows_a[:, width:]
    selw = small[:, :xw]
    delta_t = small[:, xw : xw + DT_RANK]
    chan = small[:, xw + DT_RANK : xw + DT_RANK + vrows].astype(f32).T
    delta_w = delta_t.T
    out_w = jnp.concatenate(
        [jnp.concatenate(out_a + [zero_rows[:, :half]]), jnp.concatenate(out_b + [zero_rows[:, half:]])], axis=1
    )

    slot_index = (expert_ids ^ me) * CAP + slot_ids
    dispatch = (
        lax.broadcasted_iota(jnp.int32, (peers * CAP, tok_rows), 0) == slot_index[None, :]
    ).astype(bf16)

    def route(rows):
        return jnp.dot(dispatch, rows, preferred_element_type=f32)

    def unroute(blocks):
        return contract_rows(dispatch, blocks)

    def exchange(blocks):
        parts = blocks.reshape(peers, CAP, -1)
        return jnp.concatenate([parts[0]] + [swap(parts[j], j) for j in range(1, peers)])

    cot_rows = exchange(route(cotangent).astype(bf16))

    source = block_input.astype(f32)
    scale1 = scale_of(source)
    normed_b = (source * scale1 * norm_gains[0]).astype(bf16)

    def in_order(blocks):
        stacked = jnp.stack(blocks)
        return jnp.concatenate(
            [lax.dynamic_index_in_dim(stacked, me ^ m, 0, keepdims=False) for m in range(peers)]
        )

    seq = in_order(gather_mp(normed_b))
    conv_in, gate_in, pre, act, act_b, sel_part = conv_fwd(seq, w_in, chan, selw)
    selected = sum_mp(sel_part)
    rank_b = selected[:, :DT_RANK].astype(bf16)
    s_all, xlin, scanned, gated_b, mix = scan_fwd(rank_b, delta_w, act, gate_in, selected, chan, out_w)
    residual = source + scatter_mp(mix.reshape(peers, tok_rows, width))
    scale2 = scale_of(residual)
    normed2 = residual * scale2 * norm_gains[1]
    logits = jnp.dot(normed2, router_weight, precision=HIGHEST, preferred_element_type=f32)
    probs = jax.nn.softmax(logits, axis=-1)
    choose = (
        expert_ids[:, None] == jnp.arange(router_weight.shape[1], dtype=jnp.int32)[None, :]
    ).astype(f32)
    gate_prob = jnp.sum(probs * choose, axis=1)
    arrived = exchange(route(normed2.astype(bf16)).astype(bf16))
    prob_slots = (
        jnp.zeros((peers * CAP,), f32).at[slot_index].set(gate_prob)
    )
    prob_rows = exchange(prob_slots).reshape(peers * CAP)
    d_buffer = (prob_rows[:, None] * cot_rows.astype(f32)).astype(bf16)
    expert_out, d_rows, grad_up, grad_down = experts(arrived, d_buffer, up_all, down_all)
    d_arrived = exchange(d_rows)
    returned = exchange(expert_out)
    grad_out = cotangent.astype(f32)
    tokens_out = unroute(returned)
    block_output = (residual + gate_prob[:, None] * tokens_out).astype(bf16)
    d_gate = jnp.sum(grad_out * tokens_out, axis=1)
    d_logits = (d_gate * gate_prob)[:, None] * (choose - probs)
    d_normed2 = unroute(d_arrived) + lax.dot_general(
        d_logits, router_weight, (((1,), (1,)), ((), ())), precision=HIGHEST, preferred_element_type=f32
    )
    grad_router = lax.dot_general(
        normed2, d_logits, (((0,), (0,)), ((), ())), precision=HIGHEST, preferred_element_type=f32
    )
    hat2 = residual * scale2
    grad_gain2 = jnp.sum(d_normed2 * hat2, axis=0)
    a2 = norm_gains[1] * d_normed2
    d_residual = grad_out + scale2 * (a2 - hat2 * jnp.mean(a2 * hat2, axis=-1, keepdims=True))
    portion = in_order(gather_mp(d_residual.astype(bf16)))
    delta_pad = jnp.pad(delta_w, ((0, LANES - DT_RANK), (0, 0)))
    d_gate_b, d_act, ddl_b, dsel_part, gch_tail = scan_bwd(
        portion, out_w, s_all, act, gate_in, xlin, scanned, selected, chan, delta_pad
    )
    d_selected = sum_mp(dsel_part)
    d_conv_b, dnorm_part, gch_conv, gain_part = conv_bwd(
        d_act, d_selected, selw, pre, conv_in, d_gate_b, w_in, seq, chan
    )

    gparts_a = [grad_up[r * mid : (r + 1) * mid] for r in range(ring)]
    dparts_a = [grad_down[r * mid : (r + 1) * mid] for r in range(ring)]
    gparts_b = [grad_up[(ring + r) * mid : (ring + r + 1) * mid] for r in range(ring)]
    dparts_b = [grad_down[(ring + r) * mid : (ring + r + 1) * mid] for r in range(ring)]
    gu_a, gu_b = ring_scatter(gparts_a, gparts_b, "dp")
    gd_a, gd_b = ring_scatter(dparts_a, dparts_b, "dp")
    up_grad = jnp.concatenate([gu_a, gu_b]).astype(f32).T[None]
    down_grad = jnp.concatenate([gd_a, gd_b]).astype(f32)[None]

    grad_out_w = contract_rows(gated_b, portion)
    grad_delta = contract_rows(ddl_b, rank_b)
    grad_sel = contract_rows(act_b, d_selected)
    grad_in0 = contract_rows(d_conv_b, seq)
    grad_in1 = contract_rows(d_gate_b, seq)
    grad_chan = jnp.concatenate([gch_conv[: CONV + 1], gch_tail[CONV + 1 : CONV + 3 + NST], jnp.zeros((1, wide), f32)]).T
    pack_a = jnp.concatenate(
        [grad_in0, grad_sel, grad_delta, grad_chan, grad_out_w[:, :half]], axis=1
    ).astype(bf16)
    pack_b = jnp.concatenate([grad_in1, grad_out_w[:, half:]], axis=1).astype(bf16)
    split = lambda a: [a[r * own : (r + 1) * own] for r in range(ring)]
    sum_a, sum_b = ring_scatter(split(pack_a), split(pack_b), "dp")
    sum_a, sum_b = sum_a.astype(f32), sum_b.astype(f32)

    d_normed = scatter_mp(dnorm_part.reshape(peers, tok_rows, width))
    a1 = norm_gains[0] * d_normed
    hat1 = source * scale1
    block_grad = d_residual + scale1 * (a1 - hat1 * jnp.mean(a1 * hat1, axis=-1, keepdims=True))
    shared = butterfly(
        jnp.concatenate([(gain_part[:1] / norm_gains[:1]), grad_gain2[None], grad_router.T])
    )

    at = width + xw
    in_grad = jnp.stack([sum_a[:, :width].T, sum_b[:, :width].T])
    gradients = (
        in_grad,
        sum_a[:, width:at],
        sum_a[:, at : at + DT_RANK].T,
        sum_a[:, at + DT_RANK : at + DT_RANK + vrows].T,
        jnp.concatenate([sum_a[:, at + DT_RANK + vrows + 1 :], sum_b[:, width:]], axis=1),
        up_grad,
        down_grad,
        shared[:2],
        shared[2:].T,
    )
    masters = (
        inward_proj, select_proj, delta_proj, channel_params, outward_proj, expert_up, expert_down, norm_gains,
        router_weight,
    )
    velocities = (
        inward_velocity, select_velocity, delta_velocity, channel_velocity, outward_velocity, upward_velocity,
        downward_velocity, gains_velocity, router_velocity,
    )
    averages = (
        inward_average, select_average, delta_average, channel_average, outward_average, upward_average,
        downward_average, gains_average, router_average,
    )
    factor = 1.0 / math.sqrt(tok_rows * ring * peers)
    results = [block_output, block_grad]
    for position in range(9):
        results.extend(
            nesterov(
                masters[position],
                velocities[position],
                averages[position],
                gradients[position] * factor,
                LEARNING[position],
            )
        )
    return tuple(results)


def solution(mesh):
    in_specs = (
        P(("dp", "mp"), None),
        P(("dp", "mp"), None),
        P(("dp", "mp")),
        P(("dp", "mp")),
        P(None, None, ("dp", "mp")),
        P(("dp", "mp"), None),
        P(None, ("dp", "mp")),
        P(None, ("dp", "mp")),
        P(("dp", "mp"), None),
        P("mp", None, "dp"),
        P("mp", "dp", None),
        P(),
        P(),
        P(None, None, ("dp", "mp")),
        P(("dp", "mp"), None),
        P(None, ("dp", "mp")),
        P(None, ("dp", "mp")),
        P(("dp", "mp"), None),
        P("mp", None, "dp"),
        P("mp", "dp", None),
        P(),
        P(),
        P(None, None, ("dp", "mp")),
        P(("dp", "mp"), None),
        P(None, ("dp", "mp")),
        P(None, ("dp", "mp")),
        P(("dp", "mp"), None),
        P("mp", None, "dp"),
        P("mp", "dp", None),
        P(),
        P(),
    )
    out_specs = (
        P(("dp", "mp"), None),
        P(("dp", "mp"), None),
        P(None, None, ("dp", "mp")),
        P(None, None, ("dp", "mp")),
        P(None, None, ("dp", "mp")),
        P(None, None, ("dp", "mp")),
        P(("dp", "mp"), None),
        P(("dp", "mp"), None),
        P(("dp", "mp"), None),
        P(("dp", "mp"), None),
        P(None, ("dp", "mp")),
        P(None, ("dp", "mp")),
        P(None, ("dp", "mp")),
        P(None, ("dp", "mp")),
        P(None, ("dp", "mp")),
        P(None, ("dp", "mp")),
        P(None, ("dp", "mp")),
        P(None, ("dp", "mp")),
        P(("dp", "mp"), None),
        P(("dp", "mp"), None),
        P(("dp", "mp"), None),
        P(("dp", "mp"), None),
        P("mp", None, "dp"),
        P("mp", None, "dp"),
        P("mp", None, "dp"),
        P("mp", None, "dp"),
        P("mp", "dp", None),
        P("mp", "dp", None),
        P("mp", "dp", None),
        P("mp", "dp", None),
        P(),
        P(),
        P(),
        P(),
        P(),
        P(),
        P(),
        P(),
    )
    return jax.shard_map(body, mesh=mesh, in_specs=in_specs, out_specs=out_specs, check_vma=False)
```

time: 2630 us -> 952 us (0.36)
  matrix products: 633 us -> 29.6 us
  other arithmetic: 626 us -> 80.1 us
  waiting for transfers between devices: 768 us -> 332 us
  Pallas kernels: 0 us -> 253 us
  local copies, waits for them, and re-layouts: 359 us -> 124 us
  blocking collectives: 172 us -> 0 us
  starting transfers between devices: 16.6 us -> 119 us
    dot_general x47 -> x11, matrix products: 629 us -> 27.3 us  [the longest x7 19.7 us: dotf(): return lax.dot_general(a, b, (dims, ((), ())), preferred_element_type=f32)]
    ppermute x0 -> x118, waiting for transfers between devices: none -> 332 us  [the longest x21 98.3 us: ring_scatter(): one = add_up(lax.ppermute(one, axis, ahead), ahead_parts[(s + 2) % n])]
    pallas_call x0 -> x5, Pallas kernels: none -> 253 us  [the longest x1 120 us: scan_bwd(): pl.pallas_call(functools.partial(scan_bwd_kernel, T=T, g=g), grid=(g,), i...]
    all_gather x6 -> x0, waiting for transfers between devices: 248 us -> none  [the longest x1 108 us: body(): lax.all_gather(expert_down.astype(jnp.bfloat16), 'dp', axis=1, tiled=True)]
    reduce_scatter x3 -> x0, waiting for transfers between devices: 238 us -> none  [the longest x1 127 us: body(): lax.psum_scatter(grad_down.astype(jnp.bfloat16), 'dp', scatter_dimension=...]
    unnamed x21 -> x0, waiting for transfers between devices: 218 us -> none
    reduce_sum x21 -> x3, other arithmetic: 185 us -> 5.08 us  [the longest x1 2.75 us: body(): jnp.mean(a1 * hat1, axis=-1, keepdims=True)]
    ppermute x0 -> x118, starting transfers between devices: none -> 119 us  [the longest x21 31.6 us: ring_scatter(): two = add_up(lax.ppermute(two, axis, back), back_parts[(n - 2 - s) % n])]
  transfers between devices with their start and end apart: 20 -> 118, of which waited for: 13 -> 73; matrix products, arithmetic and copies ran while one was open for 19% -> 21% of each run, Pallas kernels for 0% -> 21%
where the time goes in v1:
time: 952 us; the launch traced here: 941 us
  waiting for transfers between devices  332 us (35%)
  Pallas kernels  253 us (27%)
  local copies, waits for them, and re-layouts  124 us (13%)
  starting transfers between devices  119 us (12%)
  other arithmetic  80.1 us (8%)
  matrix products  29.6 us (3%)
    pallas_call x1, Pallas kernels, scan_bwd(): pl.pallas_call(functools.partial(scan_bwd_kernel, T=T, g=g), grid=(g,), i...  120 us
    ppermute x21, waiting for transfers between devices, ring_scatter(): one = add_up(lax.ppermute(one, axis, ahead), ahead_parts[(s + 2) % n])  98.3 us
    ppermute x21, waiting for transfers between devices, ring_gather(): second.append(lax.ppermute(second[-1], axis, back))  90.2 us
    unnamed x329, local copies, waits for them, and re-layouts  83.3 us
    ppermute x31, waiting for transfers between devices, swap(): return lax.ppermute(value, 'mp', [(i, i ^ j) for i in range(n)])  73.8 us
    pallas_call x1, Pallas kernels, experts(): pl.pallas_call(functools.partial(experts_kernel, steps=steps), grid=(step...  52 us
    pallas_call x1, Pallas kernels, scan_fwd(): pl.pallas_call(functools.partial(scan_fwd_kernel, T=T), grid=(g,), in_spe...  48.3 us
    ppermute x21, waiting for transfers between devices, ring_scatter(): two = add_up(lax.ppermute(two, axis, back), back_parts[(n - 2 - s) % n])  38.8 us
  transfers between devices with their start and end apart: 118, of which 73 were waited for; matrix products, arithmetic and copies ran while one was open for 21% of the time, Pallas kernels for 21%

profile of v1, /device:TPU:0, one launch (start us, length us, event | category | flops | bytes accessed | tf_op | source)
XLA Modules:
  0.0 941.2 jit_solution(15239990383690009679)
XLA Ops:
  14.8 6.8 collective-permute-done.10
  25.1 5.0 collective-permute-done.11
  33.0 4.7 collective-permute-done.12
  59.4 3.4 collective-permute-done.15
  63.3 3.7 collective-permute-done.8
  76.4 4.9 concatenate.89
  84.7 5.2 concatenate.90
  116.1 4.7 collective-permute-done.25
  129.5 15.2 %shard_map.590 = (f32[2048,640]{1,0:T(8,128)}, f32[2048,640]{1,0:T(8,128)}, f32[2048,640]{1,0:T(8,128)}, f32[2048,640]{1,0:T(8,128)}, bf16[2048,640]{1,0:T(8,128)(2,1)S(1)}, /*index=5*/f32[2048,104]{1,0:T(8,128)S(1)}) custom-call(bf16[2048,1152]{1,0:T(8,128)(2,1)} %pad_maximum_fusion.1.seq_ref, bf16[1280,1152]{1,0:T(8,128)(2,1)} %copy.168.w_ref, ...), custom_call_target="tpu_custom_call" | custom-call | flops 6039797760 | bytes 26214400 | tf_op jit(solution)/shard_map/pallas_call | solution.py:228
  163.2 10.8 %collective-permute-done.51 = bf16[384,1152]{1,0:T(8,128)(2,1)} collective-permute-done((bf16[384,1152]{1,0:T(8,128)(2,1)}, bf16[384,1152]{1,0:T(8,128)(2,1)}, u32[]{:S(2)}, u32[]{:S(2)}) %collective-permute-start.51) | collective-permute-done | bytes 884768 | tf_op jit(solution)/shard_map/ppermute | solution.py:351
  176.0 4.4 collective-permute-done.18
  184.3 48.3 %shard_map.591 = (bf16[128,256,640]{2,1,0:T(8,128)(2,1)}, f32[2048,640]{1,0:T(8,128)}, f32[2048,640]{1,0:T(8,128)}, bf16[2048,640]{1,0:T(8,128)(2,1)S(1)}, bf16[2048,1152]{1,0:T(8,128)(2,1)}) custom-call(bf16[2048,72]{1,0:T(8,128)(2,1)S(1)} %slice.870.rank_ref, bf16[72,640]{1,0:T(8,128)(2,1)S(1)} %slice_bitcast_fusion.6.delta_w_ref, ...), custom_call_target="tpu_custom_call" | custom-call | flops 3019898880 | bytes 70254592 | tf_op jit(solution)/shard_map/pallas_call | solution.py:94
  263.0 16.8 %collective-permute-done.53 = bf16[384,1152]{1,0:T(8,128)(2,1)S(1)} collective-permute-done((bf16[384,1152]{1,0:T(8,128)(2,1)}, bf16[384,1152]{1,0:T(8,128)(2,1)S(1)}, u32[]{:S(2)}, u32[]{:S(2)}) %collective-permute-start.53) | collective-permute-done | bytes 884768 | tf_op jit(solution)/shard_map/ppermute | solution.py:351
  286.1 14.6 %collective-permute-done.54 = bf16[384,1152]{1,0:T(8,128)(2,1)S(1)} collective-permute-done((bf16[384,1152]{1,0:T(8,128)(2,1)S(1)}, bf16[384,1152]{1,0:T(8,128)(2,1)S(1)}, u32[]{:S(2)}, u32[]{:S(2)}) %collective-permute-start.54) | collective-permute-done | bytes 884768 | tf_op jit(solution)/shard_map/ppermute | solution.py:351
  305.7 15.2 %collective-permute-done.55 = bf16[384,1152]{1,0:T(8,128)(2,1)} collective-permute-done((bf16[384,1152]{1,0:T(8,128)(2,1)S(1)}, bf16[384,1152]{1,0:T(8,128)(2,1)}, u32[]{:S(2)}, u32[]{:S(2)}) %collective-permute-start.55) | collective-permute-done | bytes 884768 | tf_op jit(solution)/shard_map/ppermute | solution.py:351
  325.0 3.9 collective-permute-done.34
  348.1 7.8 collective-permute-done.37
  355.9 9.6 %collective-permute-done.36 = bf16[192,1152]{1,0:T(8,128)(2,1)S(1)} collective-permute-done((bf16[192,1152]{1,0:T(8,128)(2,1)S(1)}, bf16[192,1152]{1,0:T(8,128)(2,1)S(1)}, u32[]{:S(2)}, u32[]{:S(2)}) %collective-permute-start.36) | collective-permute-done | bytes 442400 | tf_op jit(solution)/shard_map/ppermute | solution.py:371
  380.5 52.0 %shard_map.592 = (bf16[768,1152]{1,0:T(8,128)(2,1)}, bf16[768,1152]{1,0:T(8,128)(2,1)}, bf16[3072,1152]{1,0:T(8,128)(2,1)}, bf16[3072,1152]{1,0:T(8,128)(2,1)}) custom-call(bf16[768,1152]{1,0:T(8,128)(2,1)} %pad_maximum_fusion.6.x_ref, bf16[768,1152]{1,0:T(8,128)(2,1)} %multiply_convert_fusion.dz_ref, bf16[3072,1152]{1,0:T(8,128)(2,1)} %get-tuple-element.346.up_ref, ...), custom_call_target="tpu_custom_call" | custom-call | flops 32614907904 | bytes 28311552 | tf_op jit(solution)/shard_map/pallas_call | solution.py:323
  439.7 6.9 collective-permute-done.60
  446.8 9.7 %collective-permute-done.59 = bf16[192,1152]{1,0:T(8,128)(2,1)S(1)} collective-permute-done((bf16[192,1152]{1,0:T(8,128)(2,1)S(1)}, bf16[192,1152]{1,0:T(8,128)(2,1)S(1)}, u32[]{:S(2)}, u32[]{:S(2)}) %collective-permute-start.59) | collective-permute-done | bytes 442400 | tf_op jit(solution)/shard_map/ppermute | solution.py:371
  466.9 8.3 collective-permute-done.62
  482.8 5.4 collective-permute-done.106
  499.3 3.9 collective-permute-done.100
  508.8 3.9 collective-permute-done.87
  518.3 3.9 collective-permute-done.101
  528.3 3.4 collective-permute-done.88
  531.7 3.8 collective-permute-done.95
  537.3 3.9 collective-permute-done.102
  546.7 3.9 collective-permute-done.89
  556.2 3.9 collective-permute-done.103
  580.6 120.0 %shard_map.593 = (bf16[2048,640]{1,0:T(8,128)(2,1)}, f32[2048,640]{1,0:T(8,128)}, bf16[2048,640]{1,0:T(8,128)(2,1)}, bf16[2048,104]{1,0:T(8,128)(2,1)}, f32[24,640]{1,0:T(8,128)}) custom-call(bf16[2048,1152]{1,0:T(8,128)(2,1)} %pad_maximum_fusion.3.dmix_ref, bf16[640,1152]{1,0:T(8,128)(2,1)} %copy-done.2, ...), custom_call_target="tpu_custom_call" | custom-call | flops 3019898880 | bytes 78643200 | tf_op jit(solution)/shard_map/pallas_call | solution.py:175
  700.7 6.3 convolution_convert_fusion.2
  707.0 3.9 convolution_convert_fusion.3
  716.5 7.5 collective-permute-done.78
  729.5 4.0 collective-permute-done.112
  759.2 7.7 collective-permute-done.68
  767.1 17.7 %shard_map.594 = (bf16[2048,640]{1,0:T(8,128)(2,1)S(1)}, bf16[2048,1152]{1,0:T(8,128)(2,1)}, f32[8,640]{1,0:T(8,128)S(1)}, f32[8,1152]{1,0:T(8,128)S(1)}) custom-call(f32[2048,640]{1,0:T(8,128)} %get-tuple-element.79.dact_ref, bf16[2048,104]{1,0:T(8,128)(2,1)S(1)} %add.347.dsel_ref, bf16[640,104]{1,0:T(8,128)(2,1)S(1)} %copy-done.5, ...), custom_call_target="tpu_custom_call" | custom-call | flops 6039797760 | bytes 26214400 | tf_op jit(solution)/shard_map/pallas_call | solution.py:281
  789.5 4.0 fusion.3
  818.8 10.1 %collective-permute-done.72 = bf16[72,1992]{0,1:T(8,128)(2,1)S(1)} collective-permute-done((bf16[72,1992]{0,1:T(8,128)(2,1)S(1)}, bf16[72,1992]{0,1:T(8,128)(2,1)S(1)}, u32[]{:S(2)}, u32[]{:S(2)}) %collective-permute-start.72) | collective-permute-done | bytes 286880 | tf_op jit(solution)/shard_map/ppermute | solution.py:360
  831.1 10.7 %collective-permute-done.73 = bf16[72,1992]{0,1:T(8,128)(2,1)S(1)} collective-permute-done((bf16[72,1992]{0,1:T(8,128)(2,1)S(1)}, bf16[72,1992]{0,1:T(8,128)(2,1)S(1)}, u32[]{:S(2)}, u32[]{:S(2)}) %collective-permute-start.73) | collective-permute-done | bytes 286880 | tf_op jit(solution)/shard_map/ppermute | solution.py:360
  844.7 10.3 %collective-permute-done.74 = bf16[72,1992]{0,1:T(8,128)(2,1)S(1)} collective-permute-done((bf16[72,1992]{0,1:T(8,128)(2,1)S(1)}, bf16[72,1992]{0,1:T(8,128)(2,1)S(1)}, u32[]{:S(2)}, u32[]{:S(2)}) %collective-permute-start.74) | collective-permute-done | bytes 286880 | tf_op jit(solution)/shard_map/ppermute | solution.py:360
  858.1 11.5 %collective-permute-done.75 = bf16[72,1992]{0,1:T(8,128)(2,1)S(1)} collective-permute-done((bf16[72,1992]{0,1:T(8,128)(2,1)S(1)}, bf16[72,1992]{0,1:T(8,128)(2,1)S(1)}, u32[]{:S(2)}, u32[]{:S(2)}) %collective-permute-start.75) | collective-permute-done | bytes 286880 | tf_op jit(solution)/shard_map/ppermute | solution.py:360
  870.5 14.3 %collective-permute-done.76 = bf16[72,1992]{0,1:T(8,128)(2,1)S(1)} collective-permute-done((bf16[72,1992]{0,1:T(8,128)(2,1)S(1)}, bf16[72,1992]{0,1:T(8,128)(2,1)S(1)}, u32[]{:S(2)}, u32[]{:S(2)}) %collective-permute-start.76) | collective-permute-done | bytes 286880 | tf_op jit(solution)/shard_map/ppermute | solution.py:360
  885.4 9.1 collective-permute-done.77
  911.6 3.5 fusion.42
  923.8 9.5 %collective-permute-done.70 = bf16[512,1152]{1,0:T(8,128)(2,1)S(1)} collective-permute-done((bf16[512,1152]{1,0:T(8,128)(2,1)}, bf16[512,1152]{1,0:T(8,128)(2,1)S(1)}, u32[]{:S(2)}, u32[]{:S(2)}) %collective-permute-start.70) | collective-permute-done | bytes 1179680 | tf_op jit(solution)/shard_map/ppermute | solution.py:371
  936.1 4.8 fusion.9
  (686 shorter events, 385.5 us)
Async XLA Ops:
  5.8 62.8 %collective-permute-start.1 = (bf16[512,1152]{1,0:T(8,128)(2,1)}, bf16[512,1152]{1,0:T(8,128)(2,1)}, u32[]{:S(2)}, u32[]{:S(2)}) collective-permute-start(bf16[512,1152]{1,0:T(8,128)(2,1)} %fusion.5), channel_id=1, source_target_pairs={{0,2},{1,3},{2,0},{3,1},{4,6},{5,7},{6,4},{7,5},{8,10},{9,11},{10,... | collective-permute-start | bytes 3538952 | tf_op jit(solution)/shard_map/ppermute | solution.py:371
  8.8 112.7 %collective-permute-start = (bf16[512,1152]{1,0:T(8,128)(2,1)}, bf16[512,1152]{1,0:T(8,128)(2,1)}, u32[]{:S(2)}, u32[]{:S(2)}) collective-permute-start(bf16[512,1152]{1,0:T(8,128)(2,1)} %fusion.5), channel_id=1, source_target_pairs={{0,1},{1,0},{2,3},{3,2},{4,5},{5,4},{6,7},{7,6},{8,9},{9,8},{10,11... | collective-permute-start | bytes 3538952 | tf_op jit(solution)/shard_map/ppermute | solution.py:371
  68.6 52.9 %collective-permute-start.2 = (bf16[512,1152]{1,0:T(8,128)(2,1)}, bf16[512,1152]{1,0:T(8,128)(2,1)}, u32[]{:S(2)}, u32[]{:S(2)}) collective-permute-start(bf16[512,1152]{1,0:T(8,128)(2,1)} %collective-permute-done.1), channel_id=1, source_target_pairs={{0,1},{1,0},{2,3},{3,2},{4,5},{5,4},{6,7},{7,6},{8,9},{9,8},{10,11... | collective-permute-start | bytes 3538952 | tf_op jit(solution)/shard_map/ppermute | solution.py:371
  120.9 32.2 %collective-permute-start.44 = (bf16[384,1152]{1,0:T(8,128)(2,1)}, bf16[384,1152]{1,0:T(8,128)(2,1)}, u32[]{:S(2)}, u32[]{:S(2)}) collective-permute-start(bf16[384,1152]{1,0:T(8,128)(2,1)} %get-tuple-element.72), channel_id=1, source_target_pairs={{0,8},{8,16},{16,24},{24,28},{28,20},{20,12},{12,4},{4,0},{1,9},{9... | collective-permute-start | bytes 2654216 | tf_op jit(solution)/shard_map/ppermute | solution.py:350
  151.6 22.4 %collective-permute-start.51 = (bf16[384,1152]{1,0:T(8,128)(2,1)}, bf16[384,1152]{1,0:T(8,128)(2,1)}, u32[]{:S(2)}, u32[]{:S(2)}) collective-permute-start(bf16[384,1152]{1,0:T(8,128)(2,1)} %get-tuple-element.73), channel_id=1, source_target_pairs={{8,0},{16,8},{24,16},{28,24},{20,28},{12,20},{4,12},{0,4},{9,1},{1... | collective-permute-start | bytes 2654216 | tf_op jit(solution)/shard_map/ppermute | solution.py:351
  153.0 22.4 %collective-permute-start.45 = (bf16[384,1152]{1,0:T(8,128)(2,1)}, bf16[384,1152]{1,0:T(8,128)(2,1)}, u32[]{:S(2)}, u32[]{:S(2)}) collective-permute-start(bf16[384,1152]{1,0:T(8,128)(2,1)} %collective-permute-done.44), channel_id=1, source_target_pairs={{0,8},{8,16},{16,24},{24,28},{28,20},{20,12},{12,4},{4,0},{1,9},{9... | collective-permute-start | bytes 2654216 | tf_op jit(solution)/shard_map/ppermute | solution.py:350
  159.3 21.1 %collective-permute-start.18 = (f32[2048,104]{0,1:T(8,128)}, f32[2048,104]{0,1:T(8,128)}, u32[]{:S(2)}, u32[]{:S(2)}) collective-permute-start(f32[2048,104]{0,1:T(8,128)} %copy.172), channel_id=1, source_target_pairs={{0,2},{1,3},{2,0},{3,1},{4,6},{5,7},{6,4},{7,5},{8,10},{9,11},{10,... | collective-permute-start | bytes 2555912 | tf_op jit(solution)/shard_map/ppermute | solution.py:371
  174.0 83.8 %collective-permute-start.52 = (bf16[384,1152]{1,0:T(8,128)(2,1)}, bf16[384,1152]{1,0:T(8,128)(2,1)}, u32[]{:S(2)}, u32[]{:S(2)}) collective-permute-start(bf16[384,1152]{1,0:T(8,128)(2,1)} %collective-permute-done.51), channel_id=1, source_target_pairs={{8,0},{16,8},{24,16},{28,24},{20,28},{12,20},{4,12},{0,4},{9,1},{1... | collective-permute-start | bytes 2654216 | tf_op jit(solution)/shard_map/ppermute | solution.py:351
  175.4 84.8 %collective-permute-start.46 = (bf16[384,1152]{1,0:T(8,128)(2,1)}, bf16[384,1152]{1,0:T(8,128)(2,1)}, u32[]{:S(2)}, u32[]{:S(2)}) collective-permute-start(bf16[384,1152]{1,0:T(8,128)(2,1)} %collective-permute-done.45), channel_id=1, source_target_pairs={{0,8},{8,16},{16,24},{24,28},{28,20},{20,12},{12,4},{4,0},{1,9},{9... | collective-permute-start | bytes 2654216 | tf_op jit(solution)/shard_map/ppermute | solution.py:350
  237.1 65.1 %collective-permute-start.33 = (bf16[2,512,1152]{2,1,0:T(8,128)(2,1)}, bf16[2,512,1152]{2,1,0:T(8,128)(2,1)S(1)}, u32[]{:S(2)}, u32[]{:S(2)}) collective-permute-start(bf16[2,512,1152]{2,1,0:T(8,128)(2,1)} %pad_maximum_fusion.4), channel_id=1, source_target_pairs={{0,1},{1,0},{2,3},{3,2},{4,5},{5,4},{6,7},{7,6},{8,9},{9,8},{10,11... | collective-permute-start | bytes 7077896 | tf_op jit(solution)/shard_map/ppermute | solution.py:371
  238.8 104.6 %collective-permute-start.43 = (bf16[192,1152]{1,0:T(8,128)(2,1)}, bf16[192,1152]{1,0:T(8,128)(2,1)}, u32[]{:S(2)}, u32[]{:S(2)}) collective-permute-start(bf16[192,1152]{1,0:T(8,128)(2,1)} %get-tuple-element.337), channel_id=1, source_target_pairs={{0,3},{1,2},{2,1},{3,0},{4,7},{5,6},{6,5},{7,4},{8,11},{9,10},{10,... | collective-permute-start | bytes 1327112 | tf_op jit(solution)/shard_map/ppermute | solution.py:371
  238.9 104.6 %collective-permute-start.42 = (bf16[192,1152]{1,0:T(8,128)(2,1)}, bf16[192,1152]{1,0:T(8,128)(2,1)}, u32[]{:S(2)}, u32[]{:S(2)}) collective-permute-start(bf16[192,1152]{1,0:T(8,128)(2,1)} %get-tuple-element.338), channel_id=1, source_target_pairs={{0,2},{1,3},{2,0},{3,1},{4,6},{5,7},{6,4},{7,5},{8,10},{9,11},{10,... | collective-permute-start | bytes 1327112 | tf_op jit(solution)/shard_map/ppermute | solution.py:371
  257.8 22.0 %collective-permute-start.53 = (bf16[384,1152]{1,0:T(8,128)(2,1)}, bf16[384,1152]{1,0:T(8,128)(2,1)S(1)}, u32[]{:S(2)}, u32[]{:S(2)}) collective-permute-start(bf16[384,1152]{1,0:T(8,128)(2,1)} %collective-permute-done.52), channel_id=1, source_target_pairs={{8,0},{16,8},{24,16},{28,24},{20,28},{12,20},{4,12},{0,4},{9,1},{1... | collective-permute-start | bytes 2654216 | tf_op jit(solution)/shard_map/ppermute | solution.py:351
  260.3 23.1 %collective-permute-start.47 = (bf16[384,1152]{1,0:T(8,128)(2,1)}, bf16[384,1152]{1,0:T(8,128)(2,1)S(1)}, u32[]{:S(2)}, u32[]{:S(2)}) collective-permute-start(bf16[384,1152]{1,0:T(8,128)(2,1)} %collective-permute-done.46), channel_id=1, source_target_pairs={{0,8},{8,16},{16,24},{24,28},{28,20},{20,12},{12,4},{4,0},{1,9},{9... | collective-permute-start | bytes 2654216 | tf_op jit(solution)/shard_map/ppermute | solution.py:350
  279.8 20.9 %collective-permute-start.54 = (bf16[384,1152]{1,0:T(8,128)(2,1)S(1)}, bf16[384,1152]{1,0:T(8,128)(2,1)S(1)}, u32[]{:S(2)}, u32[]{:S(2)}) collective-permute-start(bf16[384,1152]{1,0:T(8,128)(2,1)S(1)} %collective-permute-done.53), channel_id=1, source_target_pairs={{8,0},{16,8},{24,16},{28,24},{20,28},{12,20},{4,12},{0,4},{9,1},{1... | collective-permute-start | bytes 2654216 | tf_op jit(solution)/shard_map/ppermute | solution.py:351
  283.4 20.6 %collective-permute-start.48 = (bf16[384,1152]{1,0:T(8,128)(2,1)S(1)}, bf16[384,1152]{1,0:T(8,128)(2,1)S(1)}, u32[]{:S(2)}, u32[]{:S(2)}) collective-permute-start(bf16[384,1152]{1,0:T(8,128)(2,1)S(1)} %collective-permute-done.47), channel_id=1, source_target_pairs={{0,8},{8,16},{16,24},{24,28},{28,20},{20,12},{12,4},{4,0},{1,9},{9... | collective-permute-start | bytes 2654216 | tf_op jit(solution)/shard_map/ppermute | solution.py:350
  300.7 20.1 %collective-permute-start.55 = (bf16[384,1152]{1,0:T(8,128)(2,1)S(1)}, bf16[384,1152]{1,0:T(8,128)(2,1)}, u32[]{:S(2)}, u32[]{:S(2)}) collective-permute-start(bf16[384,1152]{1,0:T(8,128)(2,1)S(1)} %collective-permute-done.54), channel_id=1, source_target_pairs={{8,0},{16,8},{24,16},{28,24},{20,28},{12,20},{4,12},{0,4},{9,1},{1... | collective-permute-start | bytes 2654216 | tf_op jit(solution)/shard_map/ppermute | solution.py:351
  302.7 26.1 %collective-permute-start.34 = (bf16[512,1152]{1,0:T(8,128)(2,1)S(1)}, bf16[512,1152]{1,0:T(8,128)(2,1)S(1)}, u32[]{:S(2)}, u32[]{:S(2)}) collective-permute-start(bf16[512,1152]{1,0:T(8,128)(2,1)S(1)} %fusion.41), channel_id=1, source_target_pairs={{0,2},{1,3},{2,0},{3,1},{4,6},{5,7},{6,4},{7,5},{8,10},{9,11},{10,... | collective-permute-start | bytes 3538952 | tf_op jit(solution)/shard_map/ppermute | solution.py:371
  304.0 19.7 %collective-permute-start.49 = (bf16[384,1152]{1,0:T(8,128)(2,1)S(1)}, bf16[384,1152]{1,0:T(8,128)(2,1)S(1)}, u32[]{:S(2)}, u32[]{:S(2)}) collective-permute-start(bf16[384,1152]{1,0:T(8,128)(2,1)S(1)} %collective-permute-done.48), channel_id=1, source_target_pairs={{0,8},{8,16},{16,24},{24,28},{28,20},{20,12},{12,4},{4,0},{1,9},{9... | collective-permute-start | bytes 2654216 | tf_op jit(solution)/shard_map/ppermute | solution.py:350
  320.8 19.3 %collective-permute-start.56 = (bf16[384,1152]{1,0:T(8,128)(2,1)}, bf16[384,1152]{1,0:T(8,128)(2,1)S(1)}, u32[]{:S(2)}, u32[]{:S(2)}) collective-permute-start(bf16[384,1152]{1,0:T(8,128)(2,1)} %collective-permute-done.55), channel_id=1, source_target_pairs={{8,0},{16,8},{24,16},{28,24},{20,28},{12,20},{4,12},{0,4},{9,1},{1... | collective-permute-start | bytes 2654216 | tf_op jit(solution)/shard_map/ppermute | solution.py:351
  340.1 26.7 %collective-permute-start.50 = (bf16[384,1152]{1,0:T(8,128)(2,1)S(1)}, bf16[384,1152]{1,0:T(8,128)(2,1)S(1)}, u32[]{:S(2)}, u32[]{:S(2)}) collective-permute-start(bf16[384,1152]{1,0:T(8,128)(2,1)S(1)} %copy-done.73), channel_id=1, source_target_pairs={{0,8},{8,16},{16,24},{24,28},{28,20},{20,12},{12,4},{4,0},{1,9},{9... | collective-permute-start | bytes 2654216 | tf_op jit(solution)/shard_map/ppermute | solution.py:350
  342.7 27.3 %collective-permute-start.57 = (bf16[384,1152]{1,0:T(8,128)(2,1)S(1)}, bf16[384,1152]{1,0:T(8,128)(2,1)S(1)}, u32[]{:S(2)}, u32[]{:S(2)}) collective-permute-start(bf16[384,1152]{1,0:T(8,128)(2,1)S(1)} %collective-permute-done.56), channel_id=1, source_target_pairs={{8,0},{16,8},{24,16},{28,24},{20,28},{12,20},{4,12},{0,4},{9,1},{1... | collective-permute-start | bytes 2654216 | tf_op jit(solution)/shard_map/ppermute | solution.py:351
  343.5 21.9 %collective-permute-start.36 = (bf16[192,1152]{1,0:T(8,128)(2,1)S(1)}, bf16[192,1152]{1,0:T(8,128)(2,1)S(1)}, u32[]{:S(2)}, u32[]{:S(2)}) collective-permute-start(bf16[192,1152]{1,0:T(8,128)(2,1)S(1)} %get-tuple-element.342), channel_id=1, source_target_pairs={{0,2},{1,3},{2,0},{3,1},{4,6},{5,7},{6,4},{7,5},{8,10},{9,11},{10,... | collective-permute-start | bytes 1327112 | tf_op jit(solution)/shard_map/ppermute | solution.py:371
  345.1 20.4 %collective-permute-start.35 = (bf16[192,1152]{1,0:T(8,128)(2,1)S(1)}, bf16[192,1152]{1,0:T(8,128)(2,1)S(1)}, u32[]{:S(2)}, u32[]{:S(2)}) collective-permute-start(bf16[192,1152]{1,0:T(8,128)(2,1)S(1)} %get-tuple-element.343), channel_id=1, source_target_pairs={{0,1},{1,0},{2,3},{3,2},{4,5},{5,4},{6,7},{7,6},{8,9},{9,8},{10,11... | collective-permute-start | bytes 1327112 | tf_op jit(solution)/shard_map/ppermute | solution.py:371
  434.5 22.0 %collective-permute-start.59 = (bf16[192,1152]{1,0:T(8,128)(2,1)S(1)}, bf16[192,1152]{1,0:T(8,128)(2,1)S(1)}, u32[]{:S(2)}, u32[]{:S(2)}) collective-permute-start(bf16[192,1152]{1,0:T(8,128)(2,1)S(1)} %get-tuple-element.334), channel_id=1, source_target_pairs={{0,2},{1,3},{2,0},{3,1},{4,6},{5,7},{6,4},{7,5},{8,10},{9,11},{10,... | collective-permute-start | bytes 1327112 | tf_op jit(solution)/shard_map/ppermute | solution.py:371
  436.0 21.8 %collective-permute-start.58 = (bf16[192,1152]{1,0:T(8,128)(2,1)S(1)}, bf16[192,1152]{1,0:T(8,128)(2,1)S(1)}, u32[]{:S(2)}, u32[]{:S(2)}) collective-permute-start(bf16[192,1152]{1,0:T(8,128)(2,1)S(1)} %get-tuple-element.335), channel_id=1, source_target_pairs={{0,1},{1,0},{2,3},{3,2},{4,5},{5,4},{6,7},{7,6},{8,9},{9,8},{10,11... | collective-permute-start | bytes 1327112 | tf_op jit(solution)/shard_map/ppermute | solution.py:371
  436.3 29.2 %collective-permute-start.63 = (bf16[192,1152]{1,0:T(8,128)(2,1)S(1)}, bf16[192,1152]{1,0:T(8,128)(2,1)S(1)}, u32[]{:S(2)}, u32[]{:S(2)}) collective-permute-start(bf16[192,1152]{1,0:T(8,128)(2,1)S(1)} %get-tuple-element.329), channel_id=1, source_target_pairs={{0,3},{1,2},{2,1},{3,0},{4,7},{5,6},{6,5},{7,4},{8,11},{9,10},{10,... | collective-permute-start | bytes 1327112 | tf_op jit(solution)/shard_map/ppermute | solution.py:371
  436.8 38.4 %collective-permute-start.62 = (bf16[192,1152]{1,0:T(8,128)(2,1)S(1)}, bf16[192,1152]{1,0:T(8,128)(2,1)S(1)}, u32[]{:S(2)}, u32[]{:S(2)}) collective-permute-start(bf16[192,1152]{1,0:T(8,128)(2,1)S(1)} %get-tuple-element.330), channel_id=1, source_target_pairs={{0,2},{1,3},{2,0},{3,1},{4,6},{5,7},{6,4},{7,5},{8,10},{9,11},{10,... | collective-permute-start | bytes 1327112 | tf_op jit(solution)/shard_map/ppermute | solution.py:371
  446.5 30.3 %collective-permute-start.61 = (bf16[192,1152]{1,0:T(8,128)(2,1)S(1)}, bf16[192,1152]{1,0:T(8,128)(2,1)S(1)}, u32[]{:S(2)}, u32[]{:S(2)}) collective-permute-start(bf16[192,1152]{1,0:T(8,128)(2,1)S(1)} %get-tuple-element.331), channel_id=1, source_target_pairs={{0,1},{1,0},{2,3},{3,2},{4,5},{5,4},{6,7},{7,6},{8,9},{9,8},{10,11... | collective-permute-start | bytes 1327112 | tf_op jit(solution)/shard_map/ppermute | solution.py:371
  456.5 24.0 %collective-permute-start.85 = (bf16[192,1152]{1,0:T(8,128)(2,1)S(1)}, bf16[192,1152]{1,0:T(8,128)(2,1)S(1)}, u32[]{:S(2)}, u32[]{:S(2)}) collective-permute-start(bf16[192,1152]{1,0:T(8,128)(2,1)S(1)} %get-tuple-element.310), channel_id=1, source_target_pairs={{0,8},{8,16},{16,24},{24,28},{28,20},{20,12},{12,4},{4,0},{1,9},{9... | collective-permute-start | bytes 1327112 | tf_op jit(solution)/shard_map/ppermute | solution.py:360
  457.8 22.7 %collective-permute-start.92 = (bf16[192,1152]{1,0:T(8,128)(2,1)S(1)}, bf16[192,1152]{1,0:T(8,128)(2,1)S(1)}, u32[]{:S(2)}, u32[]{:S(2)}) collective-permute-start(bf16[192,1152]{1,0:T(8,128)(2,1)S(1)} %get-tuple-element.311), channel_id=1, source_target_pairs={{8,0},{16,8},{24,16},{28,24},{20,28},{12,20},{4,12},{0,4},{9,1},{1... | collective-permute-start | bytes 1327112 | tf_op jit(solution)/shard_map/ppermute | solution.py:361
  465.5 15.7 %collective-permute-start.99 = (bf16[192,1152]{1,0:T(8,128)(2,1)S(1)}, bf16[192,1152]{1,0:T(8,128)(2,1)S(1)}, u32[]{:S(2)}, u32[]{:S(2)}) collective-permute-start(bf16[192,1152]{1,0:T(8,128)(2,1)S(1)} %get-tuple-element.294), channel_id=1, source_target_pairs={{0,8},{8,16},{16,24},{24,28},{28,20},{20,12},{12,4},{4,0},{1,9},{9... | collective-permute-start | bytes 1327112 | tf_op jit(solution)/shard_map/ppermute | solution.py:360
  480.0 47.8 %collective-permute-start.65 = (bf16[512,1152]{1,0:T(8,128)(2,1)S(1)}, bf16[512,1152]{1,0:T(8,128)(2,1)S(1)}, u32[]{:S(2)}, u32[]{:S(2)}) collective-permute-start(bf16[512,1152]{1,0:T(8,128)(2,1)S(1)} %fusion.81), channel_id=1, source_target_pairs={{0,2},{1,3},{2,0},{3,1},{4,6},{5,7},{6,4},{7,5},{8,10},{9,11},{10,... | collective-permute-start | bytes 3538952 | tf_op jit(solution)/shard_map/ppermute | solution.py:371
  480.5 95.5 %collective-permute-start.64 = (bf16[512,1152]{1,0:T(8,128)(2,1)S(1)}, bf16[512,1152]{1,0:T(8,128)(2,1)S(1)}, u32[]{:S(2)}, u32[]{:S(2)}) collective-permute-start(bf16[512,1152]{1,0:T(8,128)(2,1)S(1)} %fusion.81), channel_id=1, source_target_pairs={{0,1},{1,0},{2,3},{3,2},{4,5},{5,4},{6,7},{7,6},{8,9},{9,8},{10,11... | collective-permute-start | bytes 3538952 | tf_op jit(solution)/shard_map/ppermute | solution.py:371
  481.2 16.3 %collective-permute-start.93 = (bf16[192,1152]{1,0:T(8,128)(2,1)S(1)}, bf16[192,1152]{1,0:T(8,128)(2,1)S(1)}, u32[]{:S(2)}, u32[]{:S(2)}) collective-permute-start(bf16[192,1152]{1,0:T(8,128)(2,1)S(1)} %get-tuple-element.309), channel_id=1, source_target_pairs={{8,0},{16,8},{24,16},{28,24},{20,28},{12,20},{4,12},{0,4},{9,1},{1... | collective-permute-start | bytes 1327112 | tf_op jit(solution)/shard_map/ppermute | solution.py:361
  527.8 17.2 %collective-permute-start.109 = (bf16[192,1152]{1,0:T(8,128)(2,1)S(1)}, bf16[192,1152]{1,0:T(8,128)(2,1)S(1)}, u32[]{:S(2)}, u32[]{:S(2)}) collective-permute-start(bf16[192,1152]{1,0:T(8,128)(2,1)S(1)} %get-tuple-element.289), channel_id=1, source_target_pairs={{8,0},{16,8},{24,16},{28,24},{20,28},{12,20},{4,12},{0,4},{9,1},{1... | collective-permute-start | bytes 1327112 | tf_op jit(solution)/shard_map/ppermute | solution.py:361
  531.7 44.4 %collective-permute-start.66 = (bf16[512,1152]{1,0:T(8,128)(2,1)S(1)}, bf16[512,1152]{1,0:T(8,128)(2,1)S(1)}, u32[]{:S(2)}, u32[]{:S(2)}) collective-permute-start(bf16[512,1152]{1,0:T(8,128)(2,1)S(1)} %collective-permute-done.65), channel_id=1, source_target_pairs={{0,1},{1,0},{2,3},{3,2},{4,5},{5,4},{6,7},{7,6},{8,9},{9,8},{10,11... | collective-permute-start | bytes 3538952 | tf_op jit(solution)/shard_map/ppermute | solution.py:371
  565.0 147.8 %collective-permute-start.104 = (bf16[192,1152]{1,0:T(8,128)(2,1)}, bf16[192,1152]{1,0:T(8,128)(2,1)}, u32[]{:S(2)}, u32[]{:S(2)}) collective-permute-start(bf16[192,1152]{1,0:T(8,128)(2,1)} %get-tuple-element.284), channel_id=1, source_target_pairs={{0,8},{8,16},{16,24},{24,28},{28,20},{20,12},{12,4},{4,0},{1,9},{9... | collective-permute-start | bytes 1327112 | tf_op jit(solution)/shard_map/ppermute | solution.py:360
  569.6 143.2 %collective-permute-start.111 = (bf16[192,1152]{1,0:T(8,128)(2,1)}, bf16[192,1152]{1,0:T(8,128)(2,1)}, u32[]{:S(2)}, u32[]{:S(2)}) collective-permute-start(bf16[192,1152]{1,0:T(8,128)(2,1)} %get-tuple-element.285), channel_id=1, source_target_pairs={{8,0},{16,8},{24,16},{28,24},{20,28},{12,20},{4,12},{0,4},{9,1},{1... | collective-permute-start | bytes 1327112 | tf_op jit(solution)/shard_map/ppermute | solution.py:361
  573.9 150.3 %collective-permute-start.91 = (bf16[192,1152]{1,0:T(8,128)(2,1)}, bf16[192,1152]{1,0:T(8,128)(2,1)}, u32[]{:S(2)}, u32[]{:S(2)}) collective-permute-start(bf16[192,1152]{1,0:T(8,128)(2,1)} %get-tuple-element.298), channel_id=1, source_target_pairs={{0,8},{8,16},{16,24},{24,28},{28,20},{20,12},{12,4},{4,0},{1,9},{9... | collective-permute-start | bytes 1327112 | tf_op jit(solution)/shard_map/ppermute | solution.py:360
  576.0 149.8 %collective-permute-start.98 = (bf16[192,1152]{1,0:T(8,128)(2,1)}, bf16[192,1152]{1,0:T(8,128)(2,1)}, u32[]{:S(2)}, u32[]{:S(2)}) collective-permute-start(bf16[192,1152]{1,0:T(8,128)(2,1)} %get-tuple-element.299), channel_id=1, source_target_pairs={{8,0},{16,8},{24,16},{28,24},{20,28},{12,20},{4,12},{0,4},{9,1},{1... | collective-permute-start | bytes 1327112 | tf_op jit(solution)/shard_map/ppermute | solution.py:361
  715.2 18.3 %collective-permute-start.112 = (bf16[192,1152]{1,0:T(8,128)(2,1)S(1)}, bf16[192,1152]{1,0:T(8,128)(2,1)S(1)}, u32[]{:S(2)}, u32[]{:S(2)}) collective-permute-start(bf16[192,1152]{1,0:T(8,128)(2,1)S(1)} %get-tuple-element.283), channel_id=1, source_target_pairs={{8,0},{16,8},{24,16},{28,24},{20,28},{12,20},{4,12},{0,4},{9,1},{1... | collective-permute-start | bytes 1327112 | tf_op jit(solution)/shard_map/ppermute | solution.py:361
  724.0 30.5 %collective-permute-start.67 = (bf16[2048,104]{1,0:T(8,128)(2,1)}, bf16[2048,104]{1,0:T(8,128)(2,1)}, u32[]{:S(2)}, u32[]{:S(2)}) collective-permute-start(bf16[2048,104]{1,0:T(8,128)(2,1)} %get-tuple-element.80), channel_id=1, source_target_pairs={{0,1},{1,0},{2,3},{3,2},{4,5},{5,4},{6,7},{7,6},{8,9},{9,8},{10,11... | collective-permute-start | bytes 1277960 | tf_op jit(solution)/shard_map/ppermute | solution.py:371
  724.2 15.7 %collective-permute-start.79 = (bf16[72,1664]{0,1:T(8,128)(2,1)S(1)}, bf16[72,1664]{0,1:T(8,128)(2,1)S(1)}, u32[]{:S(2)}, u32[]{:S(2)}) collective-permute-start(bf16[72,1664]{0,1:T(8,128)(2,1)S(1)} %add_convert_fusion.42), channel_id=1, source_target_pairs={{8,0},{16,8},{24,16},{28,24},{20,28},{12,20},{4,12},{0,4},{9,1},{1... | collective-permute-start | bytes 718856 | tf_op jit(solution)/shard_map/ppermute | solution.py:361
  757.6 51.3 %collective-permute-start.81 = (bf16[72,1664]{0,1:T(8,128)(2,1)S(1)}, bf16[72,1664]{0,1:T(8,128)(2,1)}, u32[]{:S(2)}, u32[]{:S(2)}) collective-permute-start(bf16[72,1664]{0,1:T(8,128)(2,1)S(1)} %add_convert_fusion.40), channel_id=1, source_target_pairs={{8,0},{16,8},{24,16},{28,24},{20,28},{12,20},{4,12},{0,4},{9,1},{1... | collective-permute-start | bytes 718856 | tf_op jit(solution)/shard_map/ppermute | solution.py:361
  788.3 121.2 %collective-permute-start.69 = (bf16[2,512,1152]{2,1,0:T(8,128)(2,1)}, bf16[2,512,1152]{2,1,0:T(8,128)(2,1)}, u32[]{:S(2)}, u32[]{:S(2)}) collective-permute-start(bf16[2,512,1152]{2,1,0:T(8,128)(2,1)} %pad_maximum_fusion.5), channel_id=1, source_target_pairs={{0,1},{1,0},{2,3},{3,2},{4,5},{5,4},{6,7},{7,6},{8,9},{9,8},{10,11... | collective-permute-start | bytes 7077896 | tf_op jit(solution)/shard_map/ppermute | solution.py:371
  810.2 32.5 %collective-permute-start.82 = (bf16[72,1664]{0,1:T(8,128)(2,1)S(1)}, bf16[72,1664]{0,1:T(8,128)(2,1)S(1)}, u32[]{:S(2)}, u32[]{:S(2)}) collective-permute-start(bf16[72,1664]{0,1:T(8,128)(2,1)S(1)} %add_convert_fusion.39), channel_id=1, source_target_pairs={{8,0},{16,8},{24,16},{28,24},{20,28},{12,20},{4,12},{0,4},{9,1},{1... | collective-permute-start | bytes 718856 | tf_op jit(solution)/shard_map/ppermute | solution.py:361
  915.1 18.2 %collective-permute-start.70 = (bf16[512,1152]{1,0:T(8,128)(2,1)}, bf16[512,1152]{1,0:T(8,128)(2,1)S(1)}, u32[]{:S(2)}, u32[]{:S(2)}) collective-permute-start(bf16[512,1152]{1,0:T(8,128)(2,1)} %fusion.42), channel_id=1, source_target_pairs={{0,2},{1,3},{2,0},{3,1},{4,6},{5,7},{6,4},{7,5},{8,10},{9,11},{10,... | collective-permute-start | bytes 3538952 | tf_op jit(solution)/shard_map/ppermute | solution.py:371
  (208 other events, 2956.0 us)

commit v2 on v0

v2 whole, which is shorter than its diff:
```python
import functools
import math

import jax
import jax.numpy as jnp
from jax import lax
from jax.experimental import pallas as pl
from jax.experimental.pallas import tpu as pltpu
from jax.sharding import PartitionSpec as P

bf16, f32 = jnp.bfloat16, jnp.float32
CONV, DT_RANK, SUBT, NST = 4, 72, 16, 16
LOG2E = 1.0 / math.log(2.0)
LANES = 128
BLOCK = 256
CAP = 192
EPSILON = 1e-05
MOMENT = 0.9
SMOOTH = 0.6
LEARNING = (0.02, 0.03, 0.4, 0.3, 0.04, 0.07, 0.3, 0.3, 0.01)
HIGHEST = lax.Precision.HIGHEST
MIB = 2**20
SHAPE = jax.ShapeDtypeStruct


def dotf(a, b, dims=((1,), (0,))):
    return lax.dot_general(a, b, (dims, ((), ())), preferred_element_type=f32)


def block_mask():
    r = lax.broadcasted_iota(jnp.int32, (SUBT, SUBT * NST), 0)
    c = lax.broadcasted_iota(jnp.int32, (SUBT, SUBT * NST), 1)
    return (c // NST == r).astype(f32)


def spread(first, rows):
    r = lax.broadcasted_iota(jnp.int32, (rows, SUBT * NST), 0)
    c = lax.broadcasted_iota(jnp.int32, (rows, SUBT * NST), 1)
    return (c % NST + first == r).astype(bf16)


def soft_parts(x):
    e = jnp.exp(-jnp.abs(x))
    return jnp.maximum(x, 0.0) + jnp.log1p(e), jnp.where(x >= 0, 1.0, e) / (1.0 + e)


def row8(ref, k, t):
    d = ref[k, pl.ds(t, 8, stride=0), :]
    return jnp.concatenate([d, d], 0)


def split_states(sel_ref, bts, cts, T):
    selT = sel_ref[...].T
    for k in range(T // SUBT):
        bts[k] = selT[DT_RANK : DT_RANK + NST, SUBT * k : SUBT * k + SUBT]
        cts[k] = selT[DT_RANK + NST : DT_RANK + 2 * NST, SUBT * k : SUBT * k + SUBT]


def blocked(sel_ref, k, place, mask):
    sel = sel_ref[pl.ds(pl.multiple_of(k * SUBT, SUBT), SUBT), :]
    return (dotf(sel.astype(bf16), place) * mask).astype(bf16)


def blocked_all(sel_ref, place, T):
    r = lax.broadcasted_iota(jnp.int32, (T, SUBT * NST), 0)
    c = lax.broadcasted_iota(jnp.int32, (T, SUBT * NST), 1)
    flat = jnp.where(c // NST == r % SUBT, dotf(sel_ref[...].astype(bf16), place), 0.0)
    return flat.astype(bf16).reshape(T // SUBT, SUBT, SUBT * NST)


def rows_at(T, w, first=0):
    return pl.BlockSpec((T, w), lambda i: (first + i, 0))


def rows_back(T, w, last):
    return pl.BlockSpec((T, w), lambda i: (last - i, 0))


def whole(shape):
    shape = tuple(shape)
    return pl.BlockSpec(shape, lambda i: (0,) * len(shape))


def params(mib):
    return pltpu.CompilerParams(vmem_limit_bytes=mib * MIB)


def cost(flops=0, moved=1 << 20):
    return pl.CostEstimate(flops=flops, bytes_accessed=moved, transcendentals=0)


def turned(a):
    short = -a.shape[1] % LANES
    if short:
        a = jnp.concatenate([a, jnp.zeros((a.shape[0], short), f32)], axis=1)
    return a.T


def prep_kernel(in_ref, sel_ref, delta_ref, chan_ref, out_ref, a_ref, b_ref, *, half):
    own = sel_ref.shape[0]
    xw, vrows = sel_ref.shape[1], chan_ref.shape[0]
    width = in_ref.shape[2]
    a_ref[:, 0:width] = in_ref[0].astype(bf16)
    a_ref[:, width:] = out_ref[:, 0:half].astype(bf16)
    small = jnp.concatenate(
        [
            delta_ref[...],
            chan_ref[...],
            jnp.zeros((LANES - DT_RANK - vrows, own), f32),
        ],
        axis=0,
    )
    select = jnp.concatenate([sel_ref[...], jnp.zeros((own, LANES - xw), f32)], axis=1)
    b_ref[:, 0:width] = in_ref[1].astype(bf16)
    b_ref[:, width : width + LANES] = select.astype(bf16)
    b_ref[:, width + LANES : width + 2 * LANES] = turned(small)[0:own].astype(bf16)
    b_ref[:, width + 2 * LANES :] = out_ref[:, half:].astype(bf16)


def prep(inward, select, delta, channel, outward, half):
    own, width = outward.shape
    return pl.pallas_call(
        functools.partial(prep_kernel, half=half),
        out_shape=[SHAPE((own, width + half), bf16), SHAPE((own, 2 * width - half + 2 * LANES), bf16)],
        compiler_params=params(40),
        cost_estimate=cost(),
    )(inward, select, delta, channel, outward)


def prep_experts_kernel(up_ref, down_ref, both_ref):
    units = down_ref.shape[0]
    both_ref[0:units, :] = turned(up_ref[...])[0:units].astype(bf16)
    both_ref[units : 2 * units, :] = down_ref[...].astype(bf16)


def prep_experts(up, down):
    return pl.pallas_call(
        prep_experts_kernel,
        out_shape=SHAPE((2 * down.shape[0], down.shape[1]), bf16),
        compiler_params=params(40),
        cost_estimate=cost(),
    )(up, down)


def mixer_weights_kernel(owner_ref, *refs, ring, own, slot, width, half):
    a, b = refs[:ring], refs[ring : 2 * ring]
    w_ref, selw_ref, delta_ref, chan_ref, out_ref, small = refs[2 * ring :]
    wide = selw_ref.shape[0]
    if wide > ring * slot:
        for ref in (w_ref, selw_ref, out_ref, small):
            ref[...] = jnp.zeros_like(ref)

    def place(ref, at, value):
        if slot > own:
            value = jnp.concatenate([value, jnp.zeros((slot - own, value.shape[1]), value.dtype)], axis=0)
        ref[pl.ds(pl.multiple_of(at, 16), slot), :] = value

    for r in range(ring):
        at = owner_ref[r] * slot
        place(w_ref, at, a[r][:, 0:width])
        place(w_ref, wide + at, b[r][:, 0:width])
        place(selw_ref, at, b[r][:, width : width + LANES])
        place(small, at, b[r][:, width + LANES : width + 2 * LANES].astype(f32))
        place(out_ref, at, jnp.concatenate([a[r][:, width:], b[r][:, width + 2 * LANES :]], axis=1))
    flat = small[...].T
    delta_ref[0:DT_RANK, :] = flat[0:DT_RANK].astype(bf16)
    delta_ref[DT_RANK:LANES, :] = jnp.zeros((LANES - DT_RANK, wide), bf16)
    chan_ref[...] = flat[DT_RANK : DT_RANK + chan_ref.shape[0]]


def mixer_weights(owners, a, b, slot, wide, width, half):
    ring = len(a)
    own = b[0].shape[0]
    return pl.pallas_call(
        functools.partial(mixer_weights_kernel, ring=ring, own=own, slot=slot, width=width, half=half),
        in_specs=[pl.BlockSpec(memory_space=pltpu.SMEM)] + [pl.BlockSpec(memory_space=pltpu.VMEM)] * (2 * ring),
        out_shape=[
            SHAPE((2 * wide, width), bf16),
            SHAPE((wide, LANES), bf16),
            SHAPE((LANES, wide), bf16),
            SHAPE((24, wide), f32),
            SHAPE((wide, width), bf16),
        ],
        scratch_shapes=[pltpu.VMEM((wide, LANES), f32)],
        compiler_params=params(48),
        cost_estimate=cost(),
    )(owners, *a, *b)


def conv_fwd_kernel(seq_ref, w_ref, chan_ref, selw_ref, tail_ref, conv_ref, gate_ref, pre_ref, act_ref, actb_ref, sel_ref, end_ref, buf, *, T):
    C = conv_ref.shape[1]

    @pl.when(pl.program_id(0) == 0)
    def _():
        buf[0:8, :] = tail_ref[...]

    seq = seq_ref[...]
    conv = dotf(seq, w_ref[0:C, :], ((1,), (1,)))
    gate_ref[...] = dotf(seq, w_ref[C : 2 * C, :], ((1,), (1,)))
    conv_ref[...] = conv
    buf[8 : 8 + T, :] = conv
    pre = chan_ref[CONV : CONV + 1, :] + chan_ref[CONV - 1 : CONV, :] * conv
    for tap in range(CONV - 1):
        at = 8 - CONV + 1 + tap
        pre = pre + chan_ref[tap : tap + 1, :] * buf[at : at + T, :]
    buf[0:8, :] = buf[T : T + 8, :]
    end_ref[...] = buf[0:8, :]
    pre_ref[...] = pre
    act = pre / (1.0 + jnp.exp(-pre))
    act_ref[...] = act
    actb = act.astype(bf16)
    actb_ref[...] = actb
    sel_ref[...] = dotf(actb, selw_ref[...])


def conv_fwd(seq, first, count, w_in, chan, selw, tail, T=BLOCK):
    C, D = chan.shape[1], seq.shape[1]
    return pl.pallas_call(
        functools.partial(conv_fwd_kernel, T=T),
        grid=(count // T,),
        in_specs=[rows_at(T, D, first // T), whole(w_in.shape), whole(chan.shape), whole(selw.shape), whole(tail.shape)],
        out_specs=[rows_at(T, C)] * 5 + [rows_at(T, LANES), whole((8, C))],
        out_shape=[SHAPE((count, C), f32)] * 4 + [SHAPE((count, C), bf16), SHAPE((count, LANES), f32), SHAPE((8, C), f32)],
        scratch_shapes=[pltpu.VMEM((T + 8, C), f32)],
        compiler_params=params(48),
        cost_estimate=cost(),
    )(seq, w_in, chan, selw, tail)


def scan_fwd_kernel(
    sel_ref, delta_w_ref, act_ref, gate_ref, chan_ref, out_w_ref, start_ref,
    s_ref, xlin_ref, scanned_ref, gated_ref, mix_ref, rank_ref, end_ref,
    state, dscr, uscr, yscr, bts, cts, blocks, sA, sB, *, T
):
    C = act_ref.shape[1]
    NCH = T // SUBT

    @pl.when(pl.program_id(0) == 0)
    def _():
        state[...] = start_ref[...]

    rank = sel_ref[...].astype(bf16)
    rank_ref[...] = rank
    x = dotf(rank, delta_w_ref[...]) + chan_ref[CONV + 1 : CONV + 2, :]
    xlin_ref[...] = x
    sp, _ = soft_parts(x)
    dscr[...] = sp.reshape(NCH, SUBT, C)
    uscr[...] = (sp * act_ref[...]).reshape(NCH, SUBT, C)
    split_states(sel_ref, bts, cts, T)
    nrate = -LOG2E * jnp.exp(chan_ref[CONV + 3 : CONV + 3 + NST, :])
    blocks[...] = blocked_all(sel_ref, spread(DT_RANK + NST, LANES), T)

    def one(k, S, cur, prev):
        before = jnp.maximum(k - 1, 0)
        yv = dotf(blocks[before], prev[...])
        bt = bts[k]
        for t in range(SUBT):
            d = row8(dscr, k, t)
            u = row8(uscr, k, t)
            S = jnp.exp2(d * nrate) * S + u * jnp.broadcast_to(bt[:, t : t + 1], (NST, C))
            rounded = S.astype(bf16)
            cur[t * NST : t * NST + NST, :] = rounded
            s_ref[k, t * NST : t * NST + NST, :] = rounded
        yscr[before] = yv
        return S

    def pair(j, S):
        S = one(2 * j, S, sA, sB)
        return one(2 * j + 1, S, sB, sA)

    sB[...] = jnp.zeros_like(sB)
    state[...] = lax.fori_loop(0, NCH // 2, pair, state[...])
    end_ref[...] = state[...]
    yscr[NCH - 1] = dotf(blocks[NCH - 1], sB[...])
    scanned = yscr[...].reshape(T, C) + chan_ref[CONV + 2 : CONV + 3, :] * act_ref[...]
    scanned_ref[...] = scanned
    g = gate_ref[...]
    gated = (scanned * (g / (1.0 + jnp.exp(-g)))).astype(bf16)
    gated_ref[...] = gated
    mix_ref[...] = dotf(gated, out_w_ref[...]).astype(mix_ref.dtype)


def scan_fwd(sel, delta_w, act, gate, chan, out_w, start, T=BLOCK):
    N, C = act.shape
    W = out_w.shape[1]
    g, nch = N // T, T // SUBT
    vm = pltpu.VMEM
    return pl.pallas_call(
        functools.partial(scan_fwd_kernel, T=T),
        grid=(g,),
        in_specs=[rows_at(T, LANES), whole(delta_w.shape), rows_at(T, C), rows_at(T, C), whole(chan.shape), whole(out_w.shape), whole(start.shape)],
        out_specs=[pl.BlockSpec((nch, SUBT * NST, C), lambda i: (i, 0, 0))] + [rows_at(T, C)] * 3 + [rows_at(T, W), rows_at(T, LANES), whole((NST, C))],
        out_shape=[
            SHAPE((N // SUBT, SUBT * NST, C), bf16), SHAPE((N, C), f32), SHAPE((N, C), f32), SHAPE((N, C), bf16),
            SHAPE((N, W), bf16), SHAPE((N, LANES), bf16), SHAPE((NST, C), f32),
        ],
        scratch_shapes=[vm((NST, C), f32)] + [vm((nch, SUBT, C), f32)] * 3 + [vm((nch, NST, SUBT), f32)] * 2 + [vm((nch, SUBT, SUBT * NST), bf16)] + [vm((SUBT * NST, C), bf16)] * 2,
        compiler_params=params(48),
        cost_estimate=cost(),
    )(sel, delta_w, act, gate, chan, out_w, start)


def gather_states(first):
    r = lax.broadcasted_iota(jnp.int32, (SUBT * NST, LANES), 0)
    c = lax.broadcasted_iota(jnp.int32, (SUBT * NST, LANES), 1)
    return (r % NST + first == c).astype(bf16)


def fold(a):
    return sum(a[:, i : i + LANES] for i in range(LANES, a.shape[1], LANES)) + a[:, 0:LANES]


def scan_bwd_kernel(
    dmix_ref, out_w_ref, s_ref, before_ref, edge_ref, act_ref, gate_ref, xlin_ref, scanned_ref, sel_ref, chan_ref, delta_w_ref, q_ref,
    dgate_ref, dact_ref, ddl_ref, dsel_ref, gch_ref, qend_ref,
    qscr, dscr, uscr, dyscr, lbscr, wsscr, bts, cts, blocks, rows_b, rows_c, *bufs, T, g, opens
):
    C = act_ref.shape[1]
    NCH = T // SUBT
    step = pl.program_id(0)

    @pl.when(step == 0)
    def _():
        qscr[...] = q_ref[...]
        gch_ref[...] = jnp.zeros_like(gch_ref)

    dg = dotf(dmix_ref[...], out_w_ref[...], ((1,), (1,)))
    gt = gate_ref[...]
    sg = 1.0 / (1.0 + jnp.exp(-gt))
    dgate_ref[...] = (dg * scanned_ref[...] * (sg * (1.0 + gt * (1.0 - sg)))).astype(bf16)
    dy = dg * (gt * sg)
    act = act_ref[...]
    sp, sigd = soft_parts(xlin_ref[...])
    dscr[...] = sp.reshape(NCH, SUBT, C)
    uscr[...] = (sp * act).reshape(NCH, SUBT, C)
    dyscr[...] = dy.reshape(NCH, SUBT, C)
    split_states(sel_ref, bts, cts, T)
    nrate = -LOG2E * jnp.exp(chan_ref[CONV + 3 : CONV + 3 + NST, :])
    mask = block_mask()
    eb = spread(DT_RANK, LANES)
    half_rows = lax.broadcasted_iota(jnp.int32, (SUBT, SUBT * NST // 2), 0)
    half_cols = lax.broadcasted_iota(jnp.int32, (SUBT, SUBT * NST // 2), 1)
    halves = (half_cols // (NST // 2) == half_rows).astype(bf16)
    ones = jnp.ones((SUBT, LANES), bf16)
    last = slice(SUBT * NST - NST, SUBT * NST)
    first = before_ref[0, last, :].astype(f32)
    if opens:
        first = jnp.where(step == g - 1, edge_ref[...], first)

    def lanes_summed(partial):
        return (dotf(ones, partial[...].astype(bf16), ((1,), (1,))) * mask).astype(bf16)

    blocks[...] = blocked_all(sel_ref, eb, T)

    def one(k, q, acc, cur, prev):
        kp = jnp.minimum(k + 1, NCH - 1)
        lam_ref, w_ref, pb_ref, pc_ref = prev
        lamb = dotf(blocks[kp], lam_ref[...])
        wsum = dotf(halves, w_ref[...])
        sum_b, sum_c = lanes_summed(pb_ref), lanes_summed(pc_ref)
        lam_ref, w_ref, pb_ref, pc_ref = cur
        bt = bts[k]
        ct = cts[k]
        s_t = s_ref[k, last, :].astype(f32)
        s_before = jnp.where(k == 0, first, s_ref[jnp.maximum(k - 1, 0), last, :].astype(f32))
        held = None
        for t in range(SUBT - 1, -1, -1):
            d = row8(dscr, k, t)
            u = row8(uscr, k, t)
            dyr = row8(dyscr, k, t)
            lam = jnp.broadcast_to(ct[:, t : t + 1], (NST, C)) * dyr + q
            lam_ref[t * NST : t * NST + NST, :] = lam.astype(bf16)
            q = jnp.exp2(d * nrate) * lam
            pc_ref[t * NST : t * NST + NST, :] = fold(s_t * dyr)
            pb_ref[t * NST : t * NST + NST, :] = fold(lam * u)
            s_p = s_ref[k, t * NST - NST : t * NST, :].astype(f32) if t > 0 else s_before
            wr = q * s_p * nrate
            part = wr[0 : NST // 2] + wr[NST // 2 :]
            if t % 2:
                held = part
            else:
                w_ref[t * NST // 2 : t * NST // 2 + NST, :] = jnp.concatenate([part, held], axis=0).astype(bf16)
            acc = acc + wr * d
            s_t = s_p
        lbscr[kp] = lamb
        wsscr[kp] = wsum
        rows_b[kp] = sum_b
        rows_c[kp] = sum_c
        return q, acc

    def pair(j, carry):
        k = NCH - 1 - 2 * j
        carry = one(k, *carry, bufs[0:4], bufs[4:8])
        return one(k - 1, *carry, bufs[4:8], bufs[0:4])

    for ref in bufs[4:8]:
        ref[...] = jnp.zeros_like(ref)
    q, acc = lax.fori_loop(0, NCH // 2, pair, (qscr[...], jnp.zeros((NST, C), f32)))
    lam_ref, w_ref, pb_ref, pc_ref = bufs[4:8]
    lbscr[0] = dotf(blocks[0], lam_ref[...])
    wsscr[0] = dotf(halves, w_ref[...])
    rows_b[0] = lanes_summed(pb_ref)
    rows_c[0] = lanes_summed(pc_ref)
    qscr[...] = q
    qend_ref[...] = q
    gch_ref[CONV + 3 : CONV + 3 + NST, :] += acc * (1.0 / LOG2E)
    lamB = lbscr[...].reshape(T, C)
    ws = wsscr[...].reshape(T, C) * (-1.0 / LOG2E)
    dyf = dyscr[...].reshape(T, C)
    spf = dscr[...].reshape(T, C)
    dact_ref[...] = chan_ref[CONV + 2 : CONV + 3, :] * dyf + spf * lamB
    ddl = (act * lamB - ws) * sigd
    ddl_ref[...] = ddl.astype(bf16)
    gch_ref[CONV + 1 : CONV + 2, :] += jnp.sum(ddl, axis=0, keepdims=True)
    gch_ref[CONV + 2 : CONV + 3, :] += jnp.sum(dyf * act, axis=0, keepdims=True)
    flat = lambda ref: ref[...].reshape(T, SUBT * NST)
    dsel = dotf(ddl_ref[...], delta_w_ref[...], ((1,), (1,)))
    dsel = dsel + dotf(flat(rows_b), gather_states(DT_RANK)) + dotf(flat(rows_c), gather_states(DT_RANK + NST))
    dsel_ref[...] = dsel.astype(bf16)


def scan_bwd(dmix, at, half, kept, edge, q, count, out_w, sel, chan, delta_w, T=BLOCK):
    s_all, act, gate, xlin, scanned = kept
    C = act.shape[1]
    g, nch = count // T, T // SUBT
    low = half // T
    row = lambda w: rows_back(T, w, low + g - 1)
    out = lambda w: rows_back(T, w, g - 1)
    vm = pltpu.VMEM
    return pl.pallas_call(
        functools.partial(scan_bwd_kernel, T=T, g=g, opens=low == 0),
        grid=(g,),
        in_specs=[
            rows_back(T, dmix.shape[1], at // T + g - 1), whole(out_w.shape),
            pl.BlockSpec((nch, SUBT * NST, C), lambda i: (low + g - 1 - i, 0, 0)),
            pl.BlockSpec((1, SUBT * NST, C), lambda i: (jnp.maximum((low + g - 1 - i) * nch - 1, 0), 0, 0)),
            whole(edge.shape),
            row(C), row(C), row(C), row(C), row(LANES), whole(chan.shape), whole(delta_w.shape), whole(q.shape),
        ],
        out_specs=[out(C), out(C), out(C), out(LANES), whole((24, C)), whole((NST, C))],
        out_shape=[
            SHAPE((count, C), bf16), SHAPE((count, C), f32), SHAPE((count, C), bf16), SHAPE((count, LANES), bf16),
            SHAPE((24, C), f32), SHAPE((NST, C), f32),
        ],
        scratch_shapes=[vm((NST, C), f32)] + [vm((nch, SUBT, C), f32)] * 5 + [vm((nch, NST, SUBT), f32)] * 2 + [vm((nch, SUBT, SUBT * NST), bf16)] * 3
        + [vm((SUBT * NST, C), bf16), vm((SUBT * NST // 2, C), bf16), vm((SUBT * NST, LANES), f32), vm((SUBT * NST, LANES), f32)] * 2,
        compiler_params=params(56),
        cost_estimate=cost(),
    )(dmix, out_w, s_all, s_all, edge, act, gate, xlin, scanned, sel, chan, delta_w, q)


def conv_bwd_kernel(
    dact_ref, dsel_ref, selw_ref, pre_ref, conv_ref, dgate_ref, w_ref, seq_ref, chan_ref, next_ref,
    actb_ref, ddl_ref, rank_ref, before_ref, gchin_ref, tail_ref,
    dnorm_ref, gain_ref, head_ref, gch_ref, grad_ref, buf, acc, *, T, g, final
):
    C, D = conv_ref.shape[1], seq_ref.shape[1]
    step = pl.program_id(0)

    @pl.when(step == 0)
    def _():
        buf[T : T + 8, :] = next_ref[...]
        gch_ref[...] = gchin_ref[...]
        gain_ref[...] = jnp.zeros_like(gain_ref)
        acc[...] = before_ref[...]

    pre = pre_ref[...]
    sig = 1.0 / (1.0 + jnp.exp(-pre))
    dsel = dsel_ref[...]
    dact = dact_ref[...] + dotf(dsel, selw_ref[...], ((1,), (1,)))
    dpre = dact * (sig * (1.0 + pre * (1.0 - sig)))
    buf[0:T, :] = dpre
    conv = conv_ref[...]
    total = chan_ref[CONV - 1 : CONV, :] * dpre
    gch_ref[CONV - 1 : CONV, :] += jnp.sum(conv * dpre, axis=0, keepdims=True)
    for tap in range(CONV - 1):
        later = buf[CONV - 1 - tap : CONV - 1 - tap + T, :]
        total = total + chan_ref[tap : tap + 1, :] * later
        gch_ref[tap : tap + 1, :] += jnp.sum(conv * later, axis=0, keepdims=True)
    gch_ref[CONV : CONV + 1, :] += jnp.sum(dpre, axis=0, keepdims=True)
    buf[T : T + 8, :] = buf[0:8, :]
    head_ref[...] = buf[0:8, :]
    dconv = total.astype(bf16)
    seq = seq_ref[...]
    rows = ((0,), (0,))
    acc[:, 0:D] += dotf(dconv, seq, rows)
    acc[:, D : D + LANES] += dotf(actb_ref[...], dsel, rows)
    keep = lax.broadcasted_iota(jnp.int32, (T, LANES), 1) < DT_RANK
    rank = jnp.where(keep, rank_ref[...].astype(f32), 0.0).astype(bf16)
    acc[:, D + LANES :] += dotf(ddl_ref[...], rank, rows)
    dnorm = dotf(dconv, w_ref[0:C, :]) + dotf(dgate_ref[...], w_ref[C : 2 * C, :])
    dnorm_ref[...] = dnorm.astype(bf16)
    gain_ref[0:1, :] += jnp.sum(dnorm * seq.astype(f32), axis=0, keepdims=True)

    @pl.when(step == g - 1)
    def _():
        if final:
            taps = jnp.where(lax.broadcasted_iota(jnp.int32, (8, C), 0) <= CONV, gch_ref[...], tail_ref[0:8, :])
            side = jnp.concatenate(
                [jnp.zeros((DT_RANK, C), f32), taps, tail_ref[8:, :], jnp.zeros((LANES - DT_RANK - 24, C), f32)], axis=0
            )
            acc[:, D + LANES :] += side.T
        grad_ref[...] = acc[...].astype(grad_ref.dtype)


def conv_bwd(at, count, final, dact, dsel, selw, pre, conv, dgate, w_in, seq, chan, later, actb, ddl, rank, before, gch, tail, T=BLOCK):
    C, D = conv.shape[1], seq.shape[1]
    g = count // T
    own = lambda w: rows_back(T, w, g - 1)
    packed = SHAPE((C, D + 2 * LANES), bf16 if final else f32)
    return pl.pallas_call(
        functools.partial(conv_bwd_kernel, T=T, g=g, final=final),
        grid=(g,),
        in_specs=[
            own(C), own(LANES), whole(selw.shape), own(C), own(C), own(C), whole(w_in.shape),
            rows_back(T, D, at // T + g - 1), whole(chan.shape), whole(later.shape),
            own(C), own(C), own(LANES), whole(before.shape), whole(gch.shape), whole(tail.shape),
        ],
        out_specs=[own(D), whole((8, D)), whole((8, C)), whole((8, C)), whole(packed.shape)],
        out_shape=[SHAPE((count, D), bf16), SHAPE((8, D), f32), SHAPE((8, C), f32), SHAPE((8, C), f32), packed],
        scratch_shapes=[pltpu.VMEM((T + 8, C), f32), pltpu.VMEM(packed.shape, f32)],
        compiler_params=params(56),
        cost_estimate=cost(),
    )(dact, dsel, selw, pre, conv, dgate, w_in, seq, chan, later, actb, ddl, rank, before, gch, tail)


def as_column(row, count):
    return jnp.broadcast_to(row[0:1, :], (LANES, count)).T[:, 0:1]


def as_rows(column, count):
    return jnp.broadcast_to(column, (count, LANES)).T[0:8, :]


def experts_kernel(x_ref, cot_ref, prob_ref, w_ref, out_ref, drow_ref, dot_ref, g_ref, acc_out, acc_row, dz_ref, *, steps, per, units):
    R = x_ref.shape[0]

    @pl.when(pl.program_id(0) == 0)
    def _():
        acc_out[...] = jnp.zeros_like(acc_out)
        acc_row[...] = jnp.zeros_like(acc_row)
        dz_ref[...] = (as_column(prob_ref[...], R) * cot_ref[...].astype(f32)).astype(bf16)

    x, dz = x_ref[...], dz_ref[...]
    up = jnp.concatenate([w_ref[2 * r * units : (2 * r + 1) * units, :] for r in range(per)], axis=0)
    down = jnp.concatenate([w_ref[(2 * r + 1) * units : (2 * r + 2) * units, :] for r in range(per)], axis=0)
    lin = dotf(x, up, ((1,), (1,)))
    cdf = 0.5 * (1.0 + lax.erf(lin * math.sqrt(0.5)))
    act = (lin * cdf).astype(bf16)
    slope = cdf + lin * jnp.exp(-0.5 * lin * lin) * (1.0 / math.sqrt(2.0 * math.pi))
    acc_out[...] += dotf(act, down)
    dlin = (dotf(dz, down, ((1,), (1,))) * slope).astype(bf16)
    acc_row[...] += dotf(dlin, up)
    gdown = dotf(act, dz, ((0,), (0,))).astype(bf16)
    gup = dotf(dlin, x, ((0,), (0,))).astype(bf16)
    for r in range(per):
        g_ref[2 * r * units : (2 * r + 1) * units, :] = gup[r * units : (r + 1) * units]
        g_ref[(2 * r + 1) * units : (2 * r + 2) * units, :] = gdown[r * units : (r + 1) * units]

    @pl.when(pl.program_id(0) == steps - 1)
    def _():
        out = acc_out[...].astype(bf16)
        out_ref[...] = out
        drow_ref[...] = acc_row[...].astype(bf16)
        dot_ref[...] = as_rows(jnp.sum(out.astype(f32) * dz.astype(f32), axis=1, keepdims=True), R)


def experts(x, cot, prob, w, units, per=2):
    R, D = x.shape
    block = 2 * units * per
    steps = w.shape[0] // block
    fix = whole((R, D))
    mov = rows_at(block, D)
    return pl.pallas_call(
        functools.partial(experts_kernel, steps=steps, per=per, units=units),
        grid=(steps,),
        in_specs=[fix, fix, whole(prob.shape), mov],
        out_specs=[fix, fix, whole((8, R)), mov],
        out_shape=[SHAPE((R, D), bf16)] * 2 + [SHAPE((8, R), f32), SHAPE(w.shape, bf16)],
        scratch_shapes=[pltpu.VMEM((R, D), f32)] * 2 + [pltpu.VMEM((R, D), bf16)],
        compiler_params=params(60),
        cost_estimate=cost(),
    )(x, cot, prob, w)


def mean_scale(values):
    return lax.rsqrt(jnp.mean(values * values, axis=-1, keepdims=True) + EPSILON)


def dot32(a, b, dims):
    return lax.dot_general(a, b, (dims, ((), ())), precision=HIGHEST, preferred_element_type=f32)


def route_kernel(src_ref, near_ref, far_ref, gain_ref, router_ref, ids_ref, row_ref, col_ref, res_ref, prob_ref, gate_ref, out_ref, slotp_ref, *, count):
    res = src_ref[...].astype(f32) + near_ref[...] + far_ref[...].astype(f32)
    res_ref[...] = res
    normed = res * mean_scale(res) * gain_ref[1:2, :]
    T, S = res.shape[0], out_ref.shape[0]
    logits = dot32(normed, router_ref[...], ((1,), (0,)))
    lane = lax.broadcasted_iota(jnp.int32, (T, LANES), 1)
    logits = jnp.where(lane < count, logits, -jnp.inf)
    e = jnp.exp(logits - jnp.max(logits, axis=1, keepdims=True))
    probs = e / jnp.sum(e, axis=1, keepdims=True)
    prob_ref[...] = probs
    gate = jnp.sum(jnp.where(lane == ids_ref[...], probs, 0.0), axis=1, keepdims=True)
    gate_ref[...] = jnp.broadcast_to(gate, (T, LANES))
    take = (lax.broadcasted_iota(jnp.int32, (S, T), 0) == row_ref[...]).astype(bf16)
    out_ref[...] = dotf(take, normed.astype(bf16)).astype(bf16)
    put = lax.broadcasted_iota(jnp.int32, (T, S), 1) == col_ref[...]
    slotp_ref[...] = jnp.broadcast_to(jnp.sum(jnp.where(put, gate, 0.0), axis=0, keepdims=True), (8, S))


def route_tokens(source, near, far, gains, router, ids, row, col, slots, count):
    T, D = source.shape
    return pl.pallas_call(
        functools.partial(route_kernel, count=count),
        out_shape=[SHAPE((T, D), f32), SHAPE((T, LANES), f32), SHAPE((T, LANES), f32), SHAPE((slots, D), bf16), SHAPE((8, slots), f32)],
        compiler_params=params(48),
        cost_estimate=cost(),
    )(source, near, far, gains, router, ids, row, col)


def back_kernel(rows_ref, dot_ref, col_ref, ids_ref, prob_ref, router_ref, res_ref, cot_ref, gain_ref, dres_ref, dmix_ref, part_ref, *, count):
    res = res_ref[...]
    T, S = res.shape[0], rows_ref.shape[0]
    put = lax.broadcasted_iota(jnp.int32, (T, S), 1) == col_ref[...]
    lane = lax.broadcasted_iota(jnp.int32, (T, LANES), 1)
    weighted = jnp.sum(jnp.where(put, dot_ref[0:1, :], 0.0), axis=1, keepdims=True)
    dlog = weighted * (jnp.where(lane == ids_ref[...], 1.0, 0.0) - prob_ref[...])
    dnorm = dotf(put.astype(bf16), rows_ref[...]) + dot32(dlog, router_ref[...], ((1,), (1,)))
    scale = mean_scale(res)
    hat = res * scale
    part_ref[0:8, :] = jnp.broadcast_to(jnp.sum(dnorm * hat, axis=0, keepdims=True), (8, res.shape[1]))
    part_ref[8:, :] = dot32(dlog, hat * gain_ref[1:2, :], ((0,), (0,)))[0 : part_ref.shape[0] - 8]
    a = gain_ref[1:2, :] * dnorm
    dres = cot_ref[...].astype(f32) + scale * (a - hat * jnp.mean(a * hat, axis=-1, keepdims=True))
    dres_ref[...] = dres
    dmix_ref[...] = dres.astype(bf16)


def back_tokens(rows, dots, col, ids, probs, router, res, cot, gains, count):
    T, D = res.shape
    return pl.pallas_call(
        functools.partial(back_kernel, count=count),
        out_shape=[SHAPE((T, D), f32), SHAPE((T, D), bf16), SHAPE((16, D), f32)],
        compiler_params=params(48),
        cost_estimate=cost(),
    )(rows, dots, col, ids, probs, router, res, cot, gains)


def step_of(refs, outs, grad, rate, factor, at=Ellipsis):
    weight, velocity, average = (ref[at] for ref in refs)
    g = grad * factor
    momentum = MOMENT * velocity + g
    new = weight - rate * (g + MOMENT * momentum)
    outs[0][at] = new
    outs[1][at] = momentum
    outs[2][at] = SMOOTH * average + (1.0 - SMOOTH) * new
    outs[3][at] = new.astype(bf16)


def upright(a, rows, columns):
    a = a.astype(f32)
    short = -a.shape[0] % LANES
    if short:
        a = jnp.concatenate([a, jnp.zeros((short, a.shape[1]), f32)], axis=0)
    return a.T[0:rows, 0:columns]


def mixer_step_kernel(*refs, factor, own, width, xw, vrows):
    conv_ref, early_ref = refs[:2]
    ins = [refs[2 + 3 * p : 5 + 3 * p] for p in range(5)]
    outs = [refs[17 + 4 * p : 21 + 4 * p] for p in range(5)]
    inward, select, delta, channel, outward = range(5)
    step_of(ins[inward], outs[inward], conv_ref[0:own, 0:width].astype(f32), LEARNING[0], factor, 0)
    step_of(ins[inward], outs[inward], early_ref[0:own, 0:width].astype(f32), LEARNING[0], factor, 1)
    at = width
    step_of(ins[select], outs[select], conv_ref[0:own, at : at + LANES].astype(f32)[:, 0:xw], LEARNING[1], factor)
    rest = upright(conv_ref[:, at + LANES : at + 2 * LANES], LANES, own)
    step_of(ins[delta], outs[delta], rest[0:DT_RANK], LEARNING[2], factor)
    step_of(ins[channel], outs[channel], rest[DT_RANK : DT_RANK + vrows], LEARNING[3], factor)
    step_of(ins[outward], outs[outward], early_ref[0:own, width:].astype(f32), LEARNING[4], factor)


def mixer_step(conv, early, triples, factor):
    own, width = triples[4][0].shape
    xw, vrows = triples[1][0].shape[1], triples[3][0].shape[0]
    shapes = []
    for triple in triples:
        shapes += [SHAPE(triple[0].shape, f32)] * 3 + [SHAPE(triple[0].shape, bf16)]
    flat = pl.pallas_call(
        functools.partial(mixer_step_kernel, factor=factor, own=own, width=width, xw=xw, vrows=vrows),
        out_shape=shapes,
        compiler_params=params(56),
        cost_estimate=cost(),
    )(conv, early, *[a for triple in triples for a in triple])
    return [flat[4 * p : 4 * p + 4] for p in range(5)]


def experts_step_kernel(gup_ref, gdown_ref, *refs, factor):
    ups, downs = refs[0:3], refs[3:6]
    rows, columns = ups[0].shape[1:]
    step_of(ups, refs[6:10], upright(gup_ref[...], rows, columns), LEARNING[5], factor, 0)
    step_of(downs, refs[10:14], gdown_ref[...].astype(f32), LEARNING[6], factor, 0)


def experts_step(grads, ups, downs, factor):
    _, D, units = ups[0].shape
    block = LANES if units % LANES == 0 else units
    n = units // block
    up = pl.BlockSpec((1, D, block), lambda i: (0, 0, i))
    down = pl.BlockSpec((1, block, D), lambda i: (0, i, 0))
    shapes = lambda a: [SHAPE(a.shape, f32)] * 3 + [SHAPE(a.shape, bf16)]
    flat = pl.pallas_call(
        functools.partial(experts_step_kernel, factor=factor),
        grid=(n,),
        in_specs=[rows_at(block, D), rows_at(block, D, n)] + [up] * 3 + [down] * 3,
        out_specs=[up] * 4 + [down] * 4,
        out_shape=shapes(ups[0]) + shapes(downs[0]),
        compiler_params=params(48),
        cost_estimate=cost(),
    )(grads, grads, *ups, *downs)
    return flat[:4], flat[4:]


def contract_rows(left, right):
    return dotf(left, right, ((0,), (0,)))


def tie(*values):
    return lax.optimization_barrier(values)


def ring_order(n):
    return list(range(0, n, 2)) + list(range(n - 1, 0, -2))


def ring_gather(ahead_part, back_part, axis):
    n = lax.axis_size(axis)
    order = ring_order(n)
    ahead = [(order[i], order[(i + 1) % n]) for i in range(n)]
    back = [(b, a) for a, b in ahead]
    first, second = [ahead_part], [back_part]
    for _ in range(n - 1):
        first.append(lax.ppermute(first[-1], axis, ahead))
        second.append(lax.ppermute(second[-1], axis, back))
    place = [order.index(i) for i in range(n)]
    owners = jnp.array([[order[(place[i] - r) % n] for r in range(n)] for i in range(n)], jnp.int32)
    return owners[lax.axis_index(axis)], first, [second[-r % n] for r in range(n)]


def halving_sum(value, axis, fills=()):
    n = lax.axis_size(axis)
    me = lax.axis_index(axis)
    bit, out = 1, []
    rows = value.shape[1:]
    value = value.reshape((n,) + rows)
    while bit < n:
        mine = (me // bit) % 2
        pairs = value.reshape((value.shape[0] // 2, 2) + rows)
        keep = lax.dynamic_index_in_dim(pairs, mine, 1, keepdims=False)
        send = lax.dynamic_index_in_dim(pairs, 1 - mine, 1, keepdims=False)
        got = lax.ppermute(send, axis, [(i, i ^ bit) for i in range(n)])
        if fills:
            keep, *done = tie(keep, *fills[0]())
            fills, out = fills[1:], out + [done]
        value = (keep.astype(f32) + got.astype(f32)).astype(bf16)
        bit *= 2
    return value[0], out + [fill() for fill in fills]


def swap(value, j):
    n = lax.axis_size("mp")
    return lax.ppermute(value, "mp", [(i, i ^ j) for i in range(n)])


def gather_mp(rows):
    me, n = lax.axis_index("mp"), lax.axis_size("mp")
    near = swap(rows, 1)
    across = swap(rows, 2)
    total = jnp.zeros((n,) + rows.shape, rows.dtype)
    for j, block in enumerate([rows, near, across, swap(across, 1)]):
        total = lax.dynamic_update_index_in_dim(total, block, me ^ j, 0)
    return total.reshape(n * rows.shape[0], rows.shape[1])


def sum_mp(value):
    value = value + swap(value, 1)
    return value + swap(value, 2)


def scatter_mp(halves):
    me = lax.axis_index("mp")

    def pick(j):
        k = (me ^ j) % 2
        one = lax.dynamic_index_in_dim(halves[0], k, 0, keepdims=False)
        two = lax.dynamic_index_in_dim(halves[1], k, 0, keepdims=False)
        return jnp.where((me ^ j) < 2, one, two)

    near = swap(jnp.stack([pick(3), pick(1)]), 1).astype(f32)
    far = (pick(2).astype(f32) + near[0]).astype(bf16)
    return pick(0).astype(f32) + near[1], swap(far, 2)


def butterfly(value):
    for j in (1, 2):
        value = value + swap(value, j)
    n = lax.axis_size("dp")
    step = 1
    while step < n:
        value = value + lax.ppermute(value, "dp", [(i, i ^ step) for i in range(n)])
        step *= 2
    return value


def nesterov(weight, velocity, average, step_grad, rate):
    momentum = MOMENT * velocity + step_grad
    new_weight = weight - rate * (step_grad + MOMENT * momentum)
    smoothed = SMOOTH * average + (1.0 - SMOOTH) * new_weight
    return [new_weight, momentum, smoothed, new_weight.astype(jnp.bfloat16)]


def body(
    block_input, cotangent, expert_ids, slot_ids,
    inward_proj, select_proj, delta_proj, channel_params, outward_proj, expert_up, expert_down, norm_gains, router_weight,
    inward_velocity, select_velocity, delta_velocity, channel_velocity, outward_velocity, upward_velocity,
    downward_velocity, gains_velocity, router_velocity,
    inward_average, select_average, delta_average, channel_average, outward_average, upward_average,
    downward_average, gains_average, router_average,
):
    tok_rows, width = block_input.shape
    ring, peers = lax.axis_size("dp"), lax.axis_size("mp")
    me = lax.axis_index("mp")
    own = inward_proj.shape[2]
    slot = -(-own // 16) * 16
    wide = -(-slot * ring // LANES) * LANES
    experts_all = router_weight.shape[1]
    slots = peers * CAP

    half = 5 * LANES
    owners, mix_a, mix_b = ring_gather(
        *prep(jnp.swapaxes(inward_proj, 1, 2), select_proj, delta_proj, channel_params, outward_proj, half), "dp"
    )
    units = expert_down.shape[1]
    mix_a[3], mix_b[-3], up_own = tie(mix_a[3], mix_b[-3], expert_up[0])
    expert_w = lax.all_gather(prep_experts(up_own, expert_down[0]), "dp", axis=0, tiled=True)
    w_in, selw, delta_w, chan, out_w = mixer_weights(owners, mix_a, mix_b, slot, wide, width, half)

    slot_index = (expert_ids ^ me) * CAP + slot_ids
    slot_row, slot_col, ids_col = slot_index[None, :], slot_index[:, None], expert_ids[:, None]
    dispatch = (lax.broadcasted_iota(jnp.int32, (slots, tok_rows), 0) == slot_row).astype(bf16)
    router_pad = jnp.pad(router_weight, ((0, 0), (0, LANES - experts_all)))

    def exchange(blocks):
        parts = blocks.reshape(peers, CAP, -1)
        return jnp.concatenate([parts[0]] + [swap(parts[j], j) for j in range(1, peers)])

    def exchange_row(rows):
        parts = rows[0].reshape(peers, CAP)
        row = jnp.concatenate([parts[0]] + [swap(parts[j], j) for j in range(1, peers)])
        return jnp.broadcast_to(row[None], (8, slots))

    source = block_input.astype(f32)
    scale1 = mean_scale(source)
    normed_b = (source * scale1 * norm_gains[0]).astype(bf16)
    seq = gather_mp(normed_b)
    cot_out = jnp.dot(dispatch, cotangent, preferred_element_type=f32).astype(bf16)
    cot_out, seq = tie(cot_out, seq)
    cot_rows = exchange(cot_out)

    count = seq.shape[0] // 2
    conv_tail, state = jnp.zeros((8, wide), f32), jnp.zeros((NST, wide), f32)
    convs, scans, selections = [], [], []
    for h in range(2):
        convs.append(conv_fwd(seq, h * count, count, w_in, chan, selw, conv_tail))
        conv_tail = convs[-1][6]
        selections.append(sum_mp(convs[-1][5]))
    edges = [state]
    for h in range(2):
        conv_in, gate_in, pre, act, act_b, _, _ = convs[h]
        scans.append(scan_fwd(selections[h], delta_w, act, gate_in, chan, out_w, state))
        state = scans[-1][6]
        edges.append(state)
    near, far = scatter_mp([s[4].reshape(2, tok_rows, width) for s in scans])
    residual, probs, gate_prob, outgoing, prob_slots = route_tokens(
        block_input, near, far, norm_gains, router_pad, ids_col, slot_row, slot_col, slots, experts_all
    )
    arrived = exchange(outgoing)
    expert_out, d_rows, dots, grad_experts = experts(arrived, cot_rows, exchange_row(prob_slots), expert_w, units)
    experts_grad = lax.psum_scatter(grad_experts, "dp", scatter_dimension=0, tiled=True)

    d_residual, d_mixer, parts = back_tokens(
        exchange(d_rows), exchange_row(dots), slot_col, ids_col, probs, router_pad, residual, cotangent, norm_gains,
        experts_all,
    )
    portion = gather_mp(d_mixer)
    expert_out, portion = tie(expert_out, portion)
    returned = exchange(expert_out)

    def both(left, right):
        return contract_rows(left[0], right[:count]) + contract_rows(left[1], right[count:])

    def cut(a):
        return a[: slot * ring]

    out_grad = both([s[3] for s in scans], portion).astype(bf16)
    q, later = jnp.zeros((NST, wide), f32), jnp.zeros((8, wide), f32)
    tails, sums = [None] * 2, [None] * 2
    for h in (1, 0):
        kept = scans[h][0], convs[h][3], convs[h][1], scans[h][1], scans[h][2]
        tails[h] = scan_bwd(portion, h * count, 0, kept, edges[h], q, count, out_w, selections[h], chan, delta_w)
        q = tails[h][5]
        sums[h] = sum_mp(tails[h][3])
    gate_grad = both([t[0] for t in tails], seq).astype(bf16)
    early = jnp.concatenate([cut(gate_grad), cut(out_grad)], axis=1)
    early, experts_grad = tie(early, experts_grad)
    early = lax.psum_scatter(early, "dp", scatter_dimension=0, tiled=True)
    grads, gch = jnp.zeros((wide, width + 2 * LANES), f32), jnp.zeros((8, wide), f32)
    tail_sum = tails[0][4] + tails[1][4]
    dnorms, gains = [None] * 2, [None] * 2
    for h in (1, 0):
        dnorms[h], gains[h], later, gch, grads = conv_bwd(
            h * count, count, h == 0, tails[h][1], sums[h], selw, convs[h][2], convs[h][0], tails[h][0], w_in, seq,
            chan, later, convs[h][4], tails[h][2], scans[h][5], grads, gch, tail_sum,
        )
    near, far = scatter_mp([d.reshape(2, tok_rows, width) for d in dnorms])
    factor = 1.0 / math.sqrt(tok_rows * ring * peers)
    gain_part = (gains[0][:1] + gains[1][:1]) / norm_gains[:1]
    small = jnp.concatenate([gain_part, parts[:1], parts[8 : 8 + experts_all]])

    def expert_update():
        up_new, down_new = experts_step(
            experts_grad,
            (expert_up, upward_velocity, upward_average),
            (expert_down, downward_velocity, downward_average),
            factor,
        )
        return list(up_new) + list(down_new)

    def token_results():
        d_normed = near + far.astype(f32)
        a1 = norm_gains[0] * d_normed
        hat1 = source * scale1
        block_grad = d_residual + scale1 * (a1 - hat1 * jnp.mean(a1 * hat1, axis=-1, keepdims=True))
        tokens_out = contract_rows(dispatch, returned)
        return (residual + gate_prob[:, :1] * tokens_out).astype(bf16), block_grad

    conv_grad, filled = halving_sum(
        cut(grads).reshape(ring, slot, -1), "dp", [expert_update, token_results, lambda: [butterfly(small)]]
    )
    expert_new, (block_output, block_grad), (shared,) = filled[:3]
    mixer_new = mixer_step(
        conv_grad,
        early,
        (
            tuple(jnp.swapaxes(a, 1, 2) for a in (inward_proj, inward_velocity, inward_average)),
            (select_proj, select_velocity, select_average),
            (delta_proj, delta_velocity, delta_average),
            (channel_params, channel_velocity, channel_average),
            (outward_proj, outward_velocity, outward_average),
        ),
        factor,
    )
    results = [block_output, block_grad]
    mixer_new[0] = [jnp.swapaxes(a, 1, 2) for a in mixer_new[0]]
    for new in mixer_new:
        results.extend(new)
    results.extend(expert_new)
    results.extend(nesterov(norm_gains, gains_velocity, gains_average, shared[:2] * factor, LEARNING[7]))
    results.extend(nesterov(router_weight, router_velocity, router_average, shared[2:].T * factor, LEARNING[8]))
    return tuple(results)


def solution(mesh):
    in_specs = (
        P(("dp", "mp"), None),
        P(("dp", "mp"), None),
        P(("dp", "mp")),
        P(("dp", "mp")),
        P(None, None, ("dp", "mp")),
        P(("dp", "mp"), None),
        P(None, ("dp", "mp")),
        P(None, ("dp", "mp")),
        P(("dp", "mp"), None),
        P("mp", None, "dp"),
        P("mp", "dp", None),
        P(),
        P(),
        P(None, None, ("dp", "mp")),
        P(("dp", "mp"), None),
        P(None, ("dp", "mp")),
        P(None, ("dp", "mp")),
        P(("dp", "mp"), None),
        P("mp", None, "dp"),
        P("mp", "dp", None),
        P(),
        P(),
        P(None, None, ("dp", "mp")),
        P(("dp", "mp"), None),
        P(None, ("dp", "mp")),
        P(None, ("dp", "mp")),
        P(("dp", "mp"), None),
        P("mp", None, "dp"),
        P("mp", "dp", None),
        P(),
        P(),
    )
    out_specs = (
        P(("dp", "mp"), None),
        P(("dp", "mp"), None),
        P(None, None, ("dp", "mp")),
        P(None, None, ("dp", "mp")),
        P(None, None, ("dp", "mp")),
        P(None, None, ("dp", "mp")),
        P(("dp", "mp"), None),
        P(("dp", "mp"), None),
        P(("dp", "mp"), None),
        P(("dp", "mp"), None),
        P(None, ("dp", "mp")),
        P(None, ("dp", "mp")),
        P(None, ("dp", "mp")),
        P(None, ("dp", "mp")),
        P(None, ("dp", "mp")),
        P(None, ("dp", "mp")),
        P(None, ("dp", "mp")),
        P(None, ("dp", "mp")),
        P(("dp", "mp"), None),
        P(("dp", "mp"), None),
        P(("dp", "mp"), None),
        P(("dp", "mp"), None),
        P("mp", None, "dp"),
        P("mp", None, "dp"),
        P("mp", None, "dp"),
        P("mp", None, "dp"),
        P("mp", "dp", None),
        P("mp", "dp", None),
        P("mp", "dp", None),
        P("mp", "dp", None),
        P(),
        P(),
        P(),
        P(),
        P(),
        P(),
        P(),
        P(),
    )
    return jax.shard_map(body, mesh=mesh, in_specs=in_specs, out_specs=out_specs, check_vma=False)
```

time: 2630 us -> 691 us (0.26)
  matrix products: 633 us -> 17.3 us
  other arithmetic: 626 us -> 37.1 us
  waiting for transfers between devices: 768 us -> 233 us
  local copies, waits for them, and re-layouts: 359 us -> 48.4 us
  Pallas kernels: 0 us -> 267 us
  blocking collectives: 172 us -> 0 us
  starting transfers between devices: 16.6 us -> 67.6 us
    dot_general x48 -> x6, matrix products: 633 us -> 17.3 us  [the longest x5 14.9 us: dotf(): return lax.dot_general(a, b, (dims, ((), ())), preferred_element_type=f32)]
    pallas_call x0 -> x16, Pallas kernels: none -> 267 us  [the longest x2 91.6 us: scan_bwd(): pl.pallas_call(functools.partial(scan_bwd_kernel, T=T, g=g, opens=low ==...]
    all_gather x6 -> x1, waiting for transfers between devices: 248 us -> 0.01 us  [body(): lax.all_gather(prep_experts(up_own, expert_down[0]), 'dp', axis=0, tiled=...]
    unnamed x21 -> x3, waiting for transfers between devices: 218 us -> 0.05 us
    reduce_scatter x3 -> x2, waiting for transfers between devices: 238 us -> 20.6 us  [the longest x1 20.6 us: body(): early = lax.psum_scatter(early, 'dp', scatter_dimension=0, tiled=True)]
    ppermute x0 -> x58, waiting for transfers between devices: none -> 213 us  [the longest x38 132 us: swap(): return lax.ppermute(value, 'mp', [(i, i ^ j) for i in range(n)])]
    reduce_sum x23 -> x2, other arithmetic: 186 us -> 2.5 us  [the longest x1 2.2 us: token_results(): jnp.mean(a1 * hat1, axis=-1, keepdims=True)]
    add_any x152 -> x0, other arithmetic: 104 us -> none  [the longest x128 103 us: sub_step(): return (decay_end * start_state + local_end, start_state)]
  transfers between devices with their start and end apart: 20 -> 61, of which waited for: 13 -> 32; matrix products, arithmetic and copies ran while one was open for 19% -> 11% of each run, Pallas kernels for 0% -> 31%
where the time goes in v2:
time: 691 us; the launch traced here: 686 us
  Pallas kernels  267 us (39%)
  waiting for transfers between devices  233 us (34%)
  starting transfers between devices  67.6 us (10%)
  local copies, waits for them, and re-layouts  48.4 us (7%)
  other arithmetic  37.1 us (5%)
  matrix products  17.3 us (3%)
  between operations  15.2 us (2%)
    ppermute x38, waiting for transfers between devices, swap(): return lax.ppermute(value, 'mp', [(i, i ^ j) for i in range(n)])  132 us
    pallas_call x2, Pallas kernels, scan_bwd(): pl.pallas_call(functools.partial(scan_bwd_kernel, T=T, g=g, opens=low ==...  91.6 us
    pallas_call x1, Pallas kernels, experts(): pl.pallas_call(functools.partial(experts_kernel, steps=steps, per=per, un...  48.4 us
    pallas_call x2, Pallas kernels, scan_fwd(): pl.pallas_call(functools.partial(scan_fwd_kernel, T=T), grid=(g,), in_spe...  40.1 us
    pallas_call x2, Pallas kernels, conv_bwd(): pl.pallas_call(functools.partial(conv_bwd_kernel, T=T, g=g, final=final),...  38 us
    ppermute x7, waiting for transfers between devices, ring_gather(): second.append(lax.ppermute(second[-1], axis, back))  30.2 us
    ppermute x7, waiting for transfers between devices, ring_gather(): first.append(lax.ppermute(first[-1], axis, ahead))  28.1 us
    unnamed x197, local copies, waits for them, and re-layouts  25.1 us
  transfers between devices with their start and end apart: 61, of which 32 were waited for; matrix products, arithmetic and copies ran while one was open for 11% of the time, Pallas kernels for 31%

profile of v2, /device:TPU:0, one launch (start us, length us, event | category | flops | bytes accessed | tf_op | source)
XLA Modules:
  0.0 685.5 jit_solution(17508789829549483367)
XLA Ops:
  11.7 3.0 collective-permute-start.6
  15.5 5.8 collective-permute-done.6.refs_15_
  24.8 4.4 collective-permute-done.7.refs_14_
  31.9 5.6 collective-permute-done.5.refs_3_
  50.7 12.4 %collective-permute-done.9.refs_4_ = bf16[72,1792]{1,0:T(8,128)(2,1)S(1)} collective-permute-done((bf16[72,1792]{1,0:T(8,128)(2,1)S(1)}, bf16[72,1792]{1,0:T(8,128)(2,1)S(1)}, u32[]{:S(2)}, u32[]{:S(2)}) %collective-permute-start.9) | collective-permute-done | bytes 258080 | tf_op jit(solution)/shard_map/ppermute | solution.py:745
  63.9 3.4 collective-permute-start.14
  72.8 5.5 collective-permute-done.10.refs_5_
  78.4 3.1 collective-permute-start.11
  81.5 3.5 collective-permute-done.14.refs_11_
  85.0 3.5 collective-permute-start.15
  92.7 9.8 %collective-permute-start.12 = (bf16[72,1792]{1,0:T(8,128)(2,1)S(1)}, bf16[72,1792]{1,0:T(8,128)(2,1)S(1)}, u32[]{:S(2)}, u32[]{:S(2)}) collective-permute-start(bf16[72,1792]{1,0:T(8,128)(2,1)S(1)} %collective-permute-done.11.refs_6_), channel_id=1, source_target_pairs={{0,8},{8,16},{16,24},{24,28},{28,20},{20,12},{12,4},{4,0},{1,9},{9... | collective-permute-start | bytes 774152 | tf_op jit(solution)/shard_map/ppermute | solution.py:745
  102.6 3.2 collective-permute-done.15.refs_10_
  110.8 2.9 collective-permute-done.12.refs_7_
  113.7 12.6 %collective-permute-done.16.refs_9_ = bf16[72,1920]{1,0:T(8,128)(2,1)S(1)} collective-permute-done((bf16[72,1920]{1,0:T(8,128)(2,1)S(1)}, bf16[72,1920]{1,0:T(8,128)(2,1)S(1)}, u32[]{:S(2)}, u32[]{:S(2)}) %collective-permute-start.16) | collective-permute-done | bytes 276512 | tf_op jit(solution)/shard_map/ppermute | solution.py:746
  128.3 2.8 shard_map.600
  132.4 9.1 %shard_map.601 = (f32[1024,640]{1,0:T(8,128)S(1)}, f32[1024,640]{1,0:T(8,128)}, f32[1024,640]{1,0:T(8,128)}, f32[1024,640]{1,0:T(8,128)}, bf16[1024,640]{1,0:T(8...) custom-call(bf16[2048,1152]{1,0:T(8,128)(2,1)} %bitcast.4.seq_ref, ...), custom_call_target="tpu_custom_call" | custom-call | bytes 1048576 | tf_op jit(solution)/shard_map/pallas_call | solution.py:218
  144.0 9.0 %shard_map.603 = (f32[1024,640]{1,0:T(8,128)S(1)}, f32[1024,640]{1,0:T(8,128)}, f32[1024,640]{1,0:T(8,128)}, f32[1024,640]{1,0:T(8,128)}, bf16[1024,640]{1,0:T(8...) custom-call(bf16[2048,1152]{1,0:T(8,128)(2,1)} %bitcast.4.seq_ref, ...), custom_call_target="tpu_custom_call" | custom-call | bytes 1048576 | tf_op jit(solution)/shard_map/pallas_call | solution.py:218
  159.1 12.0 %collective-permute-done.18 = f32[1024,128]{1,0:T(8,128)} collective-permute-done((f32[1024,128]{1,0:T(8,128)S(1)}, f32[1024,128]{1,0:T(8,128)}, u32[]{:S(2)}, u32[]{:S(2)}) %collective-permute-start.18) | collective-permute-done | bytes 524320 | tf_op jit(solution)/shard_map/ppermute | solution.py:774
  172.4 19.9 %shard_map.602 = (bf16[64,256,640]{2,1,0:T(8,128)(2,1)}, f32[1024,640]{1,0:T(8,128)}, f32[1024,640]{1,0:T(8,128)}, bf16[1024,640]{1,0:T(8,128)(2,1)S(1)}, bf16[1...) custom-call(f32[1024,128]{1,0:T(8,128)S(1)} %add.233.sel_ref, ...), custom_call_target="tpu_custom_call" | custom-call | bytes 1048576 | tf_op jit(solution)/shard_map/pallas_call | solution.py:288
  194.8 20.2 %shard_map.604 = (bf16[64,256,640]{2,1,0:T(8,128)(2,1)}, f32[1024,640]{1,0:T(8,128)}, f32[1024,640]{1,0:T(8,128)}, bf16[1024,640]{1,0:T(8,128)(2,1)S(1)}, bf16[1...) custom-call(f32[1024,128]{1,0:T(8,128)S(1)} %add.237.sel_ref, ...), custom_call_target="tpu_custom_call" | custom-call | bytes 1048576 | tf_op jit(solution)/shard_map/pallas_call | solution.py:288
  219.3 4.7 collective-permute-done.21
  233.2 22.7 %collective-permute-done.22.far_ref = bf16[512,1152]{1,0:T(8,128)(2,1)S(1)} collective-permute-done((bf16[512,1152]{1,0:T(8,128)(2,1)}, bf16[512,1152]{1,0:T(8,128)(2,1)S(1)}, u32[]{:S(2)}, u32[]{:S(2)}) %collective-permute-start.22) | collective-permute-done | bytes 1179680 | tf_op jit(solution)/shard_map/ppermute | solution.py:774
  255.9 5.5 shard_map.605
  265.4 7.9 %collective-permute-done.28 = bf16[192,1152]{1,0:T(8,128)(2,1)S(1)} collective-permute-done((bf16[192,1152]{1,0:T(8,128)(2,1)S(1)}, bf16[192,1152]{1,0:T(8,128)(2,1)S(1)}, u32[]{:S(2)}, u32[]{:S(2)}) %collective-permute-start.28) | collective-permute-done | bytes 442400 | tf_op jit(solution)/shard_map/ppermute | solution.py:774
  277.4 15.7 %collective-permute-done.30 = f32[192]{0:T(256)S(1)} collective-permute-done((f32[192]{0:T(256)S(1)}, f32[192]{0:T(256)S(1)}, u32[]{:S(2)}, u32[]{:S(2)}) %collective-permute-start.30) | collective-permute-done | bytes 800 | tf_op jit(solution)/shard_map/ppermute | solution.py:774
  295.1 48.4 %shard_map.607 = (bf16[768,1152]{1,0:T(8,128)(2,1)}, bf16[768,1152]{1,0:T(8,128)(2,1)}, f32[8,768]{1,0:T(8,128)}, bf16[6144,1152]{1,0:T(8,128)(2,1)}) custom-call(bf16[768,1152]{1,0:T(8,128)(2,1)} %pad_maximum_fusion.3.x_ref, bf16[768,1152]{1,0:T(8,128)(2,1)} %pad_maximum_fusion.4.cot_ref, f32[8,768]{1,0:T(8,128)} %broadcast_in_dim.58.prob_ref, ...), custom_call_target="tpu_custom_call" | custom-call | bytes 1048576 | tf_op jit(solution)/shard_map/pallas_call | solution.py:574
  350.1 17.5 %collective-permute-done.36 = f32[192]{0:T(256)S(1)} collective-permute-done((f32[192]{0:T(256)S(1)}, f32[192]{0:T(256)S(1)}, u32[]{:S(2)}, u32[]{:S(2)}) %collective-permute-start.36) | collective-permute-done | bytes 800 | tf_op jit(solution)/shard_map/ppermute | solution.py:774
  367.9 7.9 %shard_map.608 = (f32[512,1152]{1,0:T(8,128)}, bf16[512,1152]{1,0:T(8,128)(2,1)S(1)}, f32[16,1152]{1,0:T(8,128)S(1)}) custom-call(bf16[768,1152]{1,0:T(8,128)(2,1)S(1)} %pad_maximum_fusion.5.rows_ref, f32[8,768]{1,0:T(8,128)S(1)} %broadcast_in_dim.59.dot_ref, s32[512,1]{1,0:T(8,128)S(1)} %copy.73.col_ref, s32[512,1]{1,0:T(8,128)S(1)} %copy.72.ids_ref, ...), custom_call_target="tpu_custom_call" | custom-call | bytes 1048576 | tf_op jit(solution)/shard_map/pallas_call | solution.py:643
  376.0 27.8 %collective-permute-done.39 = bf16[512,1152]{1,0:T(8,128)(2,1)S(1)} collective-permute-done((bf16[512,1152]{1,0:T(8,128)(2,1)S(1)}, bf16[512,1152]{1,0:T(8,128)(2,1)S(1)}, u32[]{:S(2)}, u32[]{:S(2)}) %collective-permute-start.39) | collective-permute-done | bytes 1179680 | tf_op jit(solution)/shard_map/ppermute | solution.py:774
  409.0 46.1 %shard_map.609 = (bf16[1024,640]{1,0:T(8,128)(2,1)}, f32[1024,640]{1,0:T(8,128)}, bf16[1024,640]{1,0:T(8,128)(2,1)}, bf16[1024,128]{1,0:T(8,128)(2,1)}, f32[24,640]{1,0:T(8,128)}, /*index=5*/f32[16,640]{1,0:T(8,128)}) custom-call(bf16[2048,1152]{1,0:T(8,128)(2,1)} %bitcast.92, bf16[640,1152]{1,0:T(8,128)(2,1)} %copy-done.1, ...), custom_call_target="tpu_custom_call" | custom-call | bytes 1048576 | tf_op jit(solution)/shard_map/pallas_call | solution.py:430
  455.3 45.6 %shard_map.610 = (bf16[1024,640]{1,0:T(8,128)(2,1)}, f32[1024,640]{1,0:T(8,128)}, bf16[1024,640]{1,0:T(8,128)(2,1)}, bf16[1024,128]{1,0:T(8,128)(2,1)}, f32[24,640]{1,0:T(8,128)}, /*index=5*/f32[16,640]{1,0:T(8,128)}) custom-call(bf16[2048,1152]{1,0:T(8,128)(2,1)} %bitcast.93, bf16[640,1152]{1,0:T(8,128)(2,1)} %copy-done.1, ...), custom_call_target="tpu_custom_call" | custom-call | bytes 1048576 | tf_op jit(solution)/shard_map/pallas_call | solution.py:430
  508.1 2.9 collective-permute-done.44
  513.8 19.6 %shard_map.611 = (bf16[1024,1152]{1,0:T(8,128)(2,1)}, f32[8,1152]{1,0:T(8,128)}, f32[8,640]{1,0:T(8,128)}, f32[8,640]{1,0:T(8,128)}, f32[640,1408]{1,0:T(8,128)}) custom-call(f32[1024,640]{1,0:T(8,128)} %get-tuple-element.196.dact_ref, bf16[1024,128]{1,0:T(8,128)(2,1)} %add.250.dsel_ref, bf16[640,128]{1,0:T(8,128)(2,1)} %copy-done.10, ...), custom_call_target="tpu_custom_call" | custom-call | bytes 1048576 | tf_op jit(solution)/shard_map/pallas_call | solution.py:511
  534.2 18.4 %shard_map.612 = (bf16[1024,1152]{1,0:T(8,128)(2,1)}, f32[8,1152]{1,0:T(8,128)}, f32[8,640]{1,0:T(8,128)}, f32[8,640]{1,0:T(8,128)}, bf16[640,1408]{1,0:T(8,128)(2,1)}) custom-call(f32[1024,640]{1,0:T(8,128)} %get-tuple-element.191.dact_ref, bf16[1024,128]{1,0:T(8,128)(2,1)} %add.248.dsel_ref, bf16[640,128]{1,0:T(8,128)(2,1)} %copy-done.10, ...), custom_call_target="tpu_custom_call" | custom-call | bytes 1048576 | tf_op jit(solution)/shard_map/pallas_call | solution.py:511
  555.9 3.6 fusion.20
  561.4 3.6 fusion
  575.3 7.8 %collective-permute-done.53 = f32[6,1152]{1,0:T(8,128)S(1)} collective-permute-done((f32[6,1152]{1,0:T(8,128)S(1)}, f32[6,1152]{1,0:T(8,128)S(1)}, u32[]{:S(2)}, u32[]{:S(2)}) %collective-permute-start.53) | collective-permute-done | bytes 27680 | tf_op jit(solution)/shard_map/ppermute | solution.py:774
  587.0 4.2 collective-permute-start.55
  595.2 4.6 collective-permute-start.56
  599.8 3.8 add_convert_fusion
  603.7 4.3 collective-permute-done.50
  610.3 8.4 %shard_map.613 = (f32[1,1152,384]{2,1,0:T(8,128)}, f32[1,1152,384]{2,1,0:T(8,128)}, f32[1,1152,384]{2,1,0:T(8,128)}, bf16[1,1152,384]{2,1,0:T(8,128)(2,1)}, f32[...) custom-call(bf16[768,1152]{1,0:T(8,128)(2,1)S(1)} %copy-done.2, ...), custom_call_target="tpu_custom_call" | custom-call | bytes 1048576 | tf_op jit(solution)/shard_map/pallas_call | solution.py:714
  620.4 3.2 collective-permute-start.51
  623.5 4.5 fusion.9
  628.0 12.2 %collective-permute-done.51 = bf16[2,80,1408]{2,1,0:T(8,128)(2,1)S(1)} collective-permute-done((bf16[2,80,1408]{2,1,0:T(8,128)(2,1)S(1)}, bf16[2,80,1408]{2,1,0:T(8,128)(2,1)S(1)}, u32[]{:S(2)}, u32[]{:S(2)}) %collective-permute-start.51) | collective-permute-done | bytes 450592 | tf_op jit(solution)/shard_map/ppermute | solution.py:763
  644.5 8.8 %collective-permute-done.57 = bf16[1,80,1408]{2,1,0:T(8,128)(2,1)S(1)} collective-permute-done((bf16[1,80,1408]{2,1,0:T(8,128)(2,1)S(1)}, bf16[1,80,1408]{2,1,0:T(8,128)(2,1)S(1)}, u32[]{:S(2)}, u32[]{:S(2)}) %collective-permute-start.57) | collective-permute-done | bytes 225312 | tf_op jit(solution)/shard_map/ppermute | solution.py:763
  654.1 20.6 %reduce-scatter.5.cloned.1.call-done.refs_1_ = bf16[80,2304]{1,0:T(8,128)(2,1)} async-done(((bf16[640,2304]{1,0:T(8,128)(2,1)}), bf16[80,2304]{1,0:T(8,128)(2,1)}) %reduce-scatter.5.cloned.1.call-update) | async-done | bytes 368656 | tf_op jit(solution)/shard_map/reduce_scatter | solution.py:918
  674.7 4.1 shard_map.614
  (373 shorter events, 134.1 us)
Async XLA Ops:
  7.2 287.3 %all-gather.2.cloned.1.call-start = ((), (), s32[]{:S(2)}) async-start(), calls=%async_computation.2 | async-start | bytes 15925248 | tf_op jit(solution)/shard_map/all_gather | solution.py:847
  11.7 9.7 %collective-permute-start.6 = (bf16[72,1920]{1,0:T(8,128)(2,1)S(1)}, bf16[72,1920]{1,0:T(8,128)(2,1)S(1)}, u32[]{:S(2)}, u32[]{:S(2)}) collective-permute-start(bf16[72,1920]{1,0:T(8,128)(2,1)S(1)} %get-tuple-element.155.refs_8_), channel_id=1, source_target_pairs={{8,0},{16,8},{24,16},{28,24},{20,28},{12,20},{4,12},{0,4},{9,1},{1... | collective-permute-start | bytes 829448 | tf_op jit(solution)/shard_map/ppermute | solution.py:746
  14.7 9.1 %collective-permute-start.3 = (bf16[72,1792]{1,0:T(8,128)(2,1)S(1)}, bf16[72,1792]{1,0:T(8,128)(2,1)S(1)}, u32[]{:S(2)}, u32[]{:S(2)}) collective-permute-start(bf16[72,1792]{1,0:T(8,128)(2,1)S(1)} %get-tuple-element.154.refs_0_), channel_id=1, source_target_pairs={{0,8},{8,16},{16,24},{24,28},{28,20},{20,12},{12,4},{4,0},{1,9},{9... | collective-permute-start | bytes 774152 | tf_op jit(solution)/shard_map/ppermute | solution.py:745
  42.3 548.9 %reduce-scatter.3.cloned.1.call-start = ((), (), s32[]{:S(2)}) async-start(), calls=%async_computation.3 | async-start | bytes 15925248 | tf_op jit(solution)/shard_map/reduce_scatter | solution.py:891
  47.0 25.1 %collective-permute-start.1 = (bf16[512,1152]{1,0:T(8,128)(2,1)}, bf16[512,1152]{1,0:T(8,128)(2,1)}, u32[]{:S(2)}, u32[]{:S(2)}) collective-permute-start(bf16[512,1152]{1,0:T(8,128)(2,1)} %get-tuple-element.275), channel_id=1, source_target_pairs={{0,2},{1,3},{2,0},{3,1},{4,6},{5,7},{6,4},{7,5},{8,10},{9,11},{10,... | collective-permute-start | bytes 3538952 | tf_op jit(solution)/shard_map/ppermute | solution.py:774
  48.6 39.9 %collective-permute-start = (bf16[512,1152]{1,0:T(8,128)(2,1)}, bf16[512,1152]{1,0:T(8,128)(2,1)}, u32[]{:S(2)}, u32[]{:S(2)}) collective-permute-start(bf16[512,1152]{1,0:T(8,128)(2,1)} %get-tuple-element.275), channel_id=1, source_target_pairs={{0,1},{1,0},{2,3},{3,2},{4,5},{5,4},{6,7},{7,6},{8,9},{9,8},{10,11... | collective-permute-start | bytes 3538952 | tf_op jit(solution)/shard_map/ppermute | solution.py:774
  48.6 15.3 %collective-permute-start.13 = (bf16[72,1920]{1,0:T(8,128)(2,1)S(1)}, bf16[72,1920]{1,0:T(8,128)(2,1)S(1)}, u32[]{:S(2)}, u32[]{:S(2)}) collective-permute-start(bf16[72,1920]{1,0:T(8,128)(2,1)S(1)} %collective-permute-done.8.refs_13_), channel_id=1, source_target_pairs={{8,0},{16,8},{24,16},{28,24},{20,28},{12,20},{4,12},{0,4},{9,1},{1... | collective-permute-start | bytes 829448 | tf_op jit(solution)/shard_map/ppermute | solution.py:746
  50.2 13.0 %collective-permute-start.9 = (bf16[72,1792]{1,0:T(8,128)(2,1)S(1)}, bf16[72,1792]{1,0:T(8,128)(2,1)S(1)}, u32[]{:S(2)}, u32[]{:S(2)}) collective-permute-start(bf16[72,1792]{1,0:T(8,128)(2,1)S(1)} %collective-permute-done.5.refs_3_), channel_id=1, source_target_pairs={{0,8},{8,16},{16,24},{24,28},{28,20},{20,12},{12,4},{4,0},{1,9},{9... | collective-permute-start | bytes 774152 | tf_op jit(solution)/shard_map/ppermute | solution.py:745
  63.1 15.2 %collective-permute-start.10 = (bf16[72,1792]{1,0:T(8,128)(2,1)S(1)}, bf16[72,1792]{1,0:T(8,128)(2,1)S(1)}, u32[]{:S(2)}, u32[]{:S(2)}) collective-permute-start(bf16[72,1792]{1,0:T(8,128)(2,1)S(1)} %collective-permute-done.9.refs_4_), channel_id=1, source_target_pairs={{0,8},{8,16},{16,24},{24,28},{28,20},{20,12},{12,4},{4,0},{1,9},{9... | collective-permute-start | bytes 774152 | tf_op jit(solution)/shard_map/ppermute | solution.py:745
  63.9 21.2 %collective-permute-start.14 = (bf16[72,1920]{1,0:T(8,128)(2,1)S(1)}, bf16[72,1920]{1,0:T(8,128)(2,1)S(1)}, u32[]{:S(2)}, u32[]{:S(2)}) collective-permute-start(bf16[72,1920]{1,0:T(8,128)(2,1)S(1)} %collective-permute-done.13.refs_12_), channel_id=1, source_target_pairs={{8,0},{16,8},{24,16},{28,24},{20,28},{12,20},{4,12},{0,4},{9,1},{1... | collective-permute-start | bytes 829448 | tf_op jit(solution)/shard_map/ppermute | solution.py:746
  72.1 59.0 %collective-permute-start.2 = (bf16[512,1152]{1,0:T(8,128)(2,1)}, bf16[512,1152]{1,0:T(8,128)(2,1)S(1)}, u32[]{:S(2)}, u32[]{:S(2)}) collective-permute-start(bf16[512,1152]{1,0:T(8,128)(2,1)} %collective-permute-done.1), channel_id=1, source_target_pairs={{0,1},{1,0},{2,3},{3,2},{4,5},{5,4},{6,7},{7,6},{8,9},{9,8},{10,11... | collective-permute-start | bytes 3538952 | tf_op jit(solution)/shard_map/ppermute | solution.py:774
  78.4 14.4 %collective-permute-start.11 = (bf16[72,1792]{1,0:T(8,128)(2,1)S(1)}, bf16[72,1792]{1,0:T(8,128)(2,1)S(1)}, u32[]{:S(2)}, u32[]{:S(2)}) collective-permute-start(bf16[72,1792]{1,0:T(8,128)(2,1)S(1)} %collective-permute-done.10.refs_5_), channel_id=1, source_target_pairs={{0,8},{8,16},{16,24},{24,28},{28,20},{20,12},{12,4},{4,0},{1,9},{9... | collective-permute-start | bytes 774152 | tf_op jit(solution)/shard_map/ppermute | solution.py:745
  85.0 20.8 %collective-permute-start.15 = (bf16[72,1920]{1,0:T(8,128)(2,1)S(1)}, bf16[72,1920]{1,0:T(8,128)(2,1)S(1)}, u32[]{:S(2)}, u32[]{:S(2)}) collective-permute-start(bf16[72,1920]{1,0:T(8,128)(2,1)S(1)} %collective-permute-done.14.refs_11_), channel_id=1, source_target_pairs={{8,0},{16,8},{24,16},{28,24},{20,28},{12,20},{4,12},{0,4},{9,1},{1... | collective-permute-start | bytes 829448 | tf_op jit(solution)/shard_map/ppermute | solution.py:746
  92.7 21.0 %collective-permute-start.12 = (bf16[72,1792]{1,0:T(8,128)(2,1)S(1)}, bf16[72,1792]{1,0:T(8,128)(2,1)S(1)}, u32[]{:S(2)}, u32[]{:S(2)}) collective-permute-start(bf16[72,1792]{1,0:T(8,128)(2,1)S(1)} %collective-permute-done.11.refs_6_), channel_id=1, source_target_pairs={{0,8},{8,16},{16,24},{24,28},{28,20},{20,12},{12,4},{4,0},{1,9},{9... | collective-permute-start | bytes 774152 | tf_op jit(solution)/shard_map/ppermute | solution.py:745
  105.8 20.5 %collective-permute-start.16 = (bf16[72,1920]{1,0:T(8,128)(2,1)S(1)}, bf16[72,1920]{1,0:T(8,128)(2,1)S(1)}, u32[]{:S(2)}, u32[]{:S(2)}) collective-permute-start(bf16[72,1920]{1,0:T(8,128)(2,1)S(1)} %collective-permute-done.15.refs_10_), channel_id=1, source_target_pairs={{8,0},{16,8},{24,16},{28,24},{20,28},{12,20},{4,12},{0,4},{9,1},{1... | collective-permute-start | bytes 829448 | tf_op jit(solution)/shard_map/ppermute | solution.py:746
  144.0 12.1 %collective-permute-start.17 = (f32[1024,128]{1,0:T(8,128)S(1)}, f32[1024,128]{1,0:T(8,128)S(1)}, u32[]{:S(2)}, u32[]{:S(2)}) collective-permute-start(f32[1024,128]{1,0:T(8,128)S(1)} %get-tuple-element.161), channel_id=1, source_target_pairs={{0,1},{1,0},{2,3},{3,2},{4,5},{5,4},{6,7},{7,6},{8,9},{9,8},{10,11... | collective-permute-start | bytes 1572872 | tf_op jit(solution)/shard_map/ppermute | solution.py:774
  156.1 15.0 %collective-permute-start.18 = (f32[1024,128]{1,0:T(8,128)S(1)}, f32[1024,128]{1,0:T(8,128)}, u32[]{:S(2)}, u32[]{:S(2)}) collective-permute-start(f32[1024,128]{1,0:T(8,128)S(1)} %add.232), channel_id=1, source_target_pairs={{0,2},{1,3},{2,0},{3,1},{4,6},{5,7},{6,4},{7,5},{8,10},{9,11},{10,... | collective-permute-start | bytes 1572872 | tf_op jit(solution)/shard_map/ppermute | solution.py:774
  158.5 34.9 %collective-permute-start.20 = (f32[1024,128]{1,0:T(8,128)}, f32[1024,128]{1,0:T(8,128)}, u32[]{:S(2)}, u32[]{:S(2)}) collective-permute-start(f32[1024,128]{1,0:T(8,128)} %add.236), channel_id=1, source_target_pairs={{0,2},{1,3},{2,0},{3,1},{4,6},{5,7},{6,4},{7,5},{8,10},{9,11},{10,... | collective-permute-start | bytes 1572872 | tf_op jit(solution)/shard_map/ppermute | solution.py:774
  226.9 29.0 %collective-permute-start.22 = (bf16[512,1152]{1,0:T(8,128)(2,1)}, bf16[512,1152]{1,0:T(8,128)(2,1)S(1)}, u32[]{:S(2)}, u32[]{:S(2)}) collective-permute-start(bf16[512,1152]{1,0:T(8,128)(2,1)} %get-tuple-element.276), channel_id=1, source_target_pairs={{0,2},{1,3},{2,0},{3,1},{4,6},{5,7},{6,4},{7,5},{8,10},{9,11},{10,... | collective-permute-start | bytes 3538952 | tf_op jit(solution)/shard_map/ppermute | solution.py:774
  231.0 30.8 %collective-permute-start.26 = (bf16[192,1152]{1,0:T(8,128)(2,1)S(1)}, bf16[192,1152]{1,0:T(8,128)(2,1)S(1)}, u32[]{:S(2)}, u32[]{:S(2)}) collective-permute-start(bf16[192,1152]{1,0:T(8,128)(2,1)S(1)} %get-tuple-element.295), channel_id=1, source_target_pairs={{0,1},{1,0},{2,3},{3,2},{4,5},{5,4},{6,7},{7,6},{8,9},{9,8},{10,11... | collective-permute-start | bytes 1327112 | tf_op jit(solution)/shard_map/ppermute | solution.py:774
  231.2 34.2 %collective-permute-start.27 = (bf16[192,1152]{1,0:T(8,128)(2,1)S(1)}, bf16[192,1152]{1,0:T(8,128)(2,1)S(1)}, u32[]{:S(2)}, u32[]{:S(2)}) collective-permute-start(bf16[192,1152]{1,0:T(8,128)(2,1)S(1)} %get-tuple-element.294), channel_id=1, source_target_pairs={{0,2},{1,3},{2,0},{3,1},{4,6},{5,7},{6,4},{7,5},{8,10},{9,11},{10,... | collective-permute-start | bytes 1327112 | tf_op jit(solution)/shard_map/ppermute | solution.py:774
  233.2 40.1 %collective-permute-start.28 = (bf16[192,1152]{1,0:T(8,128)(2,1)S(1)}, bf16[192,1152]{1,0:T(8,128)(2,1)S(1)}, u32[]{:S(2)}, u32[]{:S(2)}) collective-permute-start(bf16[192,1152]{1,0:T(8,128)(2,1)S(1)} %get-tuple-element.293), channel_id=1, source_target_pairs={{0,3},{1,2},{2,1},{3,0},{4,7},{5,6},{6,5},{7,4},{8,11},{9,10},{10,... | collective-permute-start | bytes 1327112 | tf_op jit(solution)/shard_map/ppermute | solution.py:774
  261.6 31.5 %collective-permute-start.23 = (bf16[192,1152]{1,0:T(8,128)(2,1)S(1)}, bf16[192,1152]{1,0:T(8,128)(2,1)S(1)}, u32[]{:S(2)}, u32[]{:S(2)}) collective-permute-start(bf16[192,1152]{1,0:T(8,128)(2,1)S(1)} %get-tuple-element.299), channel_id=1, source_target_pairs={{0,1},{1,0},{2,3},{3,2},{4,5},{5,4},{6,7},{7,6},{8,9},{9,8},{10,11... | collective-permute-start | bytes 1327112 | tf_op jit(solution)/shard_map/ppermute | solution.py:774
  261.7 31.4 %collective-permute-start.24 = (bf16[192,1152]{1,0:T(8,128)(2,1)S(1)}, bf16[192,1152]{1,0:T(8,128)(2,1)S(1)}, u32[]{:S(2)}, u32[]{:S(2)}) collective-permute-start(bf16[192,1152]{1,0:T(8,128)(2,1)S(1)} %get-tuple-element.298), channel_id=1, source_target_pairs={{0,2},{1,3},{2,0},{3,1},{4,6},{5,7},{6,4},{7,5},{8,10},{9,11},{10,... | collective-permute-start | bytes 1327112 | tf_op jit(solution)/shard_map/ppermute | solution.py:774
  261.8 31.4 %collective-permute-start.25 = (bf16[192,1152]{1,0:T(8,128)(2,1)S(1)}, bf16[192,1152]{1,0:T(8,128)(2,1)S(1)}, u32[]{:S(2)}, u32[]{:S(2)}) collective-permute-start(bf16[192,1152]{1,0:T(8,128)(2,1)S(1)} %get-tuple-element.297), channel_id=1, source_target_pairs={{0,3},{1,2},{2,1},{3,0},{4,7},{5,6},{6,5},{7,4},{8,11},{9,10},{10,... | collective-permute-start | bytes 1327112 | tf_op jit(solution)/shard_map/ppermute | solution.py:774
  265.4 9.0 %collective-permute-start.29 = (f32[192]{0:T(256)S(1)}, f32[192]{0:T(256)S(1)}, u32[]{:S(2)}, u32[]{:S(2)}) collective-permute-start(f32[192]{0:T(256)S(1)} %bitcast.122), channel_id=1, source_target_pairs={{0,1},{1,0},{2,3},{3,2},{4,5},{5,4},{6,7},{7,6},{8,9},{9,8},{10,11... | collective-permute-start | bytes 2312 | tf_op jit(solution)/shard_map/ppermute | solution.py:774
  273.3 19.8 %collective-permute-start.30 = (f32[192]{0:T(256)S(1)}, f32[192]{0:T(256)S(1)}, u32[]{:S(2)}, u32[]{:S(2)}) collective-permute-start(f32[192]{0:T(256)S(1)} %bitcast.120), channel_id=1, source_target_pairs={{0,2},{1,3},{2,0},{3,1},{4,6},{5,7},{6,4},{7,5},{8,10},{9,11},{10,... | collective-permute-start | bytes 2312 | tf_op jit(solution)/shard_map/ppermute | solution.py:774
  274.4 18.6 %collective-permute-start.31 = (f32[192]{0:T(256)S(1)}, f32[192]{0:T(256)S(1)}, u32[]{:S(2)}, u32[]{:S(2)}) collective-permute-start(f32[192]{0:T(256)S(1)} %bitcast.119), channel_id=1, source_target_pairs={{0,3},{1,2},{2,1},{3,0},{4,7},{5,6},{6,5},{7,4},{8,11},{9,10},{10,... | collective-permute-start | bytes 2312 | tf_op jit(solution)/shard_map/ppermute | solution.py:774
  343.6 331.1 %reduce-scatter.5.cloned.1.call-start = ((), (), s32[]{:S(2)}) async-start(), calls=%async_computation.4 | async-start | bytes 3317760 | tf_op jit(solution)/shard_map/reduce_scatter | solution.py:918
  345.4 22.3 %collective-permute-start.32 = (bf16[192,1152]{1,0:T(8,128)(2,1)S(1)}, bf16[192,1152]{1,0:T(8,128)(2,1)S(1)}, u32[]{:S(2)}, u32[]{:S(2)}) collective-permute-start(bf16[192,1152]{1,0:T(8,128)(2,1)S(1)} %get-tuple-element.291), channel_id=1, source_target_pairs={{0,1},{1,0},{2,3},{3,2},{4,5},{5,4},{6,7},{7,6},{8,9},{9,8},{10,11... | collective-permute-start | bytes 1327112 | tf_op jit(solution)/shard_map/ppermute | solution.py:774
  345.6 22.1 %collective-permute-start.33 = (bf16[192,1152]{1,0:T(8,128)(2,1)S(1)}, bf16[192,1152]{1,0:T(8,128)(2,1)S(1)}, u32[]{:S(2)}, u32[]{:S(2)}) collective-permute-start(bf16[192,1152]{1,0:T(8,128)(2,1)S(1)} %get-tuple-element.290), channel_id=1, source_target_pairs={{0,2},{1,3},{2,0},{3,1},{4,6},{5,7},{6,4},{7,5},{8,10},{9,11},{10,... | collective-permute-start | bytes 1327112 | tf_op jit(solution)/shard_map/ppermute | solution.py:774
  345.9 21.8 %collective-permute-start.34 = (bf16[192,1152]{1,0:T(8,128)(2,1)S(1)}, bf16[192,1152]{1,0:T(8,128)(2,1)S(1)}, u32[]{:S(2)}, u32[]{:S(2)}) collective-permute-start(bf16[192,1152]{1,0:T(8,128)(2,1)S(1)} %get-tuple-element.289), channel_id=1, source_target_pairs={{0,3},{1,2},{2,1},{3,0},{4,7},{5,6},{6,5},{7,4},{8,11},{9,10},{10,... | collective-permute-start | bytes 1327112 | tf_op jit(solution)/shard_map/ppermute | solution.py:774
  348.6 19.0 %collective-permute-start.36 = (f32[192]{0:T(256)S(1)}, f32[192]{0:T(256)S(1)}, u32[]{:S(2)}, u32[]{:S(2)}) collective-permute-start(f32[192]{0:T(256)S(1)} %bitcast.123), channel_id=1, source_target_pairs={{0,2},{1,3},{2,0},{3,1},{4,6},{5,7},{6,4},{7,5},{8,10},{9,11},{10,... | collective-permute-start | bytes 2312 | tf_op jit(solution)/shard_map/ppermute | solution.py:774
  349.4 18.2 %collective-permute-start.37 = (f32[192]{0:T(256)S(1)}, f32[192]{0:T(256)S(1)}, u32[]{:S(2)}, u32[]{:S(2)}) collective-permute-start(f32[192]{0:T(256)S(1)} %bitcast.121), channel_id=1, source_target_pairs={{0,3},{1,2},{2,1},{3,0},{4,7},{5,6},{6,5},{7,4},{8,11},{9,10},{10,... | collective-permute-start | bytes 2312 | tf_op jit(solution)/shard_map/ppermute | solution.py:774
  375.7 28.1 %collective-permute-start.39 = (bf16[512,1152]{1,0:T(8,128)(2,1)S(1)}, bf16[512,1152]{1,0:T(8,128)(2,1)S(1)}, u32[]{:S(2)}, u32[]{:S(2)}) collective-permute-start(bf16[512,1152]{1,0:T(8,128)(2,1)S(1)} %get-tuple-element.182), channel_id=1, source_target_pairs={{0,2},{1,3},{2,0},{3,1},{4,6},{5,7},{6,4},{7,5},{8,10},{9,11},{10,... | collective-permute-start | bytes 3538952 | tf_op jit(solution)/shard_map/ppermute | solution.py:774
  376.0 28.4 %collective-permute-start.38 = (bf16[512,1152]{1,0:T(8,128)(2,1)S(1)}, bf16[512,1152]{1,0:T(8,128)(2,1)S(1)}, u32[]{:S(2)}, u32[]{:S(2)}) collective-permute-start(bf16[512,1152]{1,0:T(8,128)(2,1)S(1)} %get-tuple-element.182), channel_id=1, source_target_pairs={{0,1},{1,0},{2,3},{3,2},{4,5},{5,4},{6,7},{7,6},{8,9},{9,8},{10,11... | collective-permute-start | bytes 3538952 | tf_op jit(solution)/shard_map/ppermute | solution.py:774
  455.1 46.5 %collective-permute-start.43 = (bf16[1024,128]{1,0:T(8,128)(2,1)}, bf16[1024,128]{1,0:T(8,128)(2,1)S(1)}, u32[]{:S(2)}, u32[]{:S(2)}) collective-permute-start(bf16[1024,128]{1,0:T(8,128)(2,1)} %get-tuple-element.197), channel_id=1, source_target_pairs={{0,1},{1,0},{2,3},{3,2},{4,5},{5,4},{6,7},{7,6},{8,9},{9,8},{10,11... | collective-permute-start | bytes 786440 | tf_op jit(solution)/shard_map/ppermute | solution.py:774
  501.8 9.2 %collective-permute-start.44 = (bf16[1024,128]{1,0:T(8,128)(2,1)S(1)}, bf16[1024,128]{1,0:T(8,128)(2,1)S(1)}, u32[]{:S(2)}, u32[]{:S(2)}) collective-permute-start(bf16[1024,128]{1,0:T(8,128)(2,1)S(1)} %add.249), channel_id=1, source_target_pairs={{0,2},{1,3},{2,0},{3,1},{4,6},{5,7},{6,4},{7,5},{8,10},{9,11},{10,... | collective-permute-start | bytes 786440 | tf_op jit(solution)/shard_map/ppermute | solution.py:774
  503.9 29.5 %collective-permute-start.42 = (bf16[1024,128]{1,0:T(8,128)(2,1)S(1)}, bf16[1024,128]{1,0:T(8,128)(2,1)S(1)}, u32[]{:S(2)}, u32[]{:S(2)}) collective-permute-start(bf16[1024,128]{1,0:T(8,128)(2,1)S(1)} %add.247), channel_id=1, source_target_pairs={{0,2},{1,3},{2,0},{3,1},{4,6},{5,7},{6,4},{7,5},{8,10},{9,11},{10,... | collective-permute-start | bytes 786440 | tf_op jit(solution)/shard_map/ppermute | solution.py:774
  554.8 13.8 %collective-permute-start.49 = (bf16[2,512,1152]{2,1,0:T(8,128)(2,1)S(1)}, bf16[2,512,1152]{2,1,0:T(8,128)(2,1)S(1)}, u32[]{:S(2)}, u32[]{:S(2)}) collective-permute-start(bf16[2,512,1152]{2,1,0:T(8,128)(2,1)S(1)} %pad_maximum_fusion.2), channel_id=1, source_target_pairs={{0,1},{1,0},{2,3},{3,2},{4,5},{5,4},{6,7},{7,6},{8,9},{9,8},{10,11... | collective-permute-start | bytes 7077896 | tf_op jit(solution)/shard_map/ppermute | solution.py:774
  559.5 35.7 %collective-permute-start.46 = (bf16[192,1152]{1,0:T(8,128)(2,1)}, bf16[192,1152]{1,0:T(8,128)(2,1)}, u32[]{:S(2)}, u32[]{:S(2)}) collective-permute-start(bf16[192,1152]{1,0:T(8,128)(2,1)} %get-tuple-element.287), channel_id=1, source_target_pairs={{0,1},{1,0},{2,3},{3,2},{4,5},{5,4},{6,7},{7,6},{8,9},{9,8},{10,11... | collective-permute-start | bytes 1327112 | tf_op jit(solution)/shard_map/ppermute | solution.py:774
  559.5 40.2 %collective-permute-start.47 = (bf16[192,1152]{1,0:T(8,128)(2,1)}, bf16[192,1152]{1,0:T(8,128)(2,1)}, u32[]{:S(2)}, u32[]{:S(2)}) collective-permute-start(bf16[192,1152]{1,0:T(8,128)(2,1)} %get-tuple-element.286), channel_id=1, source_target_pairs={{0,2},{1,3},{2,0},{3,1},{4,6},{5,7},{6,4},{7,5},{8,10},{9,11},{10,... | collective-permute-start | bytes 1327112 | tf_op jit(solution)/shard_map/ppermute | solution.py:774
  559.7 40.1 %collective-permute-start.48 = (bf16[192,1152]{1,0:T(8,128)(2,1)}, bf16[192,1152]{1,0:T(8,128)(2,1)}, u32[]{:S(2)}, u32[]{:S(2)}) collective-permute-start(bf16[192,1152]{1,0:T(8,128)(2,1)} %get-tuple-element.285), channel_id=1, source_target_pairs={{0,3},{1,2},{2,1},{3,0},{4,7},{5,6},{6,5},{7,4},{8,11},{9,10},{10,... | collective-permute-start | bytes 1327112 | tf_op jit(solution)/shard_map/ppermute | solution.py:774
  568.3 14.7 %collective-permute-start.53 = (f32[6,1152]{1,0:T(8,128)S(1)}, f32[6,1152]{1,0:T(8,128)S(1)}, u32[]{:S(2)}, u32[]{:S(2)}) collective-permute-start(f32[6,1152]{1,0:T(8,128)S(1)} %fusion.42), channel_id=1, source_target_pairs={{0,2},{1,3},{2,0},{3,1},{4,6},{5,7},{6,4},{7,5},{8,10},{9,11},{10,... | collective-permute-start | bytes 82952 | tf_op jit(solution)/shard_map/ppermute | solution.py:774
  572.5 35.5 %collective-permute-start.50 = (bf16[512,1152]{1,0:T(8,128)(2,1)}, bf16[512,1152]{1,0:T(8,128)(2,1)}, u32[]{:S(2)}, u32[]{:S(2)}) collective-permute-start(bf16[512,1152]{1,0:T(8,128)(2,1)} %fusion.32), channel_id=1, source_target_pairs={{0,2},{1,3},{2,0},{3,1},{4,6},{5,7},{6,4},{7,5},{8,10},{9,11},{10,... | collective-permute-start | bytes 3538952 | tf_op jit(solution)/shard_map/ppermute | solution.py:774
  593.1 25.6 %collective-permute-start.45 = (bf16[4,80,1408]{2,1,0:T(8,128)(2,1)S(1)}, bf16[4,80,1408]{2,1,0:T(8,128)(2,1)}, u32[]{:S(2)}, u32[]{:S(2)}) collective-permute-start(bf16[4,80,1408]{2,1,0:T(8,128)(2,1)S(1)} %get-tuple-element.283), channel_id=1, source_target_pairs={{0,4},{4,0},{8,12},{12,8},{16,20},{20,16},{24,28},{28,24},{1,5},{5... | collective-permute-start | bytes 2703368 | tf_op jit(solution)/shard_map/ppermute | solution.py:763
  620.4 19.9 %collective-permute-start.51 = (bf16[2,80,1408]{2,1,0:T(8,128)(2,1)S(1)}, bf16[2,80,1408]{2,1,0:T(8,128)(2,1)S(1)}, u32[]{:S(2)}, u32[]{:S(2)}) collective-permute-start(bf16[2,80,1408]{2,1,0:T(8,128)(2,1)S(1)} %get-tuple-element.300), channel_id=1, source_target_pairs={{0,8},{4,12},{8,0},{12,4},{16,24},{20,28},{24,16},{28,20},{1,9},{5... | collective-permute-start | bytes 1351688 | tf_op jit(solution)/shard_map/ppermute | solution.py:763
  640.4 12.9 %collective-permute-start.57 = (bf16[1,80,1408]{2,1,0:T(8,128)(2,1)S(1)}, bf16[1,80,1408]{2,1,0:T(8,128)(2,1)S(1)}, u32[]{:S(2)}, u32[]{:S(2)}) collective-permute-start(bf16[1,80,1408]{2,1,0:T(8,128)(2,1)S(1)} %get-tuple-element.303), channel_id=1, source_target_pairs={{0,16},{4,20},{8,24},{12,28},{16,0},{20,4},{24,8},{28,12},{1,17},{... | collective-permute-start | bytes 675848 | tf_op jit(solution)/shard_map/ppermute | solution.py:763
  (111 other events, 1387.8 us)
Sparse Core Ops, SparseCore 0:
  42.4 215.8 all-gather.1
  343.7 234.1 reduce-scatter.2
  591.3 83.2 reduce-scatter.4

commit v3 on v2

--- a/solution.py
+++ b/solution.py
@@ -452,7 +452,7 @@
 def conv_bwd_kernel(
     dact_ref, dsel_ref, selw_ref, pre_ref, conv_ref, dgate_ref, w_ref, seq_ref, chan_ref, next_ref,
     actb_ref, ddl_ref, rank_ref, before_ref, gchin_ref, tail_ref,
-    dnorm_ref, gain_ref, head_ref, gch_ref, grad_ref, buf, acc, *, T, g, final
+    dnorm_ref, gain_ref, head_ref, gch_ref, grad_ref, buf, acc, *, T, g, opens, final
 ):
     C, D = conv_ref.shape[1], seq_ref.shape[1]
     step = pl.program_id(0)
@@ -460,9 +460,13 @@
     @pl.when(step == 0)
     def _():
         buf[T : T + 8, :] = next_ref[...]
-        gch_ref[...] = gchin_ref[...]
         gain_ref[...] = jnp.zeros_like(gain_ref)
-        acc[...] = before_ref[...]
+        if opens:
+            gch_ref[...] = jnp.zeros_like(gch_ref)
+            acc[...] = jnp.zeros_like(acc)
+        else:
+            gch_ref[...] = gchin_ref[...]
+            acc[...] = before_ref[...]
 
     pre = pre_ref[...]
     sig = 1.0 / (1.0 + jnp.exp(-pre))
@@ -506,22 +510,23 @@
 def conv_bwd(at, count, final, dact, dsel, selw, pre, conv, dgate, w_in, seq, chan, later, actb, ddl, rank, before, gch, tail, T=BLOCK):
     C, D = conv.shape[1], seq.shape[1]
     g = count // T
+    opens = before is None
     own = lambda w: rows_back(T, w, g - 1)
     packed = SHAPE((C, D + 2 * LANES), bf16 if final else f32)
     return pl.pallas_call(
-        functools.partial(conv_bwd_kernel, T=T, g=g, final=final),
+        functools.partial(conv_bwd_kernel, T=T, g=g, opens=opens, final=final),
         grid=(g,),
         in_specs=[
             own(C), own(LANES), whole(selw.shape), own(C), own(C), own(C), whole(w_in.shape),
             rows_back(T, D, at // T + g - 1), whole(chan.shape), whole(later.shape),
-            own(C), own(C), own(LANES), whole(before.shape), whole(gch.shape), whole(tail.shape),
+            own(C), own(C), own(LANES), whole((8, LANES) if opens else before.shape), whole(gch.shape), whole(tail.shape),
         ],
         out_specs=[own(D), whole((8, D)), whole((8, C)), whole((8, C)), whole(packed.shape)],
         out_shape=[SHAPE((count, D), bf16), SHAPE((8, D), f32), SHAPE((8, C), f32), SHAPE((8, C), f32), packed],
         scratch_shapes=[pltpu.VMEM((T + 8, C), f32), pltpu.VMEM(packed.shape, f32)],
         compiler_params=params(56),
         cost_estimate=cost(),
-    )(dact, dsel, selw, pre, conv, dgate, w_in, seq, chan, later, actb, ddl, rank, before, gch, tail)
+    )(dact, dsel, selw, pre, conv, dgate, w_in, seq, chan, later, actb, ddl, rank, jnp.zeros((8, LANES), f32) if opens else before, gch, tail)
 
 
 def as_column(row, count):
@@ -532,27 +537,31 @@
     return jnp.broadcast_to(column, (count, LANES)).T[0:8, :]
 
 
-def experts_kernel(x_ref, cot_ref, prob_ref, w_ref, out_ref, drow_ref, dot_ref, g_ref, acc_out, acc_row, dz_ref, *, steps, per, units):
+def experts_kernel(x0, x1, x2, x3, c0, c1, c2, c3, prob_ref, w_ref, out_ref, drow_ref, dot_ref, g_ref, acc_out, acc_row, x_ref, dz_ref, xt_ref, dzt_ref, *, steps, per, units):
     R = x_ref.shape[0]
 
     @pl.when(pl.program_id(0) == 0)
     def _():
         acc_out[...] = jnp.zeros_like(acc_out)
         acc_row[...] = jnp.zeros_like(acc_row)
-        dz_ref[...] = (as_column(prob_ref[...], R) * cot_ref[...].astype(f32)).astype(bf16)
-
-    x, dz = x_ref[...], dz_ref[...]
+        x_ref[...] = jnp.concatenate([x0[...], x1[...], x2[...], x3[...]], axis=0)
+        cot = jnp.concatenate([c0[...], c1[...], c2[...], c3[...]], axis=0)
+        dz = as_column(prob_ref[...], R) * cot.astype(f32)
+        dz_ref[...] = dz.astype(bf16)
+        dzt_ref[...] = dz.T.astype(bf16)
+        xt_ref[...] = x_ref[...].astype(f32).T.astype(bf16)
+
     up = jnp.concatenate([w_ref[2 * r * units : (2 * r + 1) * units, :] for r in range(per)], axis=0)
     down = jnp.concatenate([w_ref[(2 * r + 1) * units : (2 * r + 2) * units, :] for r in range(per)], axis=0)
-    lin = dotf(x, up, ((1,), (1,)))
+    lin = dotf(up, xt_ref[...])
     cdf = 0.5 * (1.0 + lax.erf(lin * math.sqrt(0.5)))
     act = (lin * cdf).astype(bf16)
     slope = cdf + lin * jnp.exp(-0.5 * lin * lin) * (1.0 / math.sqrt(2.0 * math.pi))
-    acc_out[...] += dotf(act, down)
-    dlin = (dotf(dz, down, ((1,), (1,))) * slope).astype(bf16)
-    acc_row[...] += dotf(dlin, up)
-    gdown = dotf(act, dz, ((0,), (0,))).astype(bf16)
-    gup = dotf(dlin, x, ((0,), (0,))).astype(bf16)
+    dlin = (dotf(down, dzt_ref[...]) * slope).astype(bf16)
+    gdown = dotf(act, dz_ref[...]).astype(bf16)
+    gup = dotf(dlin, x_ref[...]).astype(bf16)
+    acc_out[...] += dotf(act, down, ((0,), (0,)))
+    acc_row[...] += dotf(dlin, up, ((0,), (0,)))
     for r in range(per):
         g_ref[2 * r * units : (2 * r + 1) * units, :] = gup[r * units : (r + 1) * units]
         g_ref[(2 * r + 1) * units : (2 * r + 2) * units, :] = gdown[r * units : (r + 1) * units]
@@ -562,11 +571,11 @@
         out = acc_out[...].astype(bf16)
         out_ref[...] = out
         drow_ref[...] = acc_row[...].astype(bf16)
-        dot_ref[...] = as_rows(jnp.sum(out.astype(f32) * dz.astype(f32), axis=1, keepdims=True), R)
+        dot_ref[...] = as_rows(jnp.sum(out.astype(f32) * dz_ref[...].astype(f32), axis=1, keepdims=True), R)
 
 
 def experts(x, cot, prob, w, units, per=2):
-    R, D = x.shape
+    R, D = len(x) * x[0].shape[0], x[0].shape[1]
     block = 2 * units * per
     steps = w.shape[0] // block
     fix = whole((R, D))
@@ -574,13 +583,13 @@
     return pl.pallas_call(
         functools.partial(experts_kernel, steps=steps, per=per, units=units),
         grid=(steps,),
-        in_specs=[fix, fix, whole(prob.shape), mov],
+        in_specs=[whole(x[0].shape)] * 8 + [whole(prob.shape), mov],
         out_specs=[fix, fix, whole((8, R)), mov],
         out_shape=[SHAPE((R, D), bf16)] * 2 + [SHAPE((8, R), f32), SHAPE(w.shape, bf16)],
-        scratch_shapes=[pltpu.VMEM((R, D), f32)] * 2 + [pltpu.VMEM((R, D), bf16)],
+        scratch_shapes=[pltpu.VMEM((R, D), f32)] * 2 + [pltpu.VMEM((R, D), bf16)] * 2 + [pltpu.VMEM((D, R), bf16)] * 2,
         compiler_params=params(60),
         cost_estimate=cost(),
-    )(x, cot, prob, w)
+    )(*x, *cot, prob, w)
 
 
 def mean_scale(values):
@@ -620,14 +629,15 @@
     )(source, near, far, gains, router, ids, row, col)
 
 
-def back_kernel(rows_ref, dot_ref, col_ref, ids_ref, prob_ref, router_ref, res_ref, cot_ref, gain_ref, dres_ref, dmix_ref, part_ref, *, count):
+def back_kernel(r0, r1, r2, r3, dot_ref, col_ref, ids_ref, prob_ref, router_ref, res_ref, cot_ref, gain_ref, dres_ref, dmix_ref, part_ref, *, count):
     res = res_ref[...]
-    T, S = res.shape[0], rows_ref.shape[0]
+    T, S = res.shape[0], dot_ref.shape[1]
+    rows = jnp.concatenate([r0[...], r1[...], r2[...], r3[...]], axis=0)
     put = lax.broadcasted_iota(jnp.int32, (T, S), 1) == col_ref[...]
     lane = lax.broadcasted_iota(jnp.int32, (T, LANES), 1)
     weighted = jnp.sum(jnp.where(put, dot_ref[0:1, :], 0.0), axis=1, keepdims=True)
     dlog = weighted * (jnp.where(lane == ids_ref[...], 1.0, 0.0) - prob_ref[...])
-    dnorm = dotf(put.astype(bf16), rows_ref[...]) + dot32(dlog, router_ref[...], ((1,), (1,)))
+    dnorm = dotf(put.astype(bf16), rows) + dot32(dlog, router_ref[...], ((1,), (1,)))
     scale = mean_scale(res)
     hat = res * scale
     part_ref[0:8, :] = jnp.broadcast_to(jnp.sum(dnorm * hat, axis=0, keepdims=True), (8, res.shape[1]))
@@ -645,7 +655,7 @@
         out_shape=[SHAPE((T, D), f32), SHAPE((T, D), bf16), SHAPE((16, D), f32)],
         compiler_params=params(48),
         cost_estimate=cost(),
-    )(rows, dots, col, ids, probs, router, res, cot, gains)
+    )(*rows, dots, col, ids, probs, router, res, cot, gains)
 
 
 def step_of(refs, outs, grad, rate, factor, at=Ellipsis):
@@ -668,21 +678,21 @@
 
 
 def mixer_step_kernel(*refs, factor, own, width, xw, vrows):
-    conv_ref, early_ref = refs[:2]
-    ins = [refs[2 + 3 * p : 5 + 3 * p] for p in range(5)]
-    outs = [refs[17 + 4 * p : 21 + 4 * p] for p in range(5)]
+    conv_ref, gate_ref, outg_ref = refs[:3]
+    ins = [refs[4 + 3 * p : 7 + 3 * p] for p in range(5)]
+    outs = [refs[19 + 4 * p : 23 + 4 * p] for p in range(5)]
     inward, select, delta, channel, outward = range(5)
     step_of(ins[inward], outs[inward], conv_ref[0:own, 0:width].astype(f32), LEARNING[0], factor, 0)
-    step_of(ins[inward], outs[inward], early_ref[0:own, 0:width].astype(f32), LEARNING[0], factor, 1)
+    step_of(ins[inward], outs[inward], gate_ref[0:own, :].astype(f32), LEARNING[0], factor, 1)
     at = width
     step_of(ins[select], outs[select], conv_ref[0:own, at : at + LANES].astype(f32)[:, 0:xw], LEARNING[1], factor)
     rest = upright(conv_ref[:, at + LANES : at + 2 * LANES], LANES, own)
     step_of(ins[delta], outs[delta], rest[0:DT_RANK], LEARNING[2], factor)
     step_of(ins[channel], outs[channel], rest[DT_RANK : DT_RANK + vrows], LEARNING[3], factor)
-    step_of(ins[outward], outs[outward], early_ref[0:own, width:].astype(f32), LEARNING[4], factor)
-
-
-def mixer_step(conv, early, triples, factor):
+    step_of(ins[outward], outs[outward], outg_ref[0:own, :].astype(f32), LEARNING[4], factor)
+
+
+def mixer_step(conv, gate, outg, last, triples, factor):
     own, width = triples[4][0].shape
     xw, vrows = triples[1][0].shape[1], triples[3][0].shape[0]
     shapes = []
@@ -693,7 +703,7 @@
         out_shape=shapes,
         compiler_params=params(56),
         cost_estimate=cost(),
-    )(conv, early, *[a for triple in triples for a in triple])
+    )(conv, gate, outg, last, *[a for triple in triples for a in triple])
     return [flat[4 * p : 4 * p + 4] for p in range(5)]
 
 
@@ -720,7 +730,10 @@
         compiler_params=params(48),
         cost_estimate=cost(),
     )(grads, grads, *ups, *downs)
-    return flat[:4], flat[4:]
+    return list(flat[:4]), list(flat[4:])
+
+
+START, PIECES = 5, 4
 
 
 def contract_rows(left, right):
@@ -735,13 +748,14 @@
     return list(range(0, n, 2)) + list(range(n - 1, 0, -2))
 
 
-def ring_gather(ahead_part, back_part, axis):
+def ring_gather(ahead_part, back_part, axis, between):
     n = lax.axis_size(axis)
     order = ring_order(n)
     ahead = [(order[i], order[(i + 1) % n]) for i in range(n)]
     back = [(b, a) for a, b in ahead]
     first, second = [ahead_part], [back_part]
-    for _ in range(n - 1):
+    for s in range(n - 1):
+        first[-1], second[-1] = between(s, first[-1], second[-1])
         first.append(lax.ppermute(first[-1], axis, ahead))
         second.append(lax.ppermute(second[-1], axis, back))
     place = [order.index(i) for i in range(n)]
@@ -749,24 +763,61 @@
     return owners[lax.axis_index(axis)], first, [second[-r % n] for r in range(n)]
 
 
-def halving_sum(value, axis, fills=()):
-    n = lax.axis_size(axis)
-    me = lax.axis_index(axis)
-    bit, out = 1, []
-    rows = value.shape[1:]
-    value = value.reshape((n,) + rows)
-    while bit < n:
-        mine = (me // bit) % 2
-        pairs = value.reshape((value.shape[0] // 2, 2) + rows)
-        keep = lax.dynamic_index_in_dim(pairs, mine, 1, keepdims=False)
-        send = lax.dynamic_index_in_dim(pairs, 1 - mine, 1, keepdims=False)
-        got = lax.ppermute(send, axis, [(i, i ^ bit) for i in range(n)])
-        if fills:
-            keep, *done = tie(keep, *fills[0]())
-            fills, out = fills[1:], out + [done]
-        value = (keep.astype(f32) + got.astype(f32)).astype(bf16)
-        bit *= 2
-    return value[0], out + [fill() for fill in fills]
+class HalvingSum:
+    def __init__(self, value, axis):
+        self.axis, self.n, self.me = axis, lax.axis_size(axis), lax.axis_index(axis)
+        self.value, self.bit, self.sent = value, 1, False
+
+    def launch(self, token):
+        if self.bit < self.n:
+            self.sent = True
+            mine = (self.me // self.bit) % 2
+            shape = self.value.shape
+            pairs = self.value.reshape((shape[0] // 2, 2) + shape[1:])
+            self.keep = lax.dynamic_index_in_dim(pairs, mine, 1, keepdims=False)
+            send = lax.dynamic_index_in_dim(pairs, 1 - mine, 1, keepdims=False)
+            send, token = tie(send, token)
+            self.got = lax.ppermute(send, self.axis, [(i, i ^ self.bit) for i in range(self.n)])
+        return token
+
+    def land(self, token):
+        if self.sent:
+            self.sent = False
+            keep, token = tie(self.keep, token)
+            self.value = (keep.astype(f32) + self.got.astype(f32)).astype(bf16)
+            self.bit *= 2
+        return token
+
+    def finish(self):
+        while self.bit < self.n:
+            token = jnp.zeros((1,), f32)
+            self.land(token if self.sent else self.launch(token))
+        return self.value[0]
+
+
+class SharedSum:
+    def __init__(self, value, axis):
+        self.axis, self.n = axis, lax.axis_size(axis)
+        self.value, self.bit, self.got = value, 1, None
+
+    def launch(self, token):
+        if self.bit < self.n:
+            value, token = tie(self.value, token)
+            self.value = value
+            self.got = lax.ppermute(value, self.axis, [(i, i ^ self.bit) for i in range(self.n)])
+        return token
+
+    def land(self, token):
+        if self.got is not None:
+            value, token = tie(self.value, token)
+            self.value, self.got = value + self.got, None
+            self.bit *= 2
+        return token
+
+    def finish(self):
+        while self.bit < self.n:
+            self.land(self.launch(jnp.zeros((1,), f32)))
+        return self.value
 
 
 def swap(value, j):
@@ -774,12 +825,17 @@
     return lax.ppermute(value, "mp", [(i, i ^ j) for i in range(n)])
 
 
-def gather_mp(rows):
-    me, n = lax.axis_index("mp"), lax.axis_size("mp")
+def gather_mp_blocks(rows):
     near = swap(rows, 1)
     across = swap(rows, 2)
+    return [rows, near, across, swap(across, 1)]
+
+
+def in_order(blocks):
+    me, n = lax.axis_index("mp"), lax.axis_size("mp")
+    rows = blocks[0]
     total = jnp.zeros((n,) + rows.shape, rows.dtype)
-    for j, block in enumerate([rows, near, across, swap(across, 1)]):
+    for j, block in enumerate(blocks):
         total = lax.dynamic_update_index_in_dim(total, block, me ^ j, 0)
     return total.reshape(n * rows.shape[0], rows.shape[1])
 
@@ -789,7 +845,7 @@
     return value + swap(value, 2)
 
 
-def scatter_mp(halves):
+def scatter_near(halves):
     me = lax.axis_index("mp")
 
     def pick(j):
@@ -798,20 +854,12 @@
         two = lax.dynamic_index_in_dim(halves[1], k, 0, keepdims=False)
         return jnp.where((me ^ j) < 2, one, two)
 
-    near = swap(jnp.stack([pick(3), pick(1)]), 1).astype(f32)
-    far = (pick(2).astype(f32) + near[0]).astype(bf16)
-    return pick(0).astype(f32) + near[1], swap(far, 2)
-
-
-def butterfly(value):
-    for j in (1, 2):
-        value = value + swap(value, j)
-    n = lax.axis_size("dp")
-    step = 1
-    while step < n:
-        value = value + lax.ppermute(value, "dp", [(i, i ^ step) for i in range(n)])
-        step *= 2
-    return value
+    return [pick(0), pick(2), swap(jnp.stack([pick(3), pick(1)]), 1)]
+
+
+def scatter_far(mine, others, near):
+    near = near.astype(f32)
+    return mine.astype(f32) + near[1], (others.astype(f32) + near[0]).astype(bf16)
 
 
 def nesterov(weight, velocity, average, step_grad, rate):
@@ -838,36 +886,57 @@
     experts_all = router_weight.shape[1]
     slots = peers * CAP
 
+    source = block_input.astype(f32)
+    scale1 = mean_scale(source)
+    normed_b = (source * scale1 * norm_gains[0]).astype(bf16)
+    blocks = [normed_b]
+    piece = tok_rows // PIECES
+    pieces = [normed_b[i * piece : (i + 1) * piece] for i in range(PIECES)]
+
     half = 5 * LANES
-    owners, mix_a, mix_b = ring_gather(
-        *prep(jnp.swapaxes(inward_proj, 1, 2), select_proj, delta_proj, channel_params, outward_proj, half), "dp"
+    units = expert_down.shape[1]
+    ring_a, ring_b = prep(
+        jnp.swapaxes(inward_proj, 1, 2), select_proj, delta_proj, channel_params, outward_proj, half
     )
-    units = expert_down.shape[1]
-    mix_a[3], mix_b[-3], up_own = tie(mix_a[3], mix_b[-3], expert_up[0])
-    expert_w = lax.all_gather(prep_experts(up_own, expert_down[0]), "dp", axis=0, tiled=True)
-    w_in, selw, delta_w, chan, out_w = mixer_weights(owners, mix_a, mix_b, slot, wide, width, half)
+
+    def exchange(blocks):
+        parts = blocks.reshape(peers, CAP, -1)
+        return [parts[0]] + [swap(parts[j], j) for j in range(1, peers)]
 
     slot_index = (expert_ids ^ me) * CAP + slot_ids
     slot_row, slot_col, ids_col = slot_index[None, :], slot_index[:, None], expert_ids[:, None]
     dispatch = (lax.broadcasted_iota(jnp.int32, (slots, tok_rows), 0) == slot_row).astype(bf16)
+    early = {"cot": jnp.dot(dispatch, cotangent, preferred_element_type=f32).astype(bf16), "up": expert_up[0]}
+
+    def between(s, a, b):
+        if s == START:
+            a, b, early["up"] = tie(a, b, early["up"])
+        if s < PIECES:
+            pieces[s], a, b = tie(pieces[s], a, b)
+            pieces[s] = swap(pieces[s], 2)
+        if 0 < s <= PIECES:
+            a, b, pieces[s - 1] = tie(a, b, pieces[s - 1])
+        if s == PIECES:
+            blocks.extend([swap(normed_b, 1), jnp.concatenate(pieces)])
+            blocks.append(swap(blocks[2], 1))
+            a, b, early["cot"] = tie(a, b, early["cot"])
+            early["cot"] = exchange(early["cot"])
+        if s == PIECES + 1:
+            a, b, blocks[1], blocks[3] = tie(a, b, blocks[1], blocks[3])
+        return a, b
+
+    owners, mix_a, mix_b = ring_gather(ring_a, ring_b, "dp", between)
+    expert_w = lax.all_gather(prep_experts(early["up"], expert_down[0]), "dp", axis=0, tiled=True)
+    w_in, selw, delta_w, chan, out_w = mixer_weights(owners, mix_a, mix_b, slot, wide, width, half)
+    seq = in_order(blocks)
+    seq, *cot_rows = tie(seq, *early["cot"])
+
     router_pad = jnp.pad(router_weight, ((0, 0), (0, LANES - experts_all)))
-
-    def exchange(blocks):
-        parts = blocks.reshape(peers, CAP, -1)
-        return jnp.concatenate([parts[0]] + [swap(parts[j], j) for j in range(1, peers)])
 
     def exchange_row(rows):
         parts = rows[0].reshape(peers, CAP)
         row = jnp.concatenate([parts[0]] + [swap(parts[j], j) for j in range(1, peers)])
         return jnp.broadcast_to(row[None], (8, slots))
-
-    source = block_input.astype(f32)
-    scale1 = mean_scale(source)
-    normed_b = (source * scale1 * norm_gains[0]).astype(bf16)
-    seq = gather_mp(normed_b)
-    cot_out = jnp.dot(dispatch, cotangent, preferred_element_type=f32).astype(bf16)
-    cot_out, seq = tie(cot_out, seq)
-    cot_rows = exchange(cot_out)
 
     count = seq.shape[0] // 2
     conv_tail, state = jnp.zeros((8, wide), f32), jnp.zeros((NST, wide), f32)
@@ -882,7 +951,8 @@
         scans.append(scan_fwd(selections[h], delta_w, act, gate_in, chan, out_w, state))
         state = scans[-1][6]
         edges.append(state)
-    near, far = scatter_mp([s[4].reshape(2, tok_rows, width) for s in scans])
+    near, far = scatter_far(*scatter_near([s[4].reshape(2, tok_rows, width) for s in scans]))
+    far = swap(far, 2)
     residual, probs, gate_prob, outgoing, prob_slots = route_tokens(
         block_input, near, far, norm_gains, router_pad, ids_col, slot_row, slot_col, slots, experts_all
     )
@@ -894,7 +964,7 @@
         exchange(d_rows), exchange_row(dots), slot_col, ids_col, probs, router_pad, residual, cotangent, norm_gains,
         experts_all,
     )
-    portion = gather_mp(d_mixer)
+    portion = in_order(gather_mp_blocks(d_mixer))
     expert_out, portion = tie(expert_out, portion)
     returned = exchange(expert_out)
 
@@ -904,55 +974,63 @@
     def cut(a):
         return a[: slot * ring]
 
-    out_grad = both([s[3] for s in scans], portion).astype(bf16)
+    by_owner = lambda a: HalvingSum(cut(a).reshape(ring, slot, -1), "dp")
+    out_sum = by_owner(both([s[3] for s in scans], portion).astype(bf16))
     q, later = jnp.zeros((NST, wide), f32), jnp.zeros((8, wide), f32)
     tails, sums = [None] * 2, [None] * 2
     for h in (1, 0):
         kept = scans[h][0], convs[h][3], convs[h][1], scans[h][1], scans[h][2]
+        q = out_sum.launch(q)
         tails[h] = scan_bwd(portion, h * count, 0, kept, edges[h], q, count, out_w, selections[h], chan, delta_w)
-        q = tails[h][5]
+        q = out_sum.land(tails[h][5])
         sums[h] = sum_mp(tails[h][3])
-    gate_grad = both([t[0] for t in tails], seq).astype(bf16)
-    early = jnp.concatenate([cut(gate_grad), cut(out_grad)], axis=1)
-    early, experts_grad = tie(early, experts_grad)
-    early = lax.psum_scatter(early, "dp", scatter_dimension=0, tiled=True)
-    grads, gch = jnp.zeros((wide, width + 2 * LANES), f32), jnp.zeros((8, wide), f32)
+    gate_sum = by_owner(both([t[0] for t in tails], seq).astype(bf16))
+    grads, gch = None, jnp.zeros((8, wide), f32)
     tail_sum = tails[0][4] + tails[1][4]
     dnorms, gains = [None] * 2, [None] * 2
     for h in (1, 0):
+        later = gate_sum.launch(out_sum.launch(later))
         dnorms[h], gains[h], later, gch, grads = conv_bwd(
             h * count, count, h == 0, tails[h][1], sums[h], selw, convs[h][2], convs[h][0], tails[h][0], w_in, seq,
             chan, later, convs[h][4], tails[h][2], scans[h][5], grads, gch, tail_sum,
         )
-    near, far = scatter_mp([d.reshape(2, tok_rows, width) for d in dnorms])
+        later = gate_sum.land(out_sum.land(later))
+    conv_sum = by_owner(grads)
     factor = 1.0 / math.sqrt(tok_rows * ring * peers)
     gain_part = (gains[0][:1] + gains[1][:1]) / norm_gains[:1]
-    small = jnp.concatenate([gain_part, parts[:1], parts[8 : 8 + experts_all]])
-
-    def expert_update():
-        up_new, down_new = experts_step(
-            experts_grad,
-            (expert_up, upward_velocity, upward_average),
-            (expert_down, downward_velocity, downward_average),
-            factor,
-        )
-        return list(up_new) + list(down_new)
-
-    def token_results():
-        d_normed = near + far.astype(f32)
-        a1 = norm_gains[0] * d_normed
-        hat1 = source * scale1
-        block_grad = d_residual + scale1 * (a1 - hat1 * jnp.mean(a1 * hat1, axis=-1, keepdims=True))
-        tokens_out = contract_rows(dispatch, returned)
-        return (residual + gate_prob[:, :1] * tokens_out).astype(bf16), block_grad
-
-    conv_grad, filled = halving_sum(
-        cut(grads).reshape(ring, slot, -1), "dp", [expert_update, token_results, lambda: [butterfly(small)]]
+    shared = SharedSum(jnp.concatenate([gain_part, parts[:1], parts[8 : 8 + experts_all]]), "dp")
+    near = scatter_near([d.reshape(2, tok_rows, width) for d in dnorms])
+    later = gate_sum.launch(conv_sum.launch(later))
+    later, experts_grad = tie(shared.launch(later), experts_grad)
+    up_new, down_new = experts_step(
+        experts_grad,
+        (expert_up, upward_velocity, upward_average),
+        (expert_down, downward_velocity, downward_average),
+        factor,
     )
-    expert_new, (block_output, block_grad), (shared,) = filled[:3]
+    later, up_new[3], near[2] = tie(later, up_new[3], near[2])
+    near, far_send = scatter_far(*near)
+    far_send, later = tie(far_send, later)
+    far = swap(far_send, 2)
+    later = shared.land(gate_sum.land(conv_sum.land(later)))
+    later, returned[0] = tie(shared.launch(conv_sum.launch(later)), returned[0])
+    tokens_out = contract_rows(dispatch, jnp.concatenate(returned))
+    block_output = (residual + gate_prob[:, :1] * tokens_out).astype(bf16)
+    later, block_output = tie(later, block_output)
+    later = shared.land(conv_sum.land(later))
+    later, far = tie(shared.launch(conv_sum.launch(later)), far)
+    d_normed = near + far.astype(f32)
+    a1 = norm_gains[0] * d_normed
+    hat1 = source * scale1
+    block_grad = d_residual + scale1 * (a1 - hat1 * jnp.mean(a1 * hat1, axis=-1, keepdims=True))
+    later, block_grad = tie(later, block_grad)
+    later = shared.land(conv_sum.land(later))
+    shared = sum_mp(shared.finish())
     mixer_new = mixer_step(
-        conv_grad,
-        early,
+        conv_sum.finish(),
+        gate_sum.finish(),
+        out_sum.finish(),
+        later,
         (
             tuple(jnp.swapaxes(a, 1, 2) for a in (inward_proj, inward_velocity, inward_average)),
             (select_proj, select_velocity, select_average),
@@ -966,7 +1044,8 @@
     mixer_new[0] = [jnp.swapaxes(a, 1, 2) for a in mixer_new[0]]
     for new in mixer_new:
         results.extend(new)
-    results.extend(expert_new)
+    results.extend(up_new)
+    results.extend(down_new)
     results.extend(nesterov(norm_gains, gains_velocity, gains_average, shared[:2] * factor, LEARNING[7]))
     results.extend(nesterov(router_weight, router_velocity, router_average, shared[2:].T * factor, LEARNING[8]))
     return tuple(results)

time: 691 us -> 648 us (0.938)
  waiting for transfers between devices: 233 us -> 195 us
    reduce_scatter x1 -> x0, waiting for transfers between devices: 20.6 us -> none  [body(): early = lax.psum_scatter(early, 'dp', scatter_dimension=0, tiled=True)]
    ppermute x7, waiting for transfers between devices: 30.2 us -> 12.2 us  [ring_gather(): second.append(lax.ppermute(second[-1], axis, back))]
    ppermute x7, waiting for transfers between devices: 28.1 us -> 40.9 us  [ring_gather(): first.append(lax.ppermute(first[-1], axis, ahead))]
    ppermute x38 -> x41, waiting for transfers between devices: 132 us -> 120 us  [swap(): return lax.ppermute(value, 'mp', [(i, i ^ j) for i in range(n)])]
    ppermute x38 -> x41, starting transfers between devices: 19 us -> 30.9 us  [swap(): return lax.ppermute(value, 'mp', [(i, i ^ j) for i in range(n)])]
    ppermute x7, starting transfers between devices: 17 us -> 9.71 us  [ring_gather(): second.append(lax.ppermute(second[-1], axis, back))]
    ppermute x6 -> x12, starting transfers between devices: 16.6 us -> 11.5 us  [the longest x9 8.84 us: launch(): lax.ppermute(send, self.axis, [(i, i ^ self.bit) for i in range(self.n)])]
    unnamed x197 -> x224, local copies, waits for them, and re-layouts: 25.1 us -> 22.6 us
  transfers between devices with their start and end apart: 61 -> 69, of which waited for: 32 -> 23; matrix products, arithmetic and copies ran while one was open for 11% -> 13% of each run, Pallas kernels for 31% -> 33%
where the time goes in v3:
time: 648 us; the launch traced here: 642 us
  Pallas kernels  263 us (41%)
  waiting for transfers between devices  195 us (30%)
  starting transfers between devices  62.8 us (10%)
  local copies, waits for them, and re-layouts  53.6 us (8%)
  other arithmetic  31.8 us (5%)
  matrix products  19.7 us (3%)
  between operations  15.8 us (2%)
    ppermute x41, waiting for transfers between devices, swap(): return lax.ppermute(value, 'mp', [(i, i ^ j) for i in range(n)])  120 us
    pallas_call x2, Pallas kernels, scan_bwd(): pl.pallas_call(functools.partial(scan_bwd_kernel, T=T, g=g, opens=low ==...  91.5 us
    pallas_call x1, Pallas kernels, experts(): pl.pallas_call(functools.partial(experts_kernel, steps=steps, per=per, un...  46.9 us
    ppermute x7, waiting for transfers between devices, ring_gather(): first.append(lax.ppermute(first[-1], axis, ahead))  40.9 us
    pallas_call x2, Pallas kernels, scan_fwd(): pl.pallas_call(functools.partial(scan_fwd_kernel, T=T), grid=(g,), in_spe...  39.9 us
    pallas_call x2, Pallas kernels, conv_bwd(): pl.pallas_call(functools.partial(conv_bwd_kernel, T=T, g=g, opens=opens,...  35.9 us
    ppermute x41, starting transfers between devices, swap(): return lax.ppermute(value, 'mp', [(i, i ^ j) for i in range(n)])  30.9 us
    unnamed x224, local copies, waits for them, and re-layouts  22.6 us
  transfers between devices with their start and end apart: 69, of which 23 were waited for; matrix products, arithmetic and copies ran while one was open for 13% of the time, Pallas kernels for 33%

profile of v3, /device:TPU:0, one launch (start us, length us, event | category | flops | bytes accessed | tf_op | source)
XLA Modules:
  0.0 642.3 jit_solution(14389029279512790427)
XLA Ops:
  13.6 3.0 collective-permute-start.2
  19.4 6.2 collective-permute-done.refs_1_
  28.8 5.2 collective-permute-done.3.refs_2_
  38.3 5.3 collective-permute-done.6.refs_3_
  46.1 2.4 convolution_convert_fusion
  48.6 6.4 collective-permute-done.9.refs_4_
  57.7 4.2 collective-permute-done.12.refs_5_
  70.7 2.5 fusion.49
  77.2 2.4 bitcast_dynamic-update-slice_fusion.6
  79.8 2.6 bitcast_dynamic-update-slice_fusion.5
  82.3 7.8 %collective-permute-done.19.refs_6_ = bf16[72,1792]{1,0:T(8,128)(2,1)S(1)} collective-permute-done((bf16[72,1792]{1,0:T(8,128)(2,1)S(1)}, bf16[72,1792]{1,0:T(8,128)(2,1)S(1)}, u32[]{:S(2)}, u32[]{:S(2)}) %collective-permute-start.19) | collective-permute-done | bytes 258080 | tf_op jit(solution)/shard_map/ppermute | solution.py:759
  90.1 6.4 collective-permute-start.20
  99.1 2.4 bitcast_dynamic-update-slice_fusion.4
  101.6 5.9 collective-permute-done.20.refs_7_
  107.5 11.3 %collective-permute-done.22.refs_9_ = bf16[72,1920]{1,0:T(8,128)(2,1)S(1)} collective-permute-done((bf16[72,1920]{1,0:T(8,128)(2,1)S(1)}, bf16[72,1920]{1,0:T(8,128)(2,1)S(1)}, u32[]{:S(2)}, u32[]{:S(2)}) %collective-permute-start.22) | collective-permute-done | bytes 276512 | tf_op jit(solution)/shard_map/ppermute | solution.py:760
  118.8 2.9 shard_map.600
  121.7 9.7 %shard_map.601 = (f32[1024,640]{1,0:T(8,128)S(1)}, f32[1024,640]{1,0:T(8,128)}, f32[1024,640]{1,0:T(8,128)}, f32[1024,640]{1,0:T(8,128)}, bf16[1024,640]{1,0:T(8...) custom-call(bf16[2048,1152]{1,0:T(8,128)(2,1)} %bitcast.115, bf16[1280,1152]{1,0:T(8,128)(2,1)} %get-tuple-element.269.w_ref, ...), custom_call_target="tpu_custom_call" | custom-call | bytes 1048576 | tf_op jit(solution)/shard_map/pallas_call | solution.py:218
  134.1 9.1 %shard_map.603 = (f32[1024,640]{1,0:T(8,128)S(1)}, f32[1024,640]{1,0:T(8,128)}, f32[1024,640]{1,0:T(8,128)}, f32[1024,640]{1,0:T(8,128)}, bf16[1024,640]{1,0:T(8...) custom-call(bf16[2048,1152]{1,0:T(8,128)(2,1)} %bitcast.116, bf16[1280,1152]{1,0:T(8,128)(2,1)} %get-tuple-element.269.w_ref, ...), custom_call_target="tpu_custom_call" | custom-call | bytes 1048576 | tf_op jit(solution)/shard_map/pallas_call | solution.py:218
  149.3 12.8 %collective-permute-done.24 = f32[1024,128]{1,0:T(8,128)} collective-permute-done((f32[1024,128]{1,0:T(8,128)}, f32[1024,128]{1,0:T(8,128)}, u32[]{:S(2)}, u32[]{:S(2)}) %collective-permute-start.24) | collective-permute-done | bytes 524320 | tf_op jit(solution)/shard_map/ppermute | solution.py:825
  163.4 19.9 %shard_map.602 = (bf16[64,256,640]{2,1,0:T(8,128)(2,1)}, f32[1024,640]{1,0:T(8,128)}, f32[1024,640]{1,0:T(8,128)}, bf16[1024,640]{1,0:T(8,128)(2,1)S(1)}, bf16[1...) custom-call(f32[1024,128]{1,0:T(8,128)S(1)} %add.270.sel_ref, ...), custom_call_target="tpu_custom_call" | custom-call | bytes 1048576 | tf_op jit(solution)/shard_map/pallas_call | solution.py:288
  185.7 20.0 %shard_map.604 = (bf16[64,256,640]{2,1,0:T(8,128)(2,1)}, f32[1024,640]{1,0:T(8,128)}, f32[1024,640]{1,0:T(8,128)}, bf16[1024,640]{1,0:T(8,128)(2,1)S(1)}, bf16[1...) custom-call(f32[1024,128]{1,0:T(8,128)S(1)} %add.274.sel_ref, ...), custom_call_target="tpu_custom_call" | custom-call | bytes 1048576 | tf_op jit(solution)/shard_map/pallas_call | solution.py:288
  205.8 2.4 dynamic-slice_select_fusion.3
  209.9 4.7 collective-permute-done.27
  215.0 2.5 fusion.31
  221.4 24.2 %collective-permute-done.28.far_ref = bf16[512,1152]{1,0:T(8,128)(2,1)S(1)} collective-permute-done((bf16[512,1152]{1,0:T(8,128)(2,1)}, bf16[512,1152]{1,0:T(8,128)(2,1)S(1)}, u32[]{:S(2)}, u32[]{:S(2)}) %collective-permute-start.28) | collective-permute-done | bytes 1179680 | tf_op jit(solution)/shard_map/ppermute | solution.py:825
  245.7 5.5 shard_map.605
  256.7 17.6 %collective-permute-done.33 = f32[192]{0:T(256)S(1)} collective-permute-done((f32[192]{0:T(256)S(1)}, f32[192]{0:T(256)S(1)}, u32[]{:S(2)}, u32[]{:S(2)}) %collective-permute-start.33) | collective-permute-done | bytes 800 | tf_op jit(solution)/shard_map/ppermute | solution.py:825
  275.2 46.9 %shard_map.607 = (bf16[768,1152]{1,0:T(8,128)(2,1)}, bf16[768,1152]{1,0:T(8,128)(2,1)}, f32[8,768]{1,0:T(8,128)}, bf16[6144,1152]{1,0:T(8,128)(2,1)}) custom-call(bf16[192,1152]{1,0:T(8,128)(2,1)} %get-tuple-element.455.x0, bf16[192,1152]{1,0:T(8,128)(2,1)} %copy-done.79, bf16[192,1152]{1,0:T(8,128)(2,1)} %copy-done.80, ...), custom_call_target="tpu_custom_call" | custom-call | bytes 1048576 | tf_op jit(solution)/shard_map/pallas_call | solution.py:583
  329.2 16.8 %collective-permute-done.39 = f32[192]{0:T(256)S(1)} collective-permute-done((f32[192]{0:T(256)S(1)}, f32[192]{0:T(256)S(1)}, u32[]{:S(2)}, u32[]{:S(2)}) %collective-permute-start.39) | collective-permute-done | bytes 800 | tf_op jit(solution)/shard_map/ppermute | solution.py:825
  346.1 7.8 %shard_map.608 = (f32[512,1152]{1,0:T(8,128)}, bf16[512,1152]{1,0:T(8,128)(2,1)S(1)}, f32[16,1152]{1,0:T(8,128)S(1)}) custom-call(bf16[192,1152]{1,0:T(8,128)(2,1)S(1)} %get-tuple-element.451.r0, bf16[192,1152]{1,0:T(8,128)(2,1)S(1)} %collective-permute-done.35.r1, bf16[192,1152]{1,0:T(8,128)(2,1)S(1)} %collective-permute-done.36.r2, ...), custom_call_target="tpu_custom_call" | custom-call | bytes 1048576 | tf_op jit(solution)/shard_map/pallas_call | solution.py:653
  356.0 26.7 %collective-permute-done.42 = bf16[512,1152]{1,0:T(8,128)(2,1)} collective-permute-done((bf16[512,1152]{1,0:T(8,128)(2,1)S(1)}, bf16[512,1152]{1,0:T(8,128)(2,1)}, u32[]{:S(2)}, u32[]{:S(2)}) %collective-permute-start.42) | collective-permute-done | bytes 1179680 | tf_op jit(solution)/shard_map/ppermute | solution.py:825
  391.2 45.8 %shard_map.609 = (bf16[1024,640]{1,0:T(8,128)(2,1)}, f32[1024,640]{1,0:T(8,128)}, bf16[1024,640]{1,0:T(8,128)(2,1)}, bf16[1024,128]{1,0:T(8,128)(2,1)}, f32[24,640]{1,0:T(8,128)}, /*index=5*/f32[16,640]{1,0:T(8,128)}) custom-call(bf16[2048,1152]{1,0:T(8,128)(2,1)} %bitcast.125, bf16[640,1152]{1,0:T(8,128)(2,1)} %copy-done.1, ...), custom_call_target="tpu_custom_call" | custom-call | bytes 1048576 | tf_op jit(solution)/shard_map/pallas_call | solution.py:430
  436.9 5.6 fusion.17
  442.8 2.6 collective-permute-start.47
  445.4 45.7 %shard_map.610 = (bf16[1024,640]{1,0:T(8,128)(2,1)}, f32[1024,640]{1,0:T(8,128)}, bf16[1024,640]{1,0:T(8,128)(2,1)}, bf16[1024,128]{1,0:T(8,128)(2,1)}, f32[24,640]{1,0:T(8,128)}, /*index=5*/f32[16,640]{1,0:T(8,128)}) custom-call(bf16[2048,1152]{1,0:T(8,128)(2,1)} %bitcast.126, bf16[640,1152]{1,0:T(8,128)(2,1)} %copy-done.1, ...), custom_call_target="tpu_custom_call" | custom-call | bytes 1048576 | tf_op jit(solution)/shard_map/pallas_call | solution.py:430
  491.1 4.1 fusion.1
  502.1 7.0 %collective-permute-done.49 = bf16[1024,128]{1,0:T(8,128)(2,1)S(1)} collective-permute-done((bf16[1024,128]{1,0:T(8,128)(2,1)S(1)}, bf16[1024,128]{1,0:T(8,128)(2,1)S(1)}, u32[]{:S(2)}, u32[]{:S(2)}) %collective-permute-start.49) | collective-permute-done | bytes 262176 | tf_op jit(solution)/shard_map/ppermute | solution.py:825
  511.1 17.9 %shard_map.611 = (bf16[1024,1152]{1,0:T(8,128)(2,1)}, f32[8,1152]{1,0:T(8,128)}, f32[8,640]{1,0:T(8,128)}, f32[8,640]{1,0:T(8,128)}, f32[640,1408]{1,0:T(8,128)}) custom-call(f32[1024,640]{1,0:T(8,128)} %get-tuple-element.319.dact_ref, bf16[1024,128]{1,0:T(8,128)(2,1)} %add.299.dsel_ref, bf16[640,128]{1,0:T(8,128)(2,1)} %copy-done.10, ...), custom_call_target="tpu_custom_call" | custom-call | bytes 1048576 | tf_op jit(solution)/shard_map/pallas_call | solution.py:516
  530.7 18.0 %shard_map.612 = (bf16[1024,1152]{1,0:T(8,128)(2,1)}, f32[8,1152]{1,0:T(8,128)}, f32[8,640]{1,0:T(8,128)}, f32[8,640]{1,0:T(8,128)}, bf16[640,1408]{1,0:T(8,128)(2,1)}) custom-call(f32[1024,640]{1,0:T(8,128)} %get-tuple-element.312.dact_ref, bf16[1024,128]{1,0:T(8,128)(2,1)} %add.292.dsel_ref, bf16[640,128]{1,0:T(8,128)(2,1)} %copy-done.10, ...), custom_call_target="tpu_custom_call" | custom-call | bytes 1048576 | tf_op jit(solution)/shard_map/pallas_call | solution.py:516
  560.3 8.9 %collective-permute-done.51 = bf16[2,80,1152]{2,1,0:T(8,128)(2,1)S(1)} collective-permute-done((bf16[2,80,1152]{2,1,0:T(8,128)(2,1)}, bf16[2,80,1152]{2,1,0:T(8,128)(2,1)S(1)}, u32[]{:S(2)}, u32[]{:S(2)}) %collective-permute-start.51) | collective-permute-done | bytes 368672 | tf_op jit(solution)/shard_map/ppermute | solution.py:780
  573.1 8.4 %shard_map.613 = (f32[1,1152,384]{2,1,0:T(8,128)}, f32[1,1152,384]{2,1,0:T(8,128)}, f32[1,1152,384]{2,1,0:T(8,128)}, bf16[1,1152,384]{2,1,0:T(8,128)(2,1)}, f32[...) custom-call(bf16[768,1152]{1,0:T(8,128)(2,1)S(1)} %copy-done.2, ...), custom_call_target="tpu_custom_call" | custom-call | bytes 1048576 | tf_op jit(solution)/shard_map/pallas_call | solution.py:724
  582.5 2.1 convert_element_type.168
  586.0 5.3 collective-permute-done.54
  599.7 3.6 add_convert_fusion
  603.3 6.2 collective-permute-done.58
  612.7 8.4 %collective-permute-done.60 = bf16[512,1152]{1,0:T(8,128)(2,1)S(1)} collective-permute-done((bf16[512,1152]{1,0:T(8,128)(2,1)S(1)}, bf16[512,1152]{1,0:T(8,128)(2,1)S(1)}, u32[]{:S(2)}, u32[]{:S(2)}) %collective-permute-start.60) | collective-permute-done | bytes 1179680 | tf_op jit(solution)/shard_map/ppermute | solution.py:825
  622.1 2.5 fusion.9
  628.5 4.1 shard_map.614
  (424 shorter events, 126.7 us)
Async XLA Ops:
  7.2 267.1 %all-gather.2.cloned.1.call-start = ((), (), s32[]{:S(2)}) async-start(), calls=%async_computation.1 | async-start | bytes 15925248 | tf_op jit(solution)/shard_map/all_gather | solution.py:929
  13.6 12.4 %collective-permute-start.2 = (bf16[128,1152]{1,0:T(8,128)(2,1)S(1)}, bf16[128,1152]{1,0:T(8,128)(2,1)S(1)}, u32[]{:S(2)}, u32[]{:S(2)}) collective-permute-start(bf16[128,1152]{1,0:T(8,128)(2,1)S(1)} %get-tuple-element.239), channel_id=1, source_target_pairs={{0,2},{1,3},{2,0},{3,1},{4,6},{5,7},{6,4},{7,5},{8,10},{9,11},{10,... | collective-permute-start | bytes 884744 | tf_op jit(solution)/shard_map/ppermute | solution.py:825
  25.6 9.9 %collective-permute-start.5 = (bf16[128,1152]{1,0:T(8,128)(2,1)S(1)}, bf16[128,1152]{1,0:T(8,128)(2,1)S(1)}, u32[]{:S(2)}, u32[]{:S(2)}) collective-permute-start(bf16[128,1152]{1,0:T(8,128)(2,1)S(1)} %get-tuple-element.244), channel_id=1, source_target_pairs={{0,2},{1,3},{2,0},{3,1},{4,6},{5,7},{6,4},{7,5},{8,10},{9,11},{10,... | collective-permute-start | bytes 884744 | tf_op jit(solution)/shard_map/ppermute | solution.py:825
  34.0 10.1 %collective-permute-start.8 = (bf16[128,1152]{1,0:T(8,128)(2,1)S(1)}, bf16[128,1152]{1,0:T(8,128)(2,1)S(1)}, u32[]{:S(2)}, u32[]{:S(2)}) collective-permute-start(bf16[128,1152]{1,0:T(8,128)(2,1)S(1)} %get-tuple-element.249), channel_id=1, source_target_pairs={{0,2},{1,3},{2,0},{3,1},{4,6},{5,7},{6,4},{7,5},{8,10},{9,11},{10,... | collective-permute-start | bytes 884744 | tf_op jit(solution)/shard_map/ppermute | solution.py:825
  43.6 11.3 %collective-permute-start.11 = (bf16[128,1152]{1,0:T(8,128)(2,1)S(1)}, bf16[128,1152]{1,0:T(8,128)(2,1)S(1)}, u32[]{:S(2)}, u32[]{:S(2)}) collective-permute-start(bf16[128,1152]{1,0:T(8,128)(2,1)S(1)} %get-tuple-element.252), channel_id=1, source_target_pairs={{0,2},{1,3},{2,0},{3,1},{4,6},{5,7},{6,4},{7,5},{8,10},{9,11},{10,... | collective-permute-start | bytes 884744 | tf_op jit(solution)/shard_map/ppermute | solution.py:825
  44.0 10.9 %collective-permute-start.10 = (bf16[72,1920]{1,0:T(8,128)(2,1)S(1)}, bf16[72,1920]{1,0:T(8,128)(2,1)S(1)}, u32[]{:S(2)}, u32[]{:S(2)}) collective-permute-start(bf16[72,1920]{1,0:T(8,128)(2,1)S(1)} %collective-permute-done.7.refs_13_), channel_id=1, source_target_pairs={{8,0},{16,8},{24,16},{28,24},{20,28},{12,20},{4,12},{0,4},{9,1},{1... | collective-permute-start | bytes 829448 | tf_op jit(solution)/shard_map/ppermute | solution.py:760
  63.5 506.6 %reduce-scatter.2.cloned.1.call-start = ((), (), s32[]{:S(2)}) async-start(), calls=%async_computation.2 | async-start | bytes 15925248 | tf_op jit(solution)/shard_map/reduce_scatter | solution.py:961
  63.6 11.6 %collective-permute-start.14 = (bf16[512,1152]{1,0:T(8,128)(2,1)S(1)}, bf16[512,1152]{1,0:T(8,128)(2,1)}, u32[]{:S(2)}, u32[]{:S(2)}) collective-permute-start(bf16[512,1152]{1,0:T(8,128)(2,1)S(1)} %get-tuple-element.435), channel_id=1, source_target_pairs={{0,1},{1,0},{2,3},{3,2},{4,5},{5,4},{6,7},{7,6},{8,9},{9,8},{10,11... | collective-permute-start | bytes 3538952 | tf_op jit(solution)/shard_map/ppermute | solution.py:825
  73.3 28.2 %collective-permute-start.16 = (bf16[192,1152]{1,0:T(8,128)(2,1)S(1)}, bf16[192,1152]{1,0:T(8,128)(2,1)S(1)}, u32[]{:S(2)}, u32[]{:S(2)}) collective-permute-start(bf16[192,1152]{1,0:T(8,128)(2,1)S(1)} %get-tuple-element.458), channel_id=1, source_target_pairs={{0,1},{1,0},{2,3},{3,2},{4,5},{5,4},{6,7},{7,6},{8,9},{9,8},{10,11... | collective-permute-start | bytes 1327112 | tf_op jit(solution)/shard_map/ppermute | solution.py:825
  73.3 28.2 %collective-permute-start.17 = (bf16[192,1152]{1,0:T(8,128)(2,1)S(1)}, bf16[192,1152]{1,0:T(8,128)(2,1)S(1)}, u32[]{:S(2)}, u32[]{:S(2)}) collective-permute-start(bf16[192,1152]{1,0:T(8,128)(2,1)S(1)} %get-tuple-element.457), channel_id=1, source_target_pairs={{0,2},{1,3},{2,0},{3,1},{4,6},{5,7},{6,4},{7,5},{8,10},{9,11},{10,... | collective-permute-start | bytes 1327112 | tf_op jit(solution)/shard_map/ppermute | solution.py:825
  74.7 26.8 %collective-permute-start.18 = (bf16[192,1152]{1,0:T(8,128)(2,1)S(1)}, bf16[192,1152]{1,0:T(8,128)(2,1)S(1)}, u32[]{:S(2)}, u32[]{:S(2)}) collective-permute-start(bf16[192,1152]{1,0:T(8,128)(2,1)S(1)} %get-tuple-element.456), channel_id=1, source_target_pairs={{0,3},{1,2},{2,1},{3,0},{4,7},{5,6},{6,5},{7,4},{8,11},{9,10},{10,... | collective-permute-start | bytes 1327112 | tf_op jit(solution)/shard_map/ppermute | solution.py:825
  75.2 22.3 %collective-permute-start.21 = (bf16[72,1920]{1,0:T(8,128)(2,1)S(1)}, bf16[72,1920]{1,0:T(8,128)(2,1)S(1)}, u32[]{:S(2)}, u32[]{:S(2)}) collective-permute-start(bf16[72,1920]{1,0:T(8,128)(2,1)S(1)} %collective-permute-done.13.refs_11_), channel_id=1, source_target_pairs={{8,0},{16,8},{24,16},{28,24},{20,28},{12,20},{4,12},{0,4},{9,1},{1... | collective-permute-start | bytes 829448 | tf_op jit(solution)/shard_map/ppermute | solution.py:760
  75.9 14.3 %collective-permute-start.19 = (bf16[72,1792]{1,0:T(8,128)(2,1)S(1)}, bf16[72,1792]{1,0:T(8,128)(2,1)S(1)}, u32[]{:S(2)}, u32[]{:S(2)}) collective-permute-start(bf16[72,1792]{1,0:T(8,128)(2,1)S(1)} %collective-permute-done.12.refs_5_), channel_id=1, source_target_pairs={{0,8},{8,16},{16,24},{24,28},{28,20},{20,12},{12,4},{4,0},{1,9},{9... | collective-permute-start | bytes 774152 | tf_op jit(solution)/shard_map/ppermute | solution.py:759
  90.1 17.3 %collective-permute-start.20 = (bf16[72,1792]{1,0:T(8,128)(2,1)S(1)}, bf16[72,1792]{1,0:T(8,128)(2,1)S(1)}, u32[]{:S(2)}, u32[]{:S(2)}) collective-permute-start(bf16[72,1792]{1,0:T(8,128)(2,1)S(1)} %collective-permute-done.19.refs_6_), channel_id=1, source_target_pairs={{0,8},{8,16},{16,24},{24,28},{28,20},{20,12},{12,4},{4,0},{1,9},{9... | collective-permute-start | bytes 774152 | tf_op jit(solution)/shard_map/ppermute | solution.py:759
  97.5 21.2 %collective-permute-start.22 = (bf16[72,1920]{1,0:T(8,128)(2,1)S(1)}, bf16[72,1920]{1,0:T(8,128)(2,1)S(1)}, u32[]{:S(2)}, u32[]{:S(2)}) collective-permute-start(bf16[72,1920]{1,0:T(8,128)(2,1)S(1)} %collective-permute-done.21.refs_10_), channel_id=1, source_target_pairs={{8,0},{16,8},{24,16},{28,24},{20,28},{12,20},{4,12},{0,4},{9,1},{1... | collective-permute-start | bytes 829448 | tf_op jit(solution)/shard_map/ppermute | solution.py:760
  134.0 12.1 %collective-permute-start.23 = (f32[1024,128]{1,0:T(8,128)S(1)}, f32[1024,128]{1,0:T(8,128)S(1)}, u32[]{:S(2)}, u32[]{:S(2)}) collective-permute-start(f32[1024,128]{1,0:T(8,128)S(1)} %get-tuple-element.272), channel_id=1, source_target_pairs={{0,1},{1,0},{2,3},{3,2},{4,5},{5,4},{6,7},{7,6},{8,9},{9,8},{10,11... | collective-permute-start | bytes 1572872 | tf_op jit(solution)/shard_map/ppermute | solution.py:825
  147.0 15.1 %collective-permute-start.24 = (f32[1024,128]{1,0:T(8,128)}, f32[1024,128]{1,0:T(8,128)}, u32[]{:S(2)}, u32[]{:S(2)}) collective-permute-start(f32[1024,128]{1,0:T(8,128)} %add.269), channel_id=1, source_target_pairs={{0,2},{1,3},{2,0},{3,1},{4,6},{5,7},{6,4},{7,5},{8,10},{9,11},{10,... | collective-permute-start | bytes 1572872 | tf_op jit(solution)/shard_map/ppermute | solution.py:825
  148.5 35.9 %collective-permute-start.26 = (f32[1024,128]{1,0:T(8,128)S(1)}, f32[1024,128]{1,0:T(8,128)}, u32[]{:S(2)}, u32[]{:S(2)}) collective-permute-start(f32[1024,128]{1,0:T(8,128)S(1)} %add.273), channel_id=1, source_target_pairs={{0,2},{1,3},{2,0},{3,1},{4,6},{5,7},{6,4},{7,5},{8,10},{9,11},{10,... | collective-permute-start | bytes 1572872 | tf_op jit(solution)/shard_map/ppermute | solution.py:825
  217.4 28.2 %collective-permute-start.28 = (bf16[512,1152]{1,0:T(8,128)(2,1)}, bf16[512,1152]{1,0:T(8,128)(2,1)S(1)}, u32[]{:S(2)}, u32[]{:S(2)}) collective-permute-start(bf16[512,1152]{1,0:T(8,128)(2,1)} %get-tuple-element.436), channel_id=1, source_target_pairs={{0,2},{1,3},{2,0},{3,1},{4,6},{5,7},{6,4},{7,5},{8,10},{9,11},{10,... | collective-permute-start | bytes 3538952 | tf_op jit(solution)/shard_map/ppermute | solution.py:825
  252.1 22.2 %collective-permute-start.29 = (bf16[192,1152]{1,0:T(8,128)(2,1)S(1)}, bf16[192,1152]{1,0:T(8,128)(2,1)S(1)}, u32[]{:S(2)}, u32[]{:S(2)}) collective-permute-start(bf16[192,1152]{1,0:T(8,128)(2,1)S(1)} %get-tuple-element.454), channel_id=1, source_target_pairs={{0,1},{1,0},{2,3},{3,2},{4,5},{5,4},{6,7},{7,6},{8,9},{9,8},{10,11... | collective-permute-start | bytes 1327112 | tf_op jit(solution)/shard_map/ppermute | solution.py:825
  252.1 22.2 %collective-permute-start.30 = (bf16[192,1152]{1,0:T(8,128)(2,1)S(1)}, bf16[192,1152]{1,0:T(8,128)(2,1)S(1)}, u32[]{:S(2)}, u32[]{:S(2)}) collective-permute-start(bf16[192,1152]{1,0:T(8,128)(2,1)S(1)} %get-tuple-element.453), channel_id=1, source_target_pairs={{0,2},{1,3},{2,0},{3,1},{4,6},{5,7},{6,4},{7,5},{8,10},{9,11},{10,... | collective-permute-start | bytes 1327112 | tf_op jit(solution)/shard_map/ppermute | solution.py:825
  253.7 20.6 %collective-permute-start.31 = (bf16[192,1152]{1,0:T(8,128)(2,1)S(1)}, bf16[192,1152]{1,0:T(8,128)(2,1)}, u32[]{:S(2)}, u32[]{:S(2)}) collective-permute-start(bf16[192,1152]{1,0:T(8,128)(2,1)S(1)} %get-tuple-element.452), channel_id=1, source_target_pairs={{0,3},{1,2},{2,1},{3,0},{4,7},{5,6},{6,5},{7,4},{8,11},{9,10},{10,... | collective-permute-start | bytes 1327112 | tf_op jit(solution)/shard_map/ppermute | solution.py:825
  254.4 19.8 %collective-permute-start.33 = (f32[192]{0:T(256)S(1)}, f32[192]{0:T(256)S(1)}, u32[]{:S(2)}, u32[]{:S(2)}) collective-permute-start(f32[192]{0:T(256)S(1)} %bitcast.152), channel_id=1, source_target_pairs={{0,2},{1,3},{2,0},{3,1},{4,6},{5,7},{6,4},{7,5},{8,10},{9,11},{10,... | collective-permute-start | bytes 2312 | tf_op jit(solution)/shard_map/ppermute | solution.py:825
  255.9 18.3 %collective-permute-start.34 = (f32[192]{0:T(256)S(1)}, f32[192]{0:T(256)S(1)}, u32[]{:S(2)}, u32[]{:S(2)}) collective-permute-start(f32[192]{0:T(256)S(1)} %bitcast.150), channel_id=1, source_target_pairs={{0,3},{1,2},{2,1},{3,0},{4,7},{5,6},{6,5},{7,4},{8,11},{9,10},{10,... | collective-permute-start | bytes 2312 | tf_op jit(solution)/shard_map/ppermute | solution.py:825
  323.8 22.3 %collective-permute-start.35 = (bf16[192,1152]{1,0:T(8,128)(2,1)S(1)}, bf16[192,1152]{1,0:T(8,128)(2,1)S(1)}, u32[]{:S(2)}, u32[]{:S(2)}) collective-permute-start(bf16[192,1152]{1,0:T(8,128)(2,1)S(1)} %get-tuple-element.450), channel_id=1, source_target_pairs={{0,1},{1,0},{2,3},{3,2},{4,5},{5,4},{6,7},{7,6},{8,9},{9,8},{10,11... | collective-permute-start | bytes 1327112 | tf_op jit(solution)/shard_map/ppermute | solution.py:825
  324.0 22.1 %collective-permute-start.36 = (bf16[192,1152]{1,0:T(8,128)(2,1)S(1)}, bf16[192,1152]{1,0:T(8,128)(2,1)S(1)}, u32[]{:S(2)}, u32[]{:S(2)}) collective-permute-start(bf16[192,1152]{1,0:T(8,128)(2,1)S(1)} %get-tuple-element.449), channel_id=1, source_target_pairs={{0,2},{1,3},{2,0},{3,1},{4,6},{5,7},{6,4},{7,5},{8,10},{9,11},{10,... | collective-permute-start | bytes 1327112 | tf_op jit(solution)/shard_map/ppermute | solution.py:825
  325.5 20.6 %collective-permute-start.37 = (bf16[192,1152]{1,0:T(8,128)(2,1)S(1)}, bf16[192,1152]{1,0:T(8,128)(2,1)S(1)}, u32[]{:S(2)}, u32[]{:S(2)}) collective-permute-start(bf16[192,1152]{1,0:T(8,128)(2,1)S(1)} %get-tuple-element.448), channel_id=1, source_target_pairs={{0,3},{1,2},{2,1},{3,0},{4,7},{5,6},{6,5},{7,4},{8,11},{9,10},{10,... | collective-permute-start | bytes 1327112 | tf_op jit(solution)/shard_map/ppermute | solution.py:825
  327.0 19.0 %collective-permute-start.39 = (f32[192]{0:T(256)S(1)}, f32[192]{0:T(256)S(1)}, u32[]{:S(2)}, u32[]{:S(2)}) collective-permute-start(f32[192]{0:T(256)S(1)} %bitcast.153), channel_id=1, source_target_pairs={{0,2},{1,3},{2,0},{3,1},{4,6},{5,7},{6,4},{7,5},{8,10},{9,11},{10,... | collective-permute-start | bytes 2312 | tf_op jit(solution)/shard_map/ppermute | solution.py:825
  328.5 17.5 %collective-permute-start.40 = (f32[192]{0:T(256)S(1)}, f32[192]{0:T(256)S(1)}, u32[]{:S(2)}, u32[]{:S(2)}) collective-permute-start(f32[192]{0:T(256)S(1)} %bitcast.151), channel_id=1, source_target_pairs={{0,3},{1,2},{2,1},{3,0},{4,7},{5,6},{6,5},{7,4},{8,11},{9,10},{10,... | collective-permute-start | bytes 2312 | tf_op jit(solution)/shard_map/ppermute | solution.py:825
  354.6 28.2 %collective-permute-start.42 = (bf16[512,1152]{1,0:T(8,128)(2,1)S(1)}, bf16[512,1152]{1,0:T(8,128)(2,1)}, u32[]{:S(2)}, u32[]{:S(2)}) collective-permute-start(bf16[512,1152]{1,0:T(8,128)(2,1)S(1)} %get-tuple-element.296), channel_id=1, source_target_pairs={{0,2},{1,3},{2,0},{3,1},{4,6},{5,7},{6,4},{7,5},{8,10},{9,11},{10,... | collective-permute-start | bytes 3538952 | tf_op jit(solution)/shard_map/ppermute | solution.py:825
  356.0 27.3 %collective-permute-start.41 = (bf16[512,1152]{1,0:T(8,128)(2,1)S(1)}, bf16[512,1152]{1,0:T(8,128)(2,1)}, u32[]{:S(2)}, u32[]{:S(2)}) collective-permute-start(bf16[512,1152]{1,0:T(8,128)(2,1)S(1)} %get-tuple-element.296), channel_id=1, source_target_pairs={{0,1},{1,0},{2,3},{3,2},{4,5},{5,4},{6,7},{7,6},{8,9},{9,8},{10,11... | collective-permute-start | bytes 3538952 | tf_op jit(solution)/shard_map/ppermute | solution.py:825
  391.0 51.5 %collective-permute-start.44 = (bf16[4,80,1152]{2,1,0:T(8,128)(2,1)S(1)}, bf16[4,80,1152]{2,1,0:T(8,128)(2,1)S(1)}, u32[]{:S(2)}, u32[]{:S(2)}) collective-permute-start(bf16[4,80,1152]{2,1,0:T(8,128)(2,1)S(1)} %get-tuple-element.309), channel_id=1, source_target_pairs={{0,4},{4,0},{8,12},{12,8},{16,20},{20,16},{24,28},{28,24},{1,5},{5... | collective-permute-start | bytes 2211848 | tf_op jit(solution)/shard_map/ppermute | solution.py:780
  442.8 52.6 %collective-permute-start.47 = (bf16[2,80,1152]{2,1,0:T(8,128)(2,1)S(1)}, bf16[2,80,1152]{2,1,0:T(8,128)(2,1)S(1)}, u32[]{:S(2)}, u32[]{:S(2)}) collective-permute-start(bf16[2,80,1152]{2,1,0:T(8,128)(2,1)S(1)} %get-tuple-element.318), channel_id=1, source_target_pairs={{0,8},{4,12},{8,0},{12,4},{16,24},{20,28},{24,16},{28,20},{1,9},{5... | collective-permute-start | bytes 1105928 | tf_op jit(solution)/shard_map/ppermute | solution.py:780
  496.3 33.4 %collective-permute-start.50 = (bf16[4,80,1152]{2,1,0:T(8,128)(2,1)S(1)}, bf16[4,80,1152]{2,1,0:T(8,128)(2,1)S(1)}, u32[]{:S(2)}, u32[]{:S(2)}) collective-permute-start(bf16[4,80,1152]{2,1,0:T(8,128)(2,1)S(1)} %get-tuple-element.333), channel_id=1, source_target_pairs={{0,4},{4,0},{8,12},{12,8},{16,20},{20,16},{24,28},{28,24},{1,5},{5... | collective-permute-start | bytes 2211848 | tf_op jit(solution)/shard_map/ppermute | solution.py:780
  501.5 27.4 %collective-permute-start.46 = (bf16[1024,128]{1,0:T(8,128)(2,1)S(1)}, bf16[1024,128]{1,0:T(8,128)(2,1)S(1)}, u32[]{:S(2)}, u32[]{:S(2)}) collective-permute-start(bf16[1024,128]{1,0:T(8,128)(2,1)S(1)} %add.291), channel_id=1, source_target_pairs={{0,2},{1,3},{2,0},{3,1},{4,6},{5,7},{6,4},{7,5},{8,10},{9,11},{10,... | collective-permute-start | bytes 786440 | tf_op jit(solution)/shard_map/ppermute | solution.py:825
  552.3 29.2 %collective-permute-start.52 = (bf16[2,512,1152]{2,1,0:T(8,128)(2,1)}, bf16[2,512,1152]{2,1,0:T(8,128)(2,1)}, u32[]{:S(2)}, u32[]{:S(2)}) collective-permute-start(bf16[2,512,1152]{2,1,0:T(8,128)(2,1)} %pad_maximum_fusion.1), channel_id=1, source_target_pairs={{0,1},{1,0},{2,3},{3,2},{4,5},{5,4},{6,7},{7,6},{8,9},{9,8},{10,11... | collective-permute-start | bytes 7077896 | tf_op jit(solution)/shard_map/ppermute | solution.py:825
  555.8 41.8 %collective-permute-start.55 = (bf16[192,1152]{1,0:T(8,128)(2,1)}, bf16[192,1152]{1,0:T(8,128)(2,1)}, u32[]{:S(2)}, u32[]{:S(2)}) collective-permute-start(bf16[192,1152]{1,0:T(8,128)(2,1)} %get-tuple-element.444), channel_id=1, source_target_pairs={{0,1},{1,0},{2,3},{3,2},{4,5},{5,4},{6,7},{7,6},{8,9},{9,8},{10,11... | collective-permute-start | bytes 1327112 | tf_op jit(solution)/shard_map/ppermute | solution.py:825
  556.3 41.8 %collective-permute-start.56 = (bf16[192,1152]{1,0:T(8,128)(2,1)}, bf16[192,1152]{1,0:T(8,128)(2,1)}, u32[]{:S(2)}, u32[]{:S(2)}) collective-permute-start(bf16[192,1152]{1,0:T(8,128)(2,1)} %get-tuple-element.446), channel_id=1, source_target_pairs={{0,2},{1,3},{2,0},{3,1},{4,6},{5,7},{6,4},{7,5},{8,10},{9,11},{10,... | collective-permute-start | bytes 1327112 | tf_op jit(solution)/shard_map/ppermute | solution.py:825
  557.9 41.8 %collective-permute-start.57 = (bf16[192,1152]{1,0:T(8,128)(2,1)}, bf16[192,1152]{1,0:T(8,128)(2,1)}, u32[]{:S(2)}, u32[]{:S(2)}) collective-permute-start(bf16[192,1152]{1,0:T(8,128)(2,1)} %get-tuple-element.445), channel_id=1, source_target_pairs={{0,3},{1,2},{2,1},{3,0},{4,7},{5,6},{6,5},{7,4},{8,11},{9,10},{10,... | collective-permute-start | bytes 1327112 | tf_op jit(solution)/shard_map/ppermute | solution.py:825
  557.9 11.3 %collective-permute-start.51 = (bf16[2,80,1152]{2,1,0:T(8,128)(2,1)}, bf16[2,80,1152]{2,1,0:T(8,128)(2,1)S(1)}, u32[]{:S(2)}, u32[]{:S(2)}) collective-permute-start(bf16[2,80,1152]{2,1,0:T(8,128)(2,1)} %get-tuple-element.346), channel_id=1, source_target_pairs={{0,8},{4,12},{8,0},{12,4},{16,24},{20,28},{24,16},{28,20},{1,9},{5... | collective-permute-start | bytes 1105928 | tf_op jit(solution)/shard_map/ppermute | solution.py:780
  569.2 22.1 %collective-permute-start.54 = (bf16[4,80,1408]{2,1,0:T(8,128)(2,1)}, bf16[4,80,1408]{2,1,0:T(8,128)(2,1)}, u32[]{:S(2)}, u32[]{:S(2)}) collective-permute-start(bf16[4,80,1408]{2,1,0:T(8,128)(2,1)} %get-tuple-element.366), channel_id=1, source_target_pairs={{0,4},{4,0},{8,12},{12,8},{16,20},{20,16},{24,28},{28,24},{1,5},{5... | collective-permute-start | bytes 2703368 | tf_op jit(solution)/shard_map/ppermute | solution.py:780
  581.5 11.6 %collective-permute-start.63 = (bf16[1,80,1152]{2,1,0:T(8,128)(2,1)S(1)}, bf16[1,80,1152]{2,1,0:T(8,128)(2,1)S(1)}, u32[]{:S(2)}, u32[]{:S(2)}) collective-permute-start(bf16[1,80,1152]{2,1,0:T(8,128)(2,1)S(1)} %copy-done.89), channel_id=1, source_target_pairs={{0,16},{4,20},{8,24},{12,28},{16,0},{20,4},{24,8},{28,12},{1,17},{... | collective-permute-start | bytes 552968 | tf_op jit(solution)/shard_map/ppermute | solution.py:780
  593.1 16.4 %collective-permute-start.59 = (bf16[2,80,1408]{2,1,0:T(8,128)(2,1)S(1)}, bf16[2,80,1408]{2,1,0:T(8,128)(2,1)S(1)}, u32[]{:S(2)}, u32[]{:S(2)}) collective-permute-start(bf16[2,80,1408]{2,1,0:T(8,128)(2,1)S(1)} %get-tuple-element.380), channel_id=1, source_target_pairs={{0,8},{4,12},{8,0},{12,4},{16,24},{20,28},{24,16},{28,20},{1,9},{5... | collective-permute-start | bytes 1351688 | tf_op jit(solution)/shard_map/ppermute | solution.py:780
  595.3 25.8 %collective-permute-start.60 = (bf16[512,1152]{1,0:T(8,128)(2,1)S(1)}, bf16[512,1152]{1,0:T(8,128)(2,1)S(1)}, u32[]{:S(2)}, u32[]{:S(2)}) collective-permute-start(bf16[512,1152]{1,0:T(8,128)(2,1)S(1)} %fusion.32), channel_id=1, source_target_pairs={{0,2},{1,3},{2,0},{3,1},{4,6},{5,7},{6,4},{7,5},{8,10},{9,11},{10,... | collective-permute-start | bytes 3538952 | tf_op jit(solution)/shard_map/ppermute | solution.py:825
  597.7 27.0 %collective-permute-start.62 = (bf16[1,80,1152]{2,1,0:T(8,128)(2,1)S(1)}, bf16[1,80,1152]{2,1,0:T(8,128)(2,1)S(1)}, u32[]{:S(2)}, u32[]{:S(2)}) collective-permute-start(bf16[1,80,1152]{2,1,0:T(8,128)(2,1)S(1)} %copy-done.90), channel_id=1, source_target_pairs={{0,16},{4,20},{8,24},{12,28},{16,0},{20,4},{24,8},{28,12},{1,17},{... | collective-permute-start | bytes 552968 | tf_op jit(solution)/shard_map/ppermute | solution.py:780
  598.2 11.3 %collective-permute-start.58 = (f32[6,1152]{1,0:T(8,128)S(1)}, f32[6,1152]{1,0:T(8,128)S(1)}, u32[]{:S(2)}, u32[]{:S(2)}) collective-permute-start(f32[6,1152]{1,0:T(8,128)S(1)} %add.306), channel_id=1, source_target_pairs={{0,8},{4,12},{8,0},{12,4},{16,24},{20,28},{24,16},{28,20},{1,9},{5... | collective-permute-start | bytes 82952 | tf_op jit(solution)/shard_map/ppermute | solution.py:807
  609.7 14.9 %collective-permute-start.64 = (f32[6,1152]{1,0:T(8,128)S(1)}, f32[6,1152]{1,0:T(8,128)S(1)}, u32[]{:S(2)}, u32[]{:S(2)}) collective-permute-start(f32[6,1152]{1,0:T(8,128)S(1)} %add.309), channel_id=1, source_target_pairs={{0,16},{4,20},{8,24},{12,28},{16,0},{20,4},{24,8},{28,12},{1,17},{... | collective-permute-start | bytes 82952 | tf_op jit(solution)/shard_map/ppermute | solution.py:807
  610.6 17.1 %collective-permute-start.61 = (bf16[1,80,1408]{2,1,0:T(8,128)(2,1)S(1)}, bf16[1,80,1408]{2,1,0:T(8,128)(2,1)S(1)}, u32[]{:S(2)}, u32[]{:S(2)}) collective-permute-start(bf16[1,80,1408]{2,1,0:T(8,128)(2,1)S(1)} %get-tuple-element.391), channel_id=1, source_target_pairs={{0,16},{4,20},{8,24},{12,28},{16,0},{20,4},{24,8},{28,12},{1,17},{... | collective-permute-start | bytes 675848 | tf_op jit(solution)/shard_map/ppermute | solution.py:780
  (131 other events, 1603.3 us)
Sparse Core Ops, SparseCore 0:
  63.7 205.2 all-gather.1
  322.3 228.3 reduce-scatter.1

commit v4 on v3

--- a/solution.py
+++ b/solution.py
@@ -313,7 +313,7 @@
 def scan_bwd_kernel(
     dmix_ref, out_w_ref, s_ref, before_ref, edge_ref, act_ref, gate_ref, xlin_ref, scanned_ref, sel_ref, chan_ref, delta_w_ref, q_ref,
     dgate_ref, dact_ref, ddl_ref, dsel_ref, gch_ref, qend_ref,
-    qscr, dscr, uscr, dyscr, lbscr, wsscr, bts, cts, blocks, rows_b, rows_c, *bufs, T, g, opens
+    qscr, dscr, uscr, dyscr, lbscr, wsscr, bts, cts, blocks, rows_b, rows_c, part_b, part_c, *bufs, T, g, opens
 ):
     C = act_ref.shape[1]
     NCH = T // SUBT
@@ -348,17 +348,16 @@
         first = jnp.where(step == g - 1, edge_ref[...], first)
 
     def lanes_summed(partial):
-        return (dotf(ones, partial[...].astype(bf16), ((1,), (1,))) * mask).astype(bf16)
+        return (dotf(ones, partial, ((1,), (1,))) * mask).astype(bf16)
 
     blocks[...] = blocked_all(sel_ref, eb, T)
 
     def one(k, q, acc, cur, prev):
         kp = jnp.minimum(k + 1, NCH - 1)
-        lam_ref, w_ref, pb_ref, pc_ref = prev
+        lam_ref, w_ref = prev
         lamb = dotf(blocks[kp], lam_ref[...])
         wsum = dotf(halves, w_ref[...])
-        sum_b, sum_c = lanes_summed(pb_ref), lanes_summed(pc_ref)
-        lam_ref, w_ref, pb_ref, pc_ref = cur
+        lam_ref, w_ref = cur
         bt = bts[k]
         ct = cts[k]
         s_t = s_ref[k, last, :].astype(f32)
@@ -371,8 +370,8 @@
             lam = jnp.broadcast_to(ct[:, t : t + 1], (NST, C)) * dyr + q
             lam_ref[t * NST : t * NST + NST, :] = lam.astype(bf16)
             q = jnp.exp2(d * nrate) * lam
-            pc_ref[t * NST : t * NST + NST, :] = fold(s_t * dyr)
-            pb_ref[t * NST : t * NST + NST, :] = fold(lam * u)
+            part_c[k, t * NST : t * NST + NST, :] = fold(s_t * dyr).astype(bf16)
+            part_b[k, t * NST : t * NST + NST, :] = fold(lam * u).astype(bf16)
             s_p = s_ref[k, t * NST - NST : t * NST, :].astype(f32) if t > 0 else s_before
             wr = q * s_p * nrate
             part = wr[0 : NST // 2] + wr[NST // 2 :]
@@ -384,23 +383,26 @@
             s_t = s_p
         lbscr[kp] = lamb
         wsscr[kp] = wsum
-        rows_b[kp] = sum_b
-        rows_c[kp] = sum_c
         return q, acc
 
     def pair(j, carry):
         k = NCH - 1 - 2 * j
-        carry = one(k, *carry, bufs[0:4], bufs[4:8])
-        return one(k - 1, *carry, bufs[4:8], bufs[0:4])
-
-    for ref in bufs[4:8]:
+        carry = one(k, *carry, bufs[0:2], bufs[2:4])
+        return one(k - 1, *carry, bufs[2:4], bufs[0:2])
+
+    for ref in bufs[2:4]:
         ref[...] = jnp.zeros_like(ref)
     q, acc = lax.fori_loop(0, NCH // 2, pair, (qscr[...], jnp.zeros((NST, C), f32)))
-    lam_ref, w_ref, pb_ref, pc_ref = bufs[4:8]
+    lam_ref, w_ref = bufs[2:4]
     lbscr[0] = dotf(blocks[0], lam_ref[...])
     wsscr[0] = dotf(halves, w_ref[...])
-    rows_b[0] = lanes_summed(pb_ref)
-    rows_c[0] = lanes_summed(pc_ref)
+
+    def sums(k, _):
+        rows_b[k] = lanes_summed(part_b[k])
+        rows_c[k] = lanes_summed(part_c[k])
+        return 0
+
+    lax.fori_loop(0, NCH, sums, 0, unroll=4)
     qscr[...] = q
     qend_ref[...] = q
     gch_ref[CONV + 3 : CONV + 3 + NST, :] += acc * (1.0 / LOG2E)
@@ -443,7 +445,8 @@
             SHAPE((24, C), f32), SHAPE((NST, C), f32),
         ],
         scratch_shapes=[vm((NST, C), f32)] + [vm((nch, SUBT, C), f32)] * 5 + [vm((nch, NST, SUBT), f32)] * 2 + [vm((nch, SUBT, SUBT * NST), bf16)] * 3
-        + [vm((SUBT * NST, C), bf16), vm((SUBT * NST // 2, C), bf16), vm((SUBT * NST, LANES), f32), vm((SUBT * NST, LANES), f32)] * 2,
+        + [vm((nch, SUBT * NST, LANES), bf16)] * 2
+        + [vm((SUBT * NST, C), bf16), vm((SUBT * NST // 2, C), bf16)] * 2,
         compiler_params=params(56),
         cost_estimate=cost(),
     )(dmix, out_w, s_all, s_all, edge, act, gate, xlin, scanned, sel, chan, delta_w, q)
@@ -763,6 +766,17 @@
     return owners[lax.axis_index(axis)], first, [second[-r % n] for r in range(n)]
 
 
+def land(results, sums, *arrived):
+    results = list(results)
+    coming = [got for one in sums for got in one.arriving()]
+    all_of = list(tie(*results, *arrived, *coming))
+    at = len(results)
+    coming = all_of[at + len(arrived) :]
+    for one in sums:
+        one.add(coming)
+    return all_of[:at], all_of[at : at + len(arrived)]
+
+
 class HalvingSum:
     def __init__(self, value, axis):
         self.axis, self.n, self.me = axis, lax.axis_size(axis), lax.axis_index(axis)
@@ -780,18 +794,20 @@
             self.got = lax.ppermute(send, self.axis, [(i, i ^ self.bit) for i in range(self.n)])
         return token
 
-    def land(self, token):
+    def arriving(self):
+        return [self.got] if self.sent else []
+
+    def add(self, arrived):
         if self.sent:
             self.sent = False
-            keep, token = tie(self.keep, token)
-            self.value = (keep.astype(f32) + self.got.astype(f32)).astype(bf16)
+            self.value = (self.keep.astype(f32) + arrived.pop(0).astype(f32)).astype(bf16)
             self.bit *= 2
-        return token
 
     def finish(self):
         while self.bit < self.n:
-            token = jnp.zeros((1,), f32)
-            self.land(token if self.sent else self.launch(token))
+            if not self.sent:
+                self.launch(jnp.zeros((1,), f32))
+            self.add(self.arriving())
         return self.value[0]
 
 
@@ -807,16 +823,19 @@
             self.got = lax.ppermute(value, self.axis, [(i, i ^ self.bit) for i in range(self.n)])
         return token
 
-    def land(self, token):
+    def arriving(self):
+        return [] if self.got is None else [self.got]
+
+    def add(self, arrived):
         if self.got is not None:
-            value, token = tie(self.value, token)
-            self.value, self.got = value + self.got, None
+            self.value, self.got = self.value + arrived.pop(0), None
             self.bit *= 2
-        return token
 
     def finish(self):
         while self.bit < self.n:
-            self.land(self.launch(jnp.zeros((1,), f32)))
+            if self.got is None:
+                self.launch(jnp.zeros((1,), f32))
+            self.add(self.arriving())
         return self.value
 
 
@@ -940,17 +959,23 @@
 
     count = seq.shape[0] // 2
     conv_tail, state = jnp.zeros((8, wide), f32), jnp.zeros((NST, wide), f32)
-    convs, scans, selections = [], [], []
-    for h in range(2):
-        convs.append(conv_fwd(seq, h * count, count, w_in, chan, selw, conv_tail))
-        conv_tail = convs[-1][6]
-        selections.append(sum_mp(convs[-1][5]))
+    convs, scans = [None] * 2, [None] * 2
+    convs[0] = list(conv_fwd(seq, 0, count, w_in, chan, selw, conv_tail))
+    pair = convs[0][5] + swap(convs[0][5], 1)
+    pair, conv_tail = tie(pair, convs[0][6])
+    other = swap(pair, 2)
+    convs[1], (other,) = land(conv_fwd(seq, count, count, w_in, chan, selw, conv_tail), [], other)
+    selections = [pair + other]
+    pair = convs[1][5] + swap(convs[1][5], 1)
+    pair, state = tie(pair, state)
+    other = swap(pair, 2)
     edges = [state]
-    for h in range(2):
-        conv_in, gate_in, pre, act, act_b, _, _ = convs[h]
-        scans.append(scan_fwd(selections[h], delta_w, act, gate_in, chan, out_w, state))
-        state = scans[-1][6]
-        edges.append(state)
+    scans[0], (other,) = land(
+        scan_fwd(selections[0], delta_w, convs[0][3], convs[0][1], chan, out_w, state), [], other
+    )
+    selections.append(pair + other)
+    edges.append(scans[0][6])
+    scans[1] = scan_fwd(selections[1], delta_w, convs[1][3], convs[1][1], chan, out_w, edges[1])
     near, far = scatter_far(*scatter_near([s[4].reshape(2, tok_rows, width) for s in scans]))
     far = swap(far, 2)
     residual, probs, gate_prob, outgoing, prob_slots = route_tokens(
@@ -965,9 +990,6 @@
         experts_all,
     )
     portion = in_order(gather_mp_blocks(d_mixer))
-    expert_out, portion = tie(expert_out, portion)
-    returned = exchange(expert_out)
-
     def both(left, right):
         return contract_rows(left[0], right[:count]) + contract_rows(left[1], right[count:])
 
@@ -977,54 +999,67 @@
     by_owner = lambda a: HalvingSum(cut(a).reshape(ring, slot, -1), "dp")
     out_sum = by_owner(both([s[3] for s in scans], portion).astype(bf16))
     q, later = jnp.zeros((NST, wide), f32), jnp.zeros((8, wide), f32)
+
+    def run_scan(h, q):
+        kept = scans[h][0], convs[h][3], convs[h][1], scans[h][1], scans[h][2]
+        return scan_bwd(portion, h * count, 0, kept, edges[h], q, count, out_w, selections[h], chan, delta_w)
+
     tails, sums = [None] * 2, [None] * 2
-    for h in (1, 0):
-        kept = scans[h][0], convs[h][3], convs[h][1], scans[h][1], scans[h][2]
-        q = out_sum.launch(q)
-        tails[h] = scan_bwd(portion, h * count, 0, kept, edges[h], q, count, out_w, selections[h], chan, delta_w)
-        q = out_sum.land(tails[h][5])
-        sums[h] = sum_mp(tails[h][3])
+    expert_out, q = tie(expert_out, out_sum.launch(q))
+    returned = exchange(expert_out)
+    tails[1], returned[1:] = land(run_scan(1, q), [out_sum], *returned[1:])
+    pair = tails[1][3] + swap(tails[1][3], 1)
+    pair, q = tie(pair, out_sum.launch(tails[1][5]))
+    other = swap(pair, 2)
+    tails[0], (other,) = land(run_scan(0, q), [out_sum], other)
+    sums[1] = pair + other
+    pair = tails[0][3] + swap(tails[0][3], 1)
     gate_sum = by_owner(both([t[0] for t in tails], seq).astype(bf16))
-    grads, gch = None, jnp.zeros((8, wide), f32)
     tail_sum = tails[0][4] + tails[1][4]
-    dnorms, gains = [None] * 2, [None] * 2
-    for h in (1, 0):
-        later = gate_sum.launch(out_sum.launch(later))
-        dnorms[h], gains[h], later, gch, grads = conv_bwd(
+    pair, later = tie(pair, gate_sum.launch(out_sum.launch(later)))
+    other = swap(pair, 2)
+
+    def run_conv(h, later, gch, grads):
+        return conv_bwd(
             h * count, count, h == 0, tails[h][1], sums[h], selw, convs[h][2], convs[h][0], tails[h][0], w_in, seq,
             chan, later, convs[h][4], tails[h][2], scans[h][5], grads, gch, tail_sum,
         )
-        later = gate_sum.land(out_sum.land(later))
-    conv_sum = by_owner(grads)
+
+    backs = [None] * 2
+    backs[1], (other,) = land(run_conv(1, later, jnp.zeros((8, wide), f32), None), [out_sum, gate_sum], other)
+    sums[0] = pair + other
+    later = gate_sum.launch(backs[1][2])
+    backs[0] = run_conv(0, later, backs[1][3], backs[1][4])
+    later = backs[0][2]
     factor = 1.0 / math.sqrt(tok_rows * ring * peers)
-    gain_part = (gains[0][:1] + gains[1][:1]) / norm_gains[:1]
+
+    conv_sum = by_owner(backs[0][4])
+    near = scatter_near([b[0].reshape(2, tok_rows, width) for b in backs])
+    gain_part = (backs[0][1][:1] + backs[1][1][:1]) / norm_gains[:1]
     shared = SharedSum(jnp.concatenate([gain_part, parts[:1], parts[8 : 8 + experts_all]]), "dp")
-    near = scatter_near([d.reshape(2, tok_rows, width) for d in dnorms])
-    later = gate_sum.launch(conv_sum.launch(later))
-    later, experts_grad = tie(shared.launch(later), experts_grad)
+    later = shared.launch(conv_sum.launch(later))
+    near[0], near[1], experts_grad, later = tie(near[0], near[1], experts_grad, later)
     up_new, down_new = experts_step(
         experts_grad,
         (expert_up, upward_velocity, upward_average),
         (expert_down, downward_velocity, downward_average),
         factor,
     )
-    later, up_new[3], near[2] = tie(later, up_new[3], near[2])
+    (up_new[3], later), (near[2],) = land([up_new[3], later], [], near[2])
     near, far_send = scatter_far(*near)
     far_send, later = tie(far_send, later)
     far = swap(far_send, 2)
-    later = shared.land(gate_sum.land(conv_sum.land(later)))
-    later, returned[0] = tie(shared.launch(conv_sum.launch(later)), returned[0])
+    (later,), _ = land([later], [conv_sum, gate_sum, shared])
+    later, returned[0] = tie(shared.launch(gate_sum.launch(conv_sum.launch(later))), returned[0])
     tokens_out = contract_rows(dispatch, jnp.concatenate(returned))
     block_output = (residual + gate_prob[:, :1] * tokens_out).astype(bf16)
-    later, block_output = tie(later, block_output)
-    later = shared.land(conv_sum.land(later))
+    (block_output, later), _ = land([block_output, later], [conv_sum, gate_sum, shared])
     later, far = tie(shared.launch(conv_sum.launch(later)), far)
     d_normed = near + far.astype(f32)
     a1 = norm_gains[0] * d_normed
     hat1 = source * scale1
     block_grad = d_residual + scale1 * (a1 - hat1 * jnp.mean(a1 * hat1, axis=-1, keepdims=True))
-    later, block_grad = tie(later, block_grad)
-    later = shared.land(conv_sum.land(later))
+    (block_grad, later), _ = land([block_grad, later], [conv_sum, shared])
     shared = sum_mp(shared.finish())
     mixer_new = mixer_step(
         conv_sum.finish(),

time: 648 us -> 633 us (0.977)
  waiting for transfers between devices: 195 us -> 176 us
    ppermute x41, waiting for transfers between devices: 120 us -> 105 us  [swap(): return lax.ppermute(value, 'mp', [(i, i ^ j) for i in range(n)])]
    ppermute x9, waiting for transfers between devices: 14.2 us -> 1.7 us  [launch(): lax.ppermute(send, self.axis, [(i, i ^ self.bit) for i in range(self.n)])]
    unnamed x224 -> x232, local copies, waits for them, and re-layouts: 22.6 us -> 23.4 us
  transfers between devices with their start and end apart: 69 -> 69, of which waited for: 23 -> 26; matrix products, arithmetic and copies ran while one was open for 13% -> 13% of each run, Pallas kernels for 33% -> 34%
where the time goes in v4:
time: 633 us; the launch traced here: 627 us
  Pallas kernels  263 us (42%)
  waiting for transfers between devices  176 us (28%)
  starting transfers between devices  65.3 us (10%)
  local copies, waits for them, and re-layouts  54.6 us (9%)
  other arithmetic  35.1 us (6%)
  matrix products  17.6 us (3%)
  between operations  15.7 us (2%)
    ppermute x41, waiting for transfers between devices, swap(): return lax.ppermute(value, 'mp', [(i, i ^ j) for i in range(n)])  105 us
    pallas_call x2, Pallas kernels, scan_bwd(): pl.pallas_call(functools.partial(scan_bwd_kernel, T=T, g=g, opens=low ==...  90.5 us
    pallas_call x1, Pallas kernels, experts(): pl.pallas_call(functools.partial(experts_kernel, steps=steps, per=per, un...  47 us
    ppermute x7, waiting for transfers between devices, ring_gather(): first.append(lax.ppermute(first[-1], axis, ahead))  41.1 us
    pallas_call x2, Pallas kernels, scan_fwd(): pl.pallas_call(functools.partial(scan_fwd_kernel, T=T), grid=(g,), in_spe...  40.1 us
    pallas_call x2, Pallas kernels, conv_bwd(): pl.pallas_call(functools.partial(conv_bwd_kernel, T=T, g=g, opens=opens,...  36 us
    ppermute x41, starting transfers between devices, swap(): return lax.ppermute(value, 'mp', [(i, i ^ j) for i in range(n)])  29.2 us
    unnamed x232, local copies, waits for them, and re-layouts  23.4 us
  transfers between devices with their start and end apart: 69, of which 26 were waited for; matrix products, arithmetic and copies ran while one was open for 13% of the time, Pallas kernels for 34%

profile of v4, /device:TPU:0, one launch (start us, length us, event | category | flops | bytes accessed | tf_op | source)
XLA Modules:
  0.0 626.8 jit_solution(13652338878561891312)
XLA Ops:
  13.6 3.0 collective-permute-start.2
  19.4 6.2 collective-permute-done.refs_1_
  28.8 5.2 collective-permute-done.3.refs_2_
  38.2 5.3 collective-permute-done.6.refs_3_
  46.1 2.4 convolution_convert_fusion
  48.6 6.4 %collective-permute-done.9.refs_4_ = bf16[72,1792]{1,0:T(8,128)(2,1)S(1)} collective-permute-done((bf16[72,1792]{1,0:T(8,128)(2,1)S(1)}, bf16[72,1792]{1,0:T(8,128)(2,1)S(1)}, u32[]{:S(2)}, u32[]{:S(2)}) %collective-permute-start.9) | collective-permute-done | bytes 258080 | tf_op jit(solution)/shard_map/ppermute | solution.py:762
  57.7 4.2 collective-permute-done.12.refs_5_
  70.7 2.5 fusion.53
  77.2 2.4 bitcast_dynamic-update-slice_fusion.6
  79.8 2.6 bitcast_dynamic-update-slice_fusion.5
  82.3 7.8 %collective-permute-done.19.refs_6_ = bf16[72,1792]{1,0:T(8,128)(2,1)S(1)} collective-permute-done((bf16[72,1792]{1,0:T(8,128)(2,1)S(1)}, bf16[72,1792]{1,0:T(8,128)(2,1)S(1)}, u32[]{:S(2)}, u32[]{:S(2)}) %collective-permute-start.19) | collective-permute-done | bytes 258080 | tf_op jit(solution)/shard_map/ppermute | solution.py:762
  90.1 6.4 %collective-permute-start.20 = (bf16[72,1792]{1,0:T(8,128)(2,1)S(1)}, bf16[72,1792]{1,0:T(8,128)(2,1)S(1)}, u32[]{:S(2)}, u32[]{:S(2)}) collective-permute-start(bf16[72,1792]{1,0:T(8,128)(2,1)S(1)} %collective-permute-done.19.refs_6_), channel_id=1, source_target_pairs={{0,8},{8,16},{16,24},{24,28},{28,20},{20,12},{12,4},{4,0},{1,9},{9... | collective-permute-start | bytes 774152 | tf_op jit(solution)/shard_map/ppermute | solution.py:762
  98.9 2.4 bitcast_dynamic-update-slice_fusion.4
  101.3 6.1 collective-permute-done.20.refs_7_
  107.4 11.1 %collective-permute-done.22.refs_9_ = bf16[72,1920]{1,0:T(8,128)(2,1)S(1)} collective-permute-done((bf16[72,1920]{1,0:T(8,128)(2,1)S(1)}, bf16[72,1920]{1,0:T(8,128)(2,1)S(1)}, u32[]{:S(2)}, u32[]{:S(2)}) %collective-permute-start.22) | collective-permute-done | bytes 276512 | tf_op jit(solution)/shard_map/ppermute | solution.py:763
  118.7 2.8 shard_map.600
  121.6 9.7 %shard_map.601 = (f32[1024,640]{1,0:T(8,128)S(1)}, f32[1024,640]{1,0:T(8,128)}, f32[1024,640]{1,0:T(8,128)}, f32[1024,640]{1,0:T(8,128)}, bf16[1024,640]{1,0:T(8...) custom-call(bf16[2048,1152]{1,0:T(8,128)(2,1)} %bitcast.147, bf16[1280,1152]{1,0:T(8,128)(2,1)} %get-tuple-element.306.w_ref, ...), custom_call_target="tpu_custom_call" | custom-call | bytes 1048576 | tf_op jit(solution)/shard_map/pallas_call | solution.py:218
  136.3 9.1 %shard_map.602 = (f32[1024,640]{1,0:T(8,128)S(1)}, f32[1024,640]{1,0:T(8,128)}, f32[1024,640]{1,0:T(8,128)}, f32[1024,640]{1,0:T(8,128)}, bf16[1024,640]{1,0:T(8...) custom-call(bf16[2048,1152]{1,0:T(8,128)(2,1)} %bitcast.148, bf16[1280,1152]{1,0:T(8,128)(2,1)} %get-tuple-element.306.w_ref, ...), custom_call_target="tpu_custom_call" | custom-call | bytes 1048576 | tf_op jit(solution)/shard_map/pallas_call | solution.py:218
  154.2 19.9 %shard_map.603 = (bf16[64,256,640]{2,1,0:T(8,128)(2,1)}, f32[1024,640]{1,0:T(8,128)}, f32[1024,640]{1,0:T(8,128)}, bf16[1024,640]{1,0:T(8,128)(2,1)S(1)}, bf16[1...) custom-call(f32[1024,128]{1,0:T(8,128)S(1)} %add.266.sel_ref, ...), custom_call_target="tpu_custom_call" | custom-call | bytes 1048576 | tf_op jit(solution)/shard_map/pallas_call | solution.py:288
  177.2 20.2 %shard_map.604 = (bf16[64,256,640]{2,1,0:T(8,128)(2,1)}, f32[1024,640]{1,0:T(8,128)}, f32[1024,640]{1,0:T(8,128)}, bf16[1024,640]{1,0:T(8,128)(2,1)S(1)}, bf16[1...) custom-call(f32[1024,128]{1,0:T(8,128)S(1)} %add.270.sel_ref, ...), custom_call_target="tpu_custom_call" | custom-call | bytes 1048576 | tf_op jit(solution)/shard_map/pallas_call | solution.py:288
  197.5 2.4 dynamic-slice_select_fusion.3
  201.6 4.7 collective-permute-done.27
  206.7 2.5 fusion.32
  212.3 25.1 %collective-permute-done.28.far_ref = bf16[512,1152]{1,0:T(8,128)(2,1)S(1)} collective-permute-done((bf16[512,1152]{1,0:T(8,128)(2,1)}, bf16[512,1152]{1,0:T(8,128)(2,1)S(1)}, u32[]{:S(2)}, u32[]{:S(2)}) %collective-permute-start.28) | collective-permute-done | bytes 1179680 | tf_op jit(solution)/shard_map/ppermute | solution.py:844
  237.4 5.5 shard_map.605
  247.7 18.3 %collective-permute-done.33 = f32[192]{0:T(256)S(1)} collective-permute-done((f32[192]{0:T(256)S(1)}, f32[192]{0:T(256)S(1)}, u32[]{:S(2)}, u32[]{:S(2)}) %collective-permute-start.33) | collective-permute-done | bytes 800 | tf_op jit(solution)/shard_map/ppermute | solution.py:844
  266.1 2.9 all-gather.2.cloned.1.call-done.w_ref
  269.6 47.0 %shard_map.607 = (bf16[768,1152]{1,0:T(8,128)(2,1)}, bf16[768,1152]{1,0:T(8,128)(2,1)}, f32[8,768]{1,0:T(8,128)}, bf16[6144,1152]{1,0:T(8,128)(2,1)}) custom-call(bf16[192,1152]{1,0:T(8,128)(2,1)} %get-tuple-element.531.x0, bf16[192,1152]{1,0:T(8,128)(2,1)} %copy-done.84, bf16[192,1152]{1,0:T(8,128)(2,1)} %copy-done.85, ...), custom_call_target="tpu_custom_call" | custom-call | bytes 1048576 | tf_op jit(solution)/shard_map/pallas_call | solution.py:586
  323.7 16.8 %collective-permute-done.39 = f32[192]{0:T(256)S(1)} collective-permute-done((f32[192]{0:T(256)S(1)}, f32[192]{0:T(256)S(1)}, u32[]{:S(2)}, u32[]{:S(2)}) %collective-permute-start.39) | collective-permute-done | bytes 800 | tf_op jit(solution)/shard_map/ppermute | solution.py:844
  340.6 7.8 %shard_map.608 = (f32[512,1152]{1,0:T(8,128)}, bf16[512,1152]{1,0:T(8,128)(2,1)S(1)}, f32[16,1152]{1,0:T(8,128)S(1)}) custom-call(bf16[192,1152]{1,0:T(8,128)(2,1)S(1)} %get-tuple-element.527.r0, bf16[192,1152]{1,0:T(8,128)(2,1)S(1)} %collective-permute-done.35.r1, bf16[192,1152]{1,0:T(8,128)(2,1)S(1)} %collective-permute-done.36.r2, ...), custom_call_target="tpu_custom_call" | custom-call | bytes 1048576 | tf_op jit(solution)/shard_map/pallas_call | solution.py:656
  350.6 26.7 %collective-permute-done.42 = bf16[512,1152]{1,0:T(8,128)(2,1)} collective-permute-done((bf16[512,1152]{1,0:T(8,128)(2,1)S(1)}, bf16[512,1152]{1,0:T(8,128)(2,1)}, u32[]{:S(2)}, u32[]{:S(2)}) %collective-permute-start.42) | collective-permute-done | bytes 1179680 | tf_op jit(solution)/shard_map/ppermute | solution.py:844
  391.6 45.4 %shard_map.609 = (bf16[1024,640]{1,0:T(8,128)(2,1)}, f32[1024,640]{1,0:T(8,128)}, bf16[1024,640]{1,0:T(8,128)(2,1)}, bf16[1024,128]{1,0:T(8,128)(2,1)}, f32[24,640]{1,0:T(8,128)}, /*index=5*/f32[16,640]{1,0:T(8,128)}) custom-call(bf16[2048,1152]{1,0:T(8,128)(2,1)} %bitcast.155, bf16[640,1152]{1,0:T(8,128)(2,1)} %copy-done.1, ...), custom_call_target="tpu_custom_call" | custom-call | bytes 1048576 | tf_op jit(solution)/shard_map/pallas_call | solution.py:432
  440.8 3.5 fusion.18
  444.3 45.1 %shard_map.610 = (bf16[1024,640]{1,0:T(8,128)(2,1)}, f32[1024,640]{1,0:T(8,128)}, bf16[1024,640]{1,0:T(8,128)(2,1)}, bf16[1024,128]{1,0:T(8,128)(2,1)}, f32[24,640]{1,0:T(8,128)}, /*index=5*/f32[16,640]{1,0:T(8,128)}) custom-call(bf16[2048,1152]{1,0:T(8,128)(2,1)} %bitcast.156, bf16[640,1152]{1,0:T(8,128)(2,1)} %copy-done.1, ...), custom_call_target="tpu_custom_call" | custom-call | bytes 1048576 | tf_op jit(solution)/shard_map/pallas_call | solution.py:432
  490.3 4.2 fusion.1
  502.4 18.0 %shard_map.611 = (bf16[1024,1152]{1,0:T(8,128)(2,1)}, f32[8,1152]{1,0:T(8,128)}, f32[8,640]{1,0:T(8,128)}, f32[8,640]{1,0:T(8,128)}, f32[640,1408]{1,0:T(8,128)}) custom-call(f32[1024,640]{1,0:T(8,128)} %get-tuple-element.392.dact_ref, bf16[1024,128]{1,0:T(8,128)(2,1)} %add.294.dsel_ref, bf16[640,128]{1,0:T(8,128)(2,1)} %copy-done.10, ...), custom_call_target="tpu_custom_call" | custom-call | bytes 1048576 | tf_op jit(solution)/shard_map/pallas_call | solution.py:519
  523.8 18.0 %shard_map.612 = (bf16[1024,1152]{1,0:T(8,128)(2,1)}, f32[8,1152]{1,0:T(8,128)}, f32[8,640]{1,0:T(8,128)}, f32[8,640]{1,0:T(8,128)}, bf16[640,1408]{1,0:T(8,128)(2,1)}) custom-call(f32[1024,640]{1,0:T(8,128)} %get-tuple-element.384.dact_ref, bf16[1024,128]{1,0:T(8,128)(2,1)} %add.296.dsel_ref, bf16[640,128]{1,0:T(8,128)(2,1)} %copy-done.10, ...), custom_call_target="tpu_custom_call" | custom-call | bytes 1048576 | tf_op jit(solution)/shard_map/pallas_call | solution.py:519
  541.9 4.3 dynamic-slice_select_fusion.1
  550.3 2.2 dynamic-slice_bitcast_fusion
  558.6 8.3 %shard_map.613 = (f32[1,1152,384]{2,1,0:T(8,128)}, f32[1,1152,384]{2,1,0:T(8,128)}, f32[1,1152,384]{2,1,0:T(8,128)}, bf16[1,1152,384]{2,1,0:T(8,128)(2,1)}, f32[...) custom-call(bf16[768,1152]{1,0:T(8,128)(2,1)S(1)} %copy-done.2, ...), custom_call_target="tpu_custom_call" | custom-call | bytes 1048576 | tf_op jit(solution)/shard_map/pallas_call | solution.py:727
  569.4 6.6 %collective-permute-done.58 = f32[6,1152]{1,0:T(8,128)} collective-permute-done((f32[6,1152]{1,0:T(8,128)S(1)}, f32[6,1152]{1,0:T(8,128)}, u32[]{:S(2)}, u32[]{:S(2)}) %collective-permute-start.58) | collective-permute-done | bytes 27680 | tf_op jit(solution)/shard_map/ppermute | solution.py:823
  580.3 5.1 collective-permute-start.60
  585.5 3.6 add_convert_fusion
  589.1 5.1 collective-permute-done.61
  594.3 3.7 collective-permute-start.63
  598.1 7.1 %collective-permute-done.62 = bf16[512,1152]{1,0:T(8,128)(2,1)S(1)} collective-permute-done((bf16[512,1152]{1,0:T(8,128)(2,1)S(1)}, bf16[512,1152]{1,0:T(8,128)(2,1)S(1)}, u32[]{:S(2)}, u32[]{:S(2)}) %collective-permute-start.62) | collective-permute-done | bytes 1179680 | tf_op jit(solution)/shard_map/ppermute | solution.py:844
  606.1 2.4 fusion.9
  613.1 4.1 shard_map.614
  (432 shorter events, 128.8 us)
Async XLA Ops:
  7.2 261.8 %all-gather.2.cloned.1.call-start = ((), (), s32[]{:S(2)}) async-start(), calls=%async_computation.1 | async-start | bytes 15925248 | tf_op jit(solution)/shard_map/all_gather | solution.py:948
  13.6 12.4 %collective-permute-start.2 = (bf16[128,1152]{1,0:T(8,128)(2,1)S(1)}, bf16[128,1152]{1,0:T(8,128)(2,1)S(1)}, u32[]{:S(2)}, u32[]{:S(2)}) collective-permute-start(bf16[128,1152]{1,0:T(8,128)(2,1)S(1)} %get-tuple-element.276), channel_id=1, source_target_pairs={{0,2},{1,3},{2,0},{3,1},{4,6},{5,7},{6,4},{7,5},{8,10},{9,11},{10,... | collective-permute-start | bytes 884744 | tf_op jit(solution)/shard_map/ppermute | solution.py:844
  25.5 9.9 %collective-permute-start.5 = (bf16[128,1152]{1,0:T(8,128)(2,1)S(1)}, bf16[128,1152]{1,0:T(8,128)(2,1)S(1)}, u32[]{:S(2)}, u32[]{:S(2)}) collective-permute-start(bf16[128,1152]{1,0:T(8,128)(2,1)S(1)} %get-tuple-element.281), channel_id=1, source_target_pairs={{0,2},{1,3},{2,0},{3,1},{4,6},{5,7},{6,4},{7,5},{8,10},{9,11},{10,... | collective-permute-start | bytes 884744 | tf_op jit(solution)/shard_map/ppermute | solution.py:844
  34.0 10.1 %collective-permute-start.8 = (bf16[128,1152]{1,0:T(8,128)(2,1)S(1)}, bf16[128,1152]{1,0:T(8,128)(2,1)S(1)}, u32[]{:S(2)}, u32[]{:S(2)}) collective-permute-start(bf16[128,1152]{1,0:T(8,128)(2,1)S(1)} %get-tuple-element.286), channel_id=1, source_target_pairs={{0,2},{1,3},{2,0},{3,1},{4,6},{5,7},{6,4},{7,5},{8,10},{9,11},{10,... | collective-permute-start | bytes 884744 | tf_op jit(solution)/shard_map/ppermute | solution.py:844
  43.6 11.3 %collective-permute-start.11 = (bf16[128,1152]{1,0:T(8,128)(2,1)S(1)}, bf16[128,1152]{1,0:T(8,128)(2,1)S(1)}, u32[]{:S(2)}, u32[]{:S(2)}) collective-permute-start(bf16[128,1152]{1,0:T(8,128)(2,1)S(1)} %get-tuple-element.289), channel_id=1, source_target_pairs={{0,2},{1,3},{2,0},{3,1},{4,6},{5,7},{6,4},{7,5},{8,10},{9,11},{10,... | collective-permute-start | bytes 884744 | tf_op jit(solution)/shard_map/ppermute | solution.py:844
  44.0 10.9 %collective-permute-start.10 = (bf16[72,1920]{1,0:T(8,128)(2,1)S(1)}, bf16[72,1920]{1,0:T(8,128)(2,1)S(1)}, u32[]{:S(2)}, u32[]{:S(2)}) collective-permute-start(bf16[72,1920]{1,0:T(8,128)(2,1)S(1)} %collective-permute-done.7.refs_13_), channel_id=1, source_target_pairs={{8,0},{16,8},{24,16},{28,24},{20,28},{12,20},{4,12},{0,4},{9,1},{1... | collective-permute-start | bytes 829448 | tf_op jit(solution)/shard_map/ppermute | solution.py:763
  63.5 492.1 %reduce-scatter.2.cloned.1.call-start = ((), (), s32[]{:S(2)}) async-start(), calls=%async_computation.2 | async-start | bytes 15925248 | tf_op jit(solution)/shard_map/reduce_scatter | solution.py:986
  63.6 11.6 %collective-permute-start.14 = (bf16[512,1152]{1,0:T(8,128)(2,1)S(1)}, bf16[512,1152]{1,0:T(8,128)(2,1)}, u32[]{:S(2)}, u32[]{:S(2)}) collective-permute-start(bf16[512,1152]{1,0:T(8,128)(2,1)S(1)} %get-tuple-element.509), channel_id=1, source_target_pairs={{0,1},{1,0},{2,3},{3,2},{4,5},{5,4},{6,7},{7,6},{8,9},{9,8},{10,11... | collective-permute-start | bytes 3538952 | tf_op jit(solution)/shard_map/ppermute | solution.py:844
  73.3 28.0 %collective-permute-start.16 = (bf16[192,1152]{1,0:T(8,128)(2,1)S(1)}, bf16[192,1152]{1,0:T(8,128)(2,1)S(1)}, u32[]{:S(2)}, u32[]{:S(2)}) collective-permute-start(bf16[192,1152]{1,0:T(8,128)(2,1)S(1)} %get-tuple-element.534), channel_id=1, source_target_pairs={{0,1},{1,0},{2,3},{3,2},{4,5},{5,4},{6,7},{7,6},{8,9},{9,8},{10,11... | collective-permute-start | bytes 1327112 | tf_op jit(solution)/shard_map/ppermute | solution.py:844
  73.3 28.0 %collective-permute-start.17 = (bf16[192,1152]{1,0:T(8,128)(2,1)S(1)}, bf16[192,1152]{1,0:T(8,128)(2,1)S(1)}, u32[]{:S(2)}, u32[]{:S(2)}) collective-permute-start(bf16[192,1152]{1,0:T(8,128)(2,1)S(1)} %get-tuple-element.533), channel_id=1, source_target_pairs={{0,2},{1,3},{2,0},{3,1},{4,6},{5,7},{6,4},{7,5},{8,10},{9,11},{10,... | collective-permute-start | bytes 1327112 | tf_op jit(solution)/shard_map/ppermute | solution.py:844
  74.7 26.6 %collective-permute-start.18 = (bf16[192,1152]{1,0:T(8,128)(2,1)S(1)}, bf16[192,1152]{1,0:T(8,128)(2,1)S(1)}, u32[]{:S(2)}, u32[]{:S(2)}) collective-permute-start(bf16[192,1152]{1,0:T(8,128)(2,1)S(1)} %get-tuple-element.532), channel_id=1, source_target_pairs={{0,3},{1,2},{2,1},{3,0},{4,7},{5,6},{6,5},{7,4},{8,11},{9,10},{10,... | collective-permute-start | bytes 1327112 | tf_op jit(solution)/shard_map/ppermute | solution.py:844
  75.1 22.3 %collective-permute-start.21 = (bf16[72,1920]{1,0:T(8,128)(2,1)S(1)}, bf16[72,1920]{1,0:T(8,128)(2,1)S(1)}, u32[]{:S(2)}, u32[]{:S(2)}) collective-permute-start(bf16[72,1920]{1,0:T(8,128)(2,1)S(1)} %collective-permute-done.13.refs_11_), channel_id=1, source_target_pairs={{8,0},{16,8},{24,16},{28,24},{20,28},{12,20},{4,12},{0,4},{9,1},{1... | collective-permute-start | bytes 829448 | tf_op jit(solution)/shard_map/ppermute | solution.py:763
  75.9 14.3 %collective-permute-start.19 = (bf16[72,1792]{1,0:T(8,128)(2,1)S(1)}, bf16[72,1792]{1,0:T(8,128)(2,1)S(1)}, u32[]{:S(2)}, u32[]{:S(2)}) collective-permute-start(bf16[72,1792]{1,0:T(8,128)(2,1)S(1)} %collective-permute-done.12.refs_5_), channel_id=1, source_target_pairs={{0,8},{8,16},{16,24},{24,28},{28,20},{20,12},{12,4},{4,0},{1,9},{9... | collective-permute-start | bytes 774152 | tf_op jit(solution)/shard_map/ppermute | solution.py:762
  90.1 17.3 %collective-permute-start.20 = (bf16[72,1792]{1,0:T(8,128)(2,1)S(1)}, bf16[72,1792]{1,0:T(8,128)(2,1)S(1)}, u32[]{:S(2)}, u32[]{:S(2)}) collective-permute-start(bf16[72,1792]{1,0:T(8,128)(2,1)S(1)} %collective-permute-done.19.refs_6_), channel_id=1, source_target_pairs={{0,8},{8,16},{16,24},{24,28},{28,20},{20,12},{12,4},{4,0},{1,9},{9... | collective-permute-start | bytes 774152 | tf_op jit(solution)/shard_map/ppermute | solution.py:762
  97.5 21.1 %collective-permute-start.22 = (bf16[72,1920]{1,0:T(8,128)(2,1)S(1)}, bf16[72,1920]{1,0:T(8,128)(2,1)S(1)}, u32[]{:S(2)}, u32[]{:S(2)}) collective-permute-start(bf16[72,1920]{1,0:T(8,128)(2,1)S(1)} %collective-permute-done.21.refs_10_), channel_id=1, source_target_pairs={{8,0},{16,8},{24,16},{28,24},{20,28},{12,20},{4,12},{0,4},{9,1},{1... | collective-permute-start | bytes 829448 | tf_op jit(solution)/shard_map/ppermute | solution.py:763
  134.8 14.1 %collective-permute-start.24 = (f32[1024,128]{1,0:T(8,128)S(1)}, f32[1024,128]{1,0:T(8,128)S(1)}, u32[]{:S(2)}, u32[]{:S(2)}) collective-permute-start(f32[1024,128]{1,0:T(8,128)S(1)} %add.265), channel_id=1, source_target_pairs={{0,2},{1,3},{2,0},{3,1},{4,6},{5,7},{6,4},{7,5},{8,10},{9,11},{10,... | collective-permute-start | bytes 1572872 | tf_op jit(solution)/shard_map/ppermute | solution.py:844
  151.6 24.3 %collective-permute-start.26 = (f32[1024,128]{1,0:T(8,128)}, f32[1024,128]{1,0:T(8,128)}, u32[]{:S(2)}, u32[]{:S(2)}) collective-permute-start(f32[1024,128]{1,0:T(8,128)} %add.267), channel_id=1, source_target_pairs={{0,2},{1,3},{2,0},{3,1},{4,6},{5,7},{6,4},{7,5},{8,10},{9,11},{10,... | collective-permute-start | bytes 1572872 | tf_op jit(solution)/shard_map/ppermute | solution.py:844
  209.2 28.2 %collective-permute-start.28 = (bf16[512,1152]{1,0:T(8,128)(2,1)}, bf16[512,1152]{1,0:T(8,128)(2,1)S(1)}, u32[]{:S(2)}, u32[]{:S(2)}) collective-permute-start(bf16[512,1152]{1,0:T(8,128)(2,1)} %get-tuple-element.510), channel_id=1, source_target_pairs={{0,2},{1,3},{2,0},{3,1},{4,6},{5,7},{6,4},{7,5},{8,10},{9,11},{10,... | collective-permute-start | bytes 3538952 | tf_op jit(solution)/shard_map/ppermute | solution.py:844
  243.9 22.2 %collective-permute-start.29 = (bf16[192,1152]{1,0:T(8,128)(2,1)S(1)}, bf16[192,1152]{1,0:T(8,128)(2,1)S(1)}, u32[]{:S(2)}, u32[]{:S(2)}) collective-permute-start(bf16[192,1152]{1,0:T(8,128)(2,1)S(1)} %get-tuple-element.530), channel_id=1, source_target_pairs={{0,1},{1,0},{2,3},{3,2},{4,5},{5,4},{6,7},{7,6},{8,9},{9,8},{10,11... | collective-permute-start | bytes 1327112 | tf_op jit(solution)/shard_map/ppermute | solution.py:844
  243.9 22.2 %collective-permute-start.30 = (bf16[192,1152]{1,0:T(8,128)(2,1)S(1)}, bf16[192,1152]{1,0:T(8,128)(2,1)S(1)}, u32[]{:S(2)}, u32[]{:S(2)}) collective-permute-start(bf16[192,1152]{1,0:T(8,128)(2,1)S(1)} %get-tuple-element.529), channel_id=1, source_target_pairs={{0,2},{1,3},{2,0},{3,1},{4,6},{5,7},{6,4},{7,5},{8,10},{9,11},{10,... | collective-permute-start | bytes 1327112 | tf_op jit(solution)/shard_map/ppermute | solution.py:844
  244.6 21.5 %collective-permute-start.31 = (bf16[192,1152]{1,0:T(8,128)(2,1)S(1)}, bf16[192,1152]{1,0:T(8,128)(2,1)}, u32[]{:S(2)}, u32[]{:S(2)}) collective-permute-start(bf16[192,1152]{1,0:T(8,128)(2,1)S(1)} %get-tuple-element.528), channel_id=1, source_target_pairs={{0,3},{1,2},{2,1},{3,0},{4,7},{5,6},{6,5},{7,4},{8,11},{9,10},{10,... | collective-permute-start | bytes 1327112 | tf_op jit(solution)/shard_map/ppermute | solution.py:844
  246.2 19.8 %collective-permute-start.33 = (f32[192]{0:T(256)S(1)}, f32[192]{0:T(256)S(1)}, u32[]{:S(2)}, u32[]{:S(2)}) collective-permute-start(f32[192]{0:T(256)S(1)} %bitcast.184), channel_id=1, source_target_pairs={{0,2},{1,3},{2,0},{3,1},{4,6},{5,7},{6,4},{7,5},{8,10},{9,11},{10,... | collective-permute-start | bytes 2312 | tf_op jit(solution)/shard_map/ppermute | solution.py:844
  247.0 19.0 %collective-permute-start.34 = (f32[192]{0:T(256)S(1)}, f32[192]{0:T(256)S(1)}, u32[]{:S(2)}, u32[]{:S(2)}) collective-permute-start(f32[192]{0:T(256)S(1)} %bitcast.182), channel_id=1, source_target_pairs={{0,3},{1,2},{2,1},{3,0},{4,7},{5,6},{6,5},{7,4},{8,11},{9,10},{10,... | collective-permute-start | bytes 2312 | tf_op jit(solution)/shard_map/ppermute | solution.py:844
  318.3 22.3 %collective-permute-start.35 = (bf16[192,1152]{1,0:T(8,128)(2,1)S(1)}, bf16[192,1152]{1,0:T(8,128)(2,1)S(1)}, u32[]{:S(2)}, u32[]{:S(2)}) collective-permute-start(bf16[192,1152]{1,0:T(8,128)(2,1)S(1)} %get-tuple-element.526), channel_id=1, source_target_pairs={{0,1},{1,0},{2,3},{3,2},{4,5},{5,4},{6,7},{7,6},{8,9},{9,8},{10,11... | collective-permute-start | bytes 1327112 | tf_op jit(solution)/shard_map/ppermute | solution.py:844
  318.4 22.2 %collective-permute-start.36 = (bf16[192,1152]{1,0:T(8,128)(2,1)S(1)}, bf16[192,1152]{1,0:T(8,128)(2,1)S(1)}, u32[]{:S(2)}, u32[]{:S(2)}) collective-permute-start(bf16[192,1152]{1,0:T(8,128)(2,1)S(1)} %get-tuple-element.525), channel_id=1, source_target_pairs={{0,2},{1,3},{2,0},{3,1},{4,6},{5,7},{6,4},{7,5},{8,10},{9,11},{10,... | collective-permute-start | bytes 1327112 | tf_op jit(solution)/shard_map/ppermute | solution.py:844
  320.0 20.6 %collective-permute-start.37 = (bf16[192,1152]{1,0:T(8,128)(2,1)S(1)}, bf16[192,1152]{1,0:T(8,128)(2,1)S(1)}, u32[]{:S(2)}, u32[]{:S(2)}) collective-permute-start(bf16[192,1152]{1,0:T(8,128)(2,1)S(1)} %get-tuple-element.524), channel_id=1, source_target_pairs={{0,3},{1,2},{2,1},{3,0},{4,7},{5,6},{6,5},{7,4},{8,11},{9,10},{10,... | collective-permute-start | bytes 1327112 | tf_op jit(solution)/shard_map/ppermute | solution.py:844
  321.5 19.0 %collective-permute-start.39 = (f32[192]{0:T(256)S(1)}, f32[192]{0:T(256)S(1)}, u32[]{:S(2)}, u32[]{:S(2)}) collective-permute-start(f32[192]{0:T(256)S(1)} %bitcast.185), channel_id=1, source_target_pairs={{0,2},{1,3},{2,0},{3,1},{4,6},{5,7},{6,4},{7,5},{8,10},{9,11},{10,... | collective-permute-start | bytes 2312 | tf_op jit(solution)/shard_map/ppermute | solution.py:844
  323.0 17.6 %collective-permute-start.40 = (f32[192]{0:T(256)S(1)}, f32[192]{0:T(256)S(1)}, u32[]{:S(2)}, u32[]{:S(2)}) collective-permute-start(f32[192]{0:T(256)S(1)} %bitcast.183), channel_id=1, source_target_pairs={{0,3},{1,2},{2,1},{3,0},{4,7},{5,6},{6,5},{7,4},{8,11},{9,10},{10,... | collective-permute-start | bytes 2312 | tf_op jit(solution)/shard_map/ppermute | solution.py:844
  349.1 28.2 %collective-permute-start.42 = (bf16[512,1152]{1,0:T(8,128)(2,1)S(1)}, bf16[512,1152]{1,0:T(8,128)(2,1)}, u32[]{:S(2)}, u32[]{:S(2)}) collective-permute-start(bf16[512,1152]{1,0:T(8,128)(2,1)S(1)} %get-tuple-element.352), channel_id=1, source_target_pairs={{0,2},{1,3},{2,0},{3,1},{4,6},{5,7},{6,4},{7,5},{8,10},{9,11},{10,... | collective-permute-start | bytes 3538952 | tf_op jit(solution)/shard_map/ppermute | solution.py:844
  350.6 27.2 %collective-permute-start.41 = (bf16[512,1152]{1,0:T(8,128)(2,1)S(1)}, bf16[512,1152]{1,0:T(8,128)(2,1)}, u32[]{:S(2)}, u32[]{:S(2)}) collective-permute-start(bf16[512,1152]{1,0:T(8,128)(2,1)S(1)} %get-tuple-element.352), channel_id=1, source_target_pairs={{0,1},{1,0},{2,3},{3,2},{4,5},{5,4},{6,7},{7,6},{8,9},{9,8},{10,11... | collective-permute-start | bytes 3538952 | tf_op jit(solution)/shard_map/ppermute | solution.py:844
  388.2 48.8 %collective-permute-start.47 = (bf16[4,80,1152]{2,1,0:T(8,128)(2,1)}, bf16[4,80,1152]{2,1,0:T(8,128)(2,1)}, u32[]{:S(2)}, u32[]{:S(2)}) collective-permute-start(bf16[4,80,1152]{2,1,0:T(8,128)(2,1)} %dynamic-slice_bitcast_fusion.2), channel_id=1, source_target_pairs={{0,4},{4,0},{8,12},{12,8},{16,20},{20,16},{24,28},{28,24},{1,5},{5... | collective-permute-start | bytes 2211848 | tf_op jit(solution)/shard_map/ppermute | solution.py:794
  389.7 47.3 %collective-permute-start.44 = (bf16[192,1152]{1,0:T(8,128)(2,1)}, bf16[192,1152]{1,0:T(8,128)(2,1)}, u32[]{:S(2)}, u32[]{:S(2)}) collective-permute-start(bf16[192,1152]{1,0:T(8,128)(2,1)} %get-tuple-element.523), channel_id=1, source_target_pairs={{0,1},{1,0},{2,3},{3,2},{4,5},{5,4},{6,7},{7,6},{8,9},{9,8},{10,11... | collective-permute-start | bytes 1327112 | tf_op jit(solution)/shard_map/ppermute | solution.py:844
  390.1 46.9 %collective-permute-start.45 = (bf16[192,1152]{1,0:T(8,128)(2,1)}, bf16[192,1152]{1,0:T(8,128)(2,1)}, u32[]{:S(2)}, u32[]{:S(2)}) collective-permute-start(bf16[192,1152]{1,0:T(8,128)(2,1)} %get-tuple-element.522), channel_id=1, source_target_pairs={{0,2},{1,3},{2,0},{3,1},{4,6},{5,7},{6,4},{7,5},{8,10},{9,11},{10,... | collective-permute-start | bytes 1327112 | tf_op jit(solution)/shard_map/ppermute | solution.py:844
  391.6 45.5 %collective-permute-start.46 = (bf16[192,1152]{1,0:T(8,128)(2,1)S(1)}, bf16[192,1152]{1,0:T(8,128)(2,1)}, u32[]{:S(2)}, u32[]{:S(2)}) collective-permute-start(bf16[192,1152]{1,0:T(8,128)(2,1)S(1)} %get-tuple-element.521), channel_id=1, source_target_pairs={{0,3},{1,2},{2,1},{3,0},{4,7},{5,6},{6,5},{7,4},{8,11},{9,10},{10,... | collective-permute-start | bytes 1327112 | tf_op jit(solution)/shard_map/ppermute | solution.py:844
  439.1 50.3 %collective-permute-start.50 = (bf16[2,80,1152]{2,1,0:T(8,128)(2,1)S(1)}, bf16[2,80,1152]{2,1,0:T(8,128)(2,1)S(1)}, u32[]{:S(2)}, u32[]{:S(2)}) collective-permute-start(bf16[2,80,1152]{2,1,0:T(8,128)(2,1)S(1)} %dynamic-slice_bitcast_fusion.5), channel_id=1, source_target_pairs={{0,8},{4,12},{8,0},{12,4},{16,24},{20,28},{24,16},{28,20},{1,9},{5... | collective-permute-start | bytes 1105928 | tf_op jit(solution)/shard_map/ppermute | solution.py:794
  439.2 50.1 %collective-permute-start.49 = (bf16[1024,128]{1,0:T(8,128)(2,1)S(1)}, bf16[1024,128]{1,0:T(8,128)(2,1)S(1)}, u32[]{:S(2)}, u32[]{:S(2)}) collective-permute-start(bf16[1024,128]{1,0:T(8,128)(2,1)S(1)} %add.283), channel_id=1, source_target_pairs={{0,2},{1,3},{2,0},{3,1},{4,6},{5,7},{6,4},{7,5},{8,10},{9,11},{10,... | collective-permute-start | bytes 786440 | tf_op jit(solution)/shard_map/ppermute | solution.py:844
  494.6 27.5 %collective-permute-start.54 = (bf16[4,80,1152]{2,1,0:T(8,128)(2,1)S(1)}, bf16[4,80,1152]{2,1,0:T(8,128)(2,1)S(1)}, u32[]{:S(2)}, u32[]{:S(2)}) collective-permute-start(bf16[4,80,1152]{2,1,0:T(8,128)(2,1)S(1)} %dynamic-slice_bitcast_fusion.1), channel_id=1, source_target_pairs={{0,4},{4,0},{8,12},{12,8},{16,20},{20,16},{24,28},{28,24},{1,5},{5... | collective-permute-start | bytes 2211848 | tf_op jit(solution)/shard_map/ppermute | solution.py:794
  498.1 24.0 %collective-permute-start.52 = (bf16[1024,128]{1,0:T(8,128)(2,1)S(1)}, bf16[1024,128]{1,0:T(8,128)(2,1)S(1)}, u32[]{:S(2)}, u32[]{:S(2)}) collective-permute-start(bf16[1024,128]{1,0:T(8,128)(2,1)S(1)} %add.288), channel_id=1, source_target_pairs={{0,2},{1,3},{2,0},{3,1},{4,6},{5,7},{6,4},{7,5},{8,10},{9,11},{10,... | collective-permute-start | bytes 786440 | tf_op jit(solution)/shard_map/ppermute | solution.py:844
  498.4 23.6 %collective-permute-start.53 = (bf16[1,80,1152]{2,1,0:T(8,128)(2,1)S(1)}, bf16[1,80,1152]{2,1,0:T(8,128)(2,1)S(1)}, u32[]{:S(2)}, u32[]{:S(2)}) collective-permute-start(bf16[1,80,1152]{2,1,0:T(8,128)(2,1)S(1)} %constant_dynamic-slice_fusion.1), channel_id=1, source_target_pairs={{0,16},{4,20},{8,24},{12,28},{16,0},{20,4},{24,8},{28,12},{1,17},{... | collective-permute-start | bytes 552968 | tf_op jit(solution)/shard_map/ppermute | solution.py:794
  547.9 19.0 %collective-permute-start.55 = (bf16[2,512,1152]{2,1,0:T(8,128)(2,1)}, bf16[2,512,1152]{2,1,0:T(8,128)(2,1)}, u32[]{:S(2)}, u32[]{:S(2)}) collective-permute-start(bf16[2,512,1152]{2,1,0:T(8,128)(2,1)} %pad_maximum_fusion.1), channel_id=1, source_target_pairs={{0,1},{1,0},{2,3},{3,2},{4,5},{5,4},{6,7},{7,6},{8,9},{9,8},{10,11... | collective-permute-start | bytes 7077896 | tf_op jit(solution)/shard_map/ppermute | solution.py:844
  552.5 23.4 %collective-permute-start.56 = (bf16[4,80,1408]{2,1,0:T(8,128)(2,1)}, bf16[4,80,1408]{2,1,0:T(8,128)(2,1)}, u32[]{:S(2)}, u32[]{:S(2)}) collective-permute-start(bf16[4,80,1408]{2,1,0:T(8,128)(2,1)} %dynamic-slice_bitcast_fusion), channel_id=1, source_target_pairs={{0,4},{4,0},{8,12},{12,8},{16,20},{20,16},{24,28},{28,24},{1,5},{5... | collective-permute-start | bytes 2703368 | tf_op jit(solution)/shard_map/ppermute | solution.py:794
  554.7 21.2 %collective-permute-start.58 = (f32[6,1152]{1,0:T(8,128)S(1)}, f32[6,1152]{1,0:T(8,128)}, u32[]{:S(2)}, u32[]{:S(2)}) collective-permute-start(f32[6,1152]{1,0:T(8,128)S(1)} %pad_maximum_fusion.2), channel_id=1, source_target_pairs={{0,4},{4,0},{8,12},{12,8},{16,20},{20,16},{24,28},{28,24},{1,5},{5... | collective-permute-start | bytes 82952 | tf_op jit(solution)/shard_map/ppermute | solution.py:823
  555.5 20.5 %collective-permute-start.57 = (bf16[2,80,1152]{2,1,0:T(8,128)(2,1)}, bf16[2,80,1152]{2,1,0:T(8,128)(2,1)S(1)}, u32[]{:S(2)}, u32[]{:S(2)}) collective-permute-start(bf16[2,80,1152]{2,1,0:T(8,128)(2,1)} %dynamic-slice_bitcast_fusion.4), channel_id=1, source_target_pairs={{0,8},{4,12},{8,0},{12,4},{16,24},{20,28},{24,16},{28,20},{1,9},{5... | collective-permute-start | bytes 1105928 | tf_op jit(solution)/shard_map/ppermute | solution.py:794
  577.5 16.6 %collective-permute-start.59 = (bf16[2,80,1408]{2,1,0:T(8,128)(2,1)S(1)}, bf16[2,80,1408]{2,1,0:T(8,128)(2,1)S(1)}, u32[]{:S(2)}, u32[]{:S(2)}) collective-permute-start(bf16[2,80,1408]{2,1,0:T(8,128)(2,1)S(1)} %dynamic-slice_bitcast_fusion.3), channel_id=1, source_target_pairs={{0,8},{4,12},{8,0},{12,4},{16,24},{20,28},{24,16},{28,20},{1,9},{5... | collective-permute-start | bytes 1351688 | tf_op jit(solution)/shard_map/ppermute | solution.py:794
  577.9 27.3 %collective-permute-start.62 = (bf16[512,1152]{1,0:T(8,128)(2,1)S(1)}, bf16[512,1152]{1,0:T(8,128)(2,1)S(1)}, u32[]{:S(2)}, u32[]{:S(2)}) collective-permute-start(bf16[512,1152]{1,0:T(8,128)(2,1)S(1)} %fusion.15), channel_id=1, source_target_pairs={{0,2},{1,3},{2,0},{3,1},{4,6},{5,7},{6,4},{7,5},{8,10},{9,11},{10,... | collective-permute-start | bytes 3538952 | tf_op jit(solution)/shard_map/ppermute | solution.py:844
  580.3 13.9 %collective-permute-start.60 = (bf16[1,80,1152]{2,1,0:T(8,128)(2,1)S(1)}, bf16[1,80,1152]{2,1,0:T(8,128)(2,1)S(1)}, u32[]{:S(2)}, u32[]{:S(2)}) collective-permute-start(bf16[1,80,1152]{2,1,0:T(8,128)(2,1)S(1)} %constant_dynamic-slice_fusion), channel_id=1, source_target_pairs={{0,16},{4,20},{8,24},{12,28},{16,0},{20,4},{24,8},{28,12},{1,17},{... | collective-permute-start | bytes 552968 | tf_op jit(solution)/shard_map/ppermute | solution.py:794
  594.3 15.0 %collective-permute-start.63 = (bf16[1,80,1408]{2,1,0:T(8,128)(2,1)S(1)}, bf16[1,80,1408]{2,1,0:T(8,128)(2,1)S(1)}, u32[]{:S(2)}, u32[]{:S(2)}) collective-permute-start(bf16[1,80,1408]{2,1,0:T(8,128)(2,1)S(1)} %constant_dynamic-slice_fusion.2), channel_id=1, source_target_pairs={{0,16},{4,20},{8,24},{12,28},{16,0},{20,4},{24,8},{28,12},{1,17},{... | collective-permute-start | bytes 675848 | tf_op jit(solution)/shard_map/ppermute | solution.py:794
  598.0 11.2 %collective-permute-start.64 = (f32[6,1152]{1,0:T(8,128)S(1)}, f32[6,1152]{1,0:T(8,128)S(1)}, u32[]{:S(2)}, u32[]{:S(2)}) collective-permute-start(f32[6,1152]{1,0:T(8,128)S(1)} %add.305), channel_id=1, source_target_pairs={{0,16},{4,20},{8,24},{12,28},{16,0},{20,4},{24,8},{28,12},{1,17},{... | collective-permute-start | bytes 82952 | tf_op jit(solution)/shard_map/ppermute | solution.py:823
  (135 other events, 1598.1 us)
Sparse Core Ops, SparseCore 0:
  63.7 205.2 all-gather.1
  316.8 235.0 reduce-scatter.1
